TPU v7x, 128 devices: a whole 4x4x4 slice. The times are simulated.
128 devices in a mesh: dp: 32 (over x, z, core), mp: 4 (over y).
Axes of the slice: x: 4, y: 4, z: 4, core: 2. Of those that a mesh axis runs over, the one named last changes fastest.
Arguments:
- preactivation: bfloat16 [14336, 32768], P('dp', 'mp'), may hold values from -6 to 6
- upstream: bfloat16 [14336, 512], P('dp'), may hold values from -0.29882812 to 0.29882812
- weight: bfloat16 [32768, 512], P('mp'), may hold values from -40 to 40
- first_moment: float32 [32768, 512], P(('mp', 'dp')), may hold values from -4 to 4
- second_moment: float32 [32768, 512], P(('mp', 'dp')), may hold values from 1 to 16
Outputs:
- input_grad: bfloat16 [14336, 32768], P('dp', 'mp')
- new_weight: bfloat16 [32768, 512], P('mp')
- first_next: float32 [32768, 512], P(('mp', 'dp'))
- second_next: float32 [32768, 512], P(('mp', 'dp'))
- trust_step: float32 [32768, 512], P(('mp', 'dp'))
All inputs are finite; a program needn't handle non-finite values.
Results may differ from a plain program's by a relative error of at most 0.015.
Values may be sent and summed in bfloat16 or wider, within the bound.
No kernel may reach another device: no remote copies, remote signals or barrier semaphores. Data moves between devices by JAX's collectives and lax.ppermute only.
A program may use at most 128 MiB of HBM per device.

v0:
```python
import jax
import jax.numpy as jnp
from jax import lax
from jax.sharding import PartitionSpec as P

STEP = 1000


def per_device(preactivation, upstream, weight, first_moment, second_moment):
    owned = first_moment.shape[0]
    start_row = lax.axis_index("dp") * owned
    own_weight = lax.dynamic_slice_in_dim(weight, start_row, owned, 0).astype(jnp.float32)
    weight_local = jnp.sum(own_weight * own_weight)
    hidden = jnp.maximum(preactivation, jnp.zeros((), jnp.bfloat16))
    gradient = lax.psum_scatter(
        lax.dot_general(
            hidden, upstream, (((0,), (0,)), ((), ())), preferred_element_type=jnp.float32
        ).astype(jnp.bfloat16),
        "dp",
        scatter_dimension=0,
        tiled=True,
    ).astype(jnp.float32)
    back = lax.dot_general(
        upstream, weight, (((1,), (1,)), ((), ())), preferred_element_type=jnp.float32
    )
    input_grad = jnp.where(preactivation > 0, back, jnp.zeros((), jnp.float32)).astype(jnp.bfloat16)
    beta_one = 0.9
    beta_two = 0.999
    bias_one = 1.0 - beta_one**STEP
    bias_two = 1.0 - beta_two**STEP
    first_next = beta_one * first_moment + (1.0 - beta_one) * gradient
    second_next = beta_two * second_moment + (1.0 - beta_two) * gradient * gradient
    update = first_next / bias_one / (jnp.sqrt(second_next / bias_two) + 1e-06) + 0.02 * own_weight
    update_local = jnp.sum(update * update)
    weight_sq, update_sq = lax.psum((weight_local, update_local), ("dp", "mp"))
    trust_step = jnp.sqrt(weight_sq) / jnp.sqrt(update_sq) * update
    new_rows = (own_weight - 0.02 * trust_step).astype(jnp.bfloat16)
    new_weight = lax.all_gather(new_rows, "dp", axis=0, tiled=True)
    return (input_grad, new_weight, first_next, second_next, trust_step)


def solution(mesh):
    return jax.shard_map(
        per_device,
        mesh=mesh,
        in_specs=(
            P("dp", "mp"),
            P("dp", None),
            P("mp", None),
            P(("mp", "dp"), None),
            P(("mp", "dp"), None),
        ),
        out_specs=(
            P("dp", "mp"),
            P("mp", None),
            P(("mp", "dp"), None),
            P(("mp", "dp"), None),
            P(("mp", "dp"), None),
        ),
        check_vma=False,
    )
```

profile of v0, /device:TPU:1, one launch (start us, length us, event | category | flops | bytes accessed | tf_op | source)
XLA Modules:
  0.0 249.3 jit_solution(5887788048788325232)
XLA Ops:
  7.2 0.0 copy-start
  7.2 0.0 reduce-scatter.2.cloned.1.call-start
  7.2 1.0 copy-done
  8.2 10.1 %convolution_convert_fusion = bf16[8192,512]{1,0:T(8,128)(2,1)} fusion(bf16[448,512]{1,0:T(8,128)(2,1)S(1)} %copy-done, bf16[448,8192]{1,0:T(8,128)(2,1)} %param.5), kind=kOutput, calls=%fused_computation.1 | convolution fusion | flops 3765960704 | bytes 16187392 | tf_op jit(solution)/shard_map/dot_general | solution.py:16
  18.2 0.0 copy-start.1
  18.2 0.0 copy-start.2
  18.2 0.0 reduce-scatter.2.cloned.1.call-update
  18.3 0.0 all-gather.2.cloned.1.call-start
  18.3 94.4 %reduce-scatter.2.cloned.1.call-done = bf16[256,512]{1,0:T(8,128)(2,1)} async-done(((bf16[8192,512]{1,0:T(8,128)(2,1)}), bf16[256,512]{1,0:T(8,128)(2,1)}) %reduce-scatter.2.cloned.1.call-update) | async-done | bytes 262160 | tf_op jit(solution)/shard_map/reduce_scatter | solution.py:15
  112.7 0.0 copy-done.1
  112.7 0.0 copy-done.2
  112.7 3.0 %multiply_reduce_fusion = (f32[]{:T(128)}, f32[256,512]{1,0:T(8,128)S(1)}, f32[256,512]{1,0:T(8,128)}, f32[256,512]{1,0:T(8,128)}, f32[]{:T(128)}) fusion(bf16[8192,512]{1,0:T(8,128)(2,1)} %param.7, s32[]{:T(128)S(6)} %select_n.8, bf16[256,512]{1,0:T(8,128)(2,1)} %reduce-scatter.2.cloned.1.call-done, f32[256,512]{1,0:T(8,128)S(1)} %copy-done.1, ...), kind=kLoop, calls=%fused_computation.14 | loop fusion | flops 2359294 | bytes 3145740 | tf_op jit(solution)/shard_map/reduce_sum | solution.py:34
  115.8 66.1 %all-reduce = (f32[]{:T(128)}, f32[]{:T(128)}) all-reduce(f32[]{:T(128)} %get-tuple-element.13, f32[]{:T(128)} %get-tuple-element.9), channel_id=1, replica_groups=mesh['dp'=32,'mp'=4] {'dp','mp'}, use_global_device_ids=true, to_apply=%region_1.0 | all-reduce | flops 2 | bytes 16 | tf_op jit(solution)/shard_map/psum | solution.py:35
  183.2 1.9 fusion.5
  185.1 0.0 all-gather.2.cloned.1.call-update
  185.2 11.6 %select_convert_fusion = bf16[448,8192]{1,0:T(8,128)(2,1)} fusion(bf16[448,8192]{1,0:T(8,128)(2,1)} %param.5, bf16[448,512]{1,0:T(8,128)(2,1)S(1)} %copy-done, bf16[8192,512]{1,0:T(8,128)(2,1)} %param.7), kind=kOutput, calls=%fused_computation | convolution fusion | flops 3769106432 | bytes 23527424 | tf_op jit(solution)/shard_map/dot_general | solution.py:23
  196.8 38.4 %all-gather.2.cloned.1.call-done = bf16[8192,512]{1,0:T(8,128)(2,1)} async-done(((bf16[256,512]{1,0:T(8,128)(2,1)}), bf16[8192,512]{1,0:T(8,128)(2,1)}) %all-gather.2.cloned.1.call-update) | async-done | bytes 8388624 | tf_op jit(solution)/shard_map/all_gather | solution.py:38
  235.2 7.3 %copy.11 = bf16[8192,512]{1,0:T(8,128)(2,1)} copy(bf16[8192,512]{1,0:T(8,128)(2,1)} %all-gather.2.cloned.1.call-done) | data formatting | bytes 16777216
Async XLA Ops:
  7.2 1.0 copy-start
  7.2 105.5 %reduce-scatter.2.cloned.1.call-start = ((), (), s32[]{:S(2)}) async-start(), calls=%async_computation.1 | async-start | bytes 8650752 | tf_op jit(solution)/shard_map/reduce_scatter | solution.py:15
  18.2 94.5 %copy-start.1 = (f32[256,512]{1,0:T(8,128)S(1)}, f32[256,512]{1,0:T(8,128)}, u32[]{:S(2)}) copy-start(f32[256,512]{1,0:T(8,128)} %param.9) | copy-start | bytes 1572868
  18.2 94.5 %copy-start.2 = (f32[256,512]{1,0:T(8,128)S(1)}, f32[256,512]{1,0:T(8,128)}, u32[]{:S(2)}) copy-start(f32[256,512]{1,0:T(8,128)} %param.8) | copy-start | bytes 1572868
  18.3 216.9 %all-gather.2.cloned.1.call-start = ((), (), s32[]{:S(2)}) async-start(), calls=%async_computation.2 | async-start | bytes 8650752 | tf_op jit(solution)/shard_map/all_gather | solution.py:38
Sparse Core Ops, SparseCore 0:
  18.4 94.2 reduce-scatter.1
  185.3 49.8 all-gather.1
where the time goes:
time: 250 us; the launch traced here: 249 us
  waiting for transfers between devices  133 us (53%)
  blocking collectives  66.1 us (26%)
  matrix products  21.7 us (9%)
  between operations  15.4 us (6%)
  local copies, waits for them, and re-layouts  8.29 us (3%)
  other arithmetic  4.96 us (2%)
    reduce_scatter x1, waiting for transfers between devices, per_device(): lax.psum_scatter(lax.dot_general(hidden, upstream, (((0,), (0,)), ((), ()...  94.4 us
    psum x1, blocking collectives, per_device(): weight_sq, update_sq = lax.psum((weight_local, update_local), ('dp', 'mp'))  66.1 us
    all_gather x1, waiting for transfers between devices, per_device(): new_weight = lax.all_gather(new_rows, 'dp', axis=0, tiled=True)  38.4 us
    dot_general x1, matrix products, per_device(): lax.dot_general(upstream, weight, (((1,), (1,)), ((), ())), preferred_ele...  11.6 us
    dot_general x1, matrix products, per_device(): lax.dot_general(hidden, upstream, (((0,), (0,)), ((), ())), preferred_ele...  10.1 us
    unnamed x7, local copies, waits for them, and re-layouts  8.29 us
  transfers between devices with their start and end apart: 2, of which 2 were waited for; matrix products, arithmetic and copies ran while one was open for 5% of the time, Pallas kernels for 0%

commit v1 on v0

v1 whole, which is shorter than its diff:
```python
import jax
import jax.numpy as jnp
from jax import lax
from jax.experimental import pallas as pl
from jax.experimental.pallas import tpu as pltpu
from jax.sharding import Mesh
from jax.sharding import PartitionSpec as P

STEP = 1000
DP = ("x", "z", "c")
ROWS = 256
D = 512


def shift_first(k):
    pairs = []
    for x in range(4):
        for z in range(4):
            pairs.append(((x * 4 + z) * 2, (((x + k) % 4) * 4 + z) * 2))
            pairs.append(((x * 4 + z) * 2 + 1, (x * 4 + (z + k) % 4) * 2 + 1))
    return pairs


def shift_second(k):
    pairs = []
    for x in range(4):
        for z in range(4):
            pairs.append(((x * 4 + z) * 2, (x * 4 + (z + k) % 4) * 2))
            pairs.append(((x * 4 + z) * 2 + 1, (((x + k) % 4) * 4 + z) * 2 + 1))
    return pairs


def along_first(value, k):
    return lax.ppermute(value, DP, shift_first(k))


def along_second(value, k):
    return lax.ppermute(value, DP, shift_second(k))


def along_y(value, k):
    return lax.ppermute(value, "y", [(i, (i + k) % 4) for i in range(4)])


def sibling(value):
    return lax.ppermute(value, "c", [(0, 1), (1, 0)])


def partial_body(blocks, own_ref, other_ref, up_ref, keep_ref, send_ref, up_t):
    @pl.when(pl.program_id(0) == 0)
    def _():
        up_t[...] = up_ref[...].T

    zero = jnp.zeros((), jnp.bfloat16)
    for source, target in ((own_ref, keep_ref), (other_ref, send_ref)):
        target[...] = jnp.dot(
            up_t[...], jnp.maximum(source[...], zero), preferred_element_type=jnp.float32
        ).astype(jnp.bfloat16)


def partial_terms(preactivation, upstream, own, other):
    count = own.shape[0]
    tokens = preactivation.shape[0]
    stacked = jax.ShapeDtypeStruct((count * D, ROWS), jnp.bfloat16)
    return pl.pallas_call(
        partial_body,
        out_shape=(stacked, stacked),
        grid_spec=pltpu.PrefetchScalarGridSpec(
            num_scalar_prefetch=1,
            grid=(count,),
            in_specs=[
                pl.BlockSpec((tokens, ROWS), lambda i, b: (0, b[i])),
                pl.BlockSpec((tokens, ROWS), lambda i, b: (0, b[count + i])),
                pl.BlockSpec((tokens, D), lambda i, b: (0, 0)),
            ],
            out_specs=[
                pl.BlockSpec((D, ROWS), lambda i, b: (i, 0)),
                pl.BlockSpec((D, ROWS), lambda i, b: (i, 0)),
            ],
            scratch_shapes=[pltpu.VMEM((D, tokens), jnp.bfloat16)],
        ),
        compiler_params=pltpu.CompilerParams(vmem_limit_bytes=16 * 2**20),
        cost_estimate=pl.CostEstimate(
            flops=4 * count * ROWS * D * tokens,
            bytes_accessed=4 * count * ROWS * (D + tokens),
            transcendentals=0,
        ),
        name="partial_terms",
    )(jnp.concatenate([own, other]), preactivation, preactivation, upstream)


def update_body(
    block, g0, g1, g2, g3, g4, g5, g6, first, second, weight,
    first_out, second_out, update_out, short_out, sums_out,
):
    beta_one = 0.9
    beta_two = 0.999
    bias_one = 1.0 - beta_one**STEP
    bias_two = 1.0 - beta_two**STEP
    total = g0[...].astype(jnp.float32)
    for ref in (g1, g2, g3, g4, g5, g6):
        total = total + ref[...].astype(jnp.float32)
    gradient = total.T
    own_weight = weight[...].astype(jnp.float32)
    first_next = beta_one * first[...] + (1.0 - beta_one) * gradient
    second_next = beta_two * second[...] + (1.0 - beta_two) * gradient * gradient
    update = first_next / bias_one / (jnp.sqrt(second_next / bias_two) + 1e-06) + 0.02 * own_weight
    first_out[...] = first_next
    second_out[...] = second_next
    update_out[...] = update
    short_out[...] = update.astype(jnp.bfloat16)
    update_sq = jnp.sum(update * update)
    weight_sq = jnp.sum(own_weight * own_weight)
    row = lax.broadcasted_iota(jnp.int32, (8, 128), 0)
    sums = jnp.where(row == 0, update_sq, weight_sq)

    @pl.when(pl.program_id(0) == 0)
    def _():
        sums_out[...] = sums

    @pl.when(pl.program_id(0) > 0)
    def _():
        sums_out[...] += sums


def update_rows(block, terms, first, second, weight):
    half = D // 2
    long = jax.ShapeDtypeStruct((ROWS, D), jnp.float32)
    rows = pl.BlockSpec((ROWS, half), lambda j, b: (0, j))
    return pl.pallas_call(
        update_body,
        out_shape=(
            long,
            long,
            long,
            jax.ShapeDtypeStruct((ROWS, D), jnp.bfloat16),
            jax.ShapeDtypeStruct((8, 128), jnp.float32),
        ),
        grid_spec=pltpu.PrefetchScalarGridSpec(
            num_scalar_prefetch=1,
            grid=(2,),
            in_specs=[pl.BlockSpec((half, ROWS), lambda j, b: (j, 0))] * 7
            + [rows, rows, pl.BlockSpec((ROWS, half), lambda j, b: (b[0], j))],
            out_specs=[rows, rows, rows, rows, pl.BlockSpec((8, 128), lambda j, b: (0, 0))],
        ),
        compiler_params=pltpu.CompilerParams(vmem_limit_bytes=24 * 2**20),
        cost_estimate=pl.CostEstimate(
            flops=20 * ROWS * D, bytes_accessed=38 * ROWS * D, transcendentals=ROWS * D
        ),
        name="update_rows",
    )(block.reshape(1), *terms, first, second, weight)


def apply_body(sizes, blocks, step_ref, weight, *refs):
    out = refs[-1]
    i = pl.program_id(0)
    begin = 0
    for size, ref in zip(sizes, refs[: len(sizes)]):

        @pl.when((i >= begin) & (i < begin + size))
        def _(ref=ref):
            out[...] = (
                weight[...].astype(jnp.float32) - step_ref[0, 0] * ref[...].astype(jnp.float32)
            ).astype(jnp.bfloat16)

        begin += size


def apply_update(blocks, step, weight, updates, before):
    sizes = [u.shape[0] // ROWS for u in updates]
    count = sum(sizes)
    specs = []
    begin = 0
    for size in sizes:
        specs.append(
            pl.BlockSpec(
                (ROWS, D),
                lambda i, b, begin=begin, size=size: (jnp.clip(i - begin, 0, size - 1), 0),
            )
        )
        begin += size
    extra = [] if before is None else [before]

    def body(blocks, *refs):
        apply_body(sizes, blocks, *refs)

    return pl.pallas_call(
        body,
        out_shape=jax.ShapeDtypeStruct(weight.shape, jnp.bfloat16),
        grid_spec=pltpu.PrefetchScalarGridSpec(
            num_scalar_prefetch=1,
            grid=(count,),
            in_specs=[
                pl.BlockSpec(memory_space=pltpu.SMEM),
                pl.BlockSpec((ROWS, D), lambda i, b: (b[i], 0)),
            ]
            + specs
            + [pl.BlockSpec(memory_space=pl.ANY)] * len(extra),
            out_specs=pl.BlockSpec((ROWS, D), lambda i, b: (b[i], 0)),
        ),
        input_output_aliases={} if before is None else {3 + len(updates): 0},
        compiler_params=pltpu.CompilerParams(vmem_limit_bytes=16 * 2**20),
        cost_estimate=pl.CostEstimate(
            flops=2 * count * ROWS * D, bytes_accessed=6 * count * ROWS * D, transcendentals=0
        ),
        name="apply_update",
    )(blocks, step, weight, *updates, *extra)


def added(*values):
    total = values[0].astype(jnp.float32)
    for value in values[1:]:
        total = total + value.astype(jnp.float32)
    return total.astype(jnp.bfloat16)


def per_device(preactivation, upstream, weight, first_moment, second_moment):
    x, z, c = lax.axis_index("x"), lax.axis_index("z"), lax.axis_index("c")
    first = jnp.where(c == 0, x, z)
    second = jnp.where(c == 0, z, x)
    first_stride = jnp.where(c == 0, 8, 2)
    second_stride = jnp.where(c == 0, 2, 8)
    four = jnp.arange(4, dtype=jnp.int32)

    def own_unit(k):
        return (first + k) % 4 * first_stride + (second + four) % 4 * second_stride + c

    def other_unit(k):
        return (second + k) % 4 * second_stride + (first + four) % 4 * first_stride + 1 - c

    keep_far, send_far = partial_terms(preactivation, upstream, own_unit(2), other_unit(2))
    far = added(keep_far, sibling(send_far))
    half = 2 * D
    from_left = along_first(far[:half], 1)
    from_right = along_first(far[half:], -1)

    keep_near, send_near = partial_terms(
        preactivation,
        upstream,
        jnp.concatenate([own_unit(1), own_unit(-1)]),
        jnp.concatenate([other_unit(1), other_unit(-1)]),
    )
    got_near = sibling(send_near)
    unit = 4 * D
    right = jnp.concatenate(
        [
            added(keep_near[:half], got_near[:half], from_left),
            added(keep_near[half:unit], got_near[half:unit]),
        ]
    )
    left = jnp.concatenate(
        [
            added(keep_near[unit : unit + half], got_near[unit : unit + half]),
            added(keep_near[unit + half :], got_near[unit + half :], from_right),
        ]
    )
    sum_left = along_first(right, 1)
    sum_right = along_first(left, -1)

    keep_here, send_here = partial_terms(preactivation, upstream, own_unit(0), other_unit(0))
    got_here = sibling(send_here)
    terms = [
        along_second(
            added(*(v[j * D : (j + 1) * D] for v in (keep_here, got_here, sum_left, sum_right))), j
        )
        for j in (1, 2, 3)
    ]

    back = lax.dot_general(
        upstream, weight, (((1,), (1,)), ((), ())), preferred_element_type=jnp.float32
    )
    input_grad = jnp.where(preactivation > 0, back, jnp.zeros((), jnp.float32)).astype(jnp.bfloat16)

    first_next, second_next, update, short, sums = update_rows(
        own_unit(0)[0],
        [keep_here, got_here, sum_left, sum_right, *terms],
        first_moment,
        second_moment,
        weight,
    )

    sums = sums + sibling(sums)
    sums = sums + along_y(sums, 1) + along_y(sums, 2) + along_y(sums, 3)
    sums = sums + along_second(sums, 1) + along_second(sums, 2) + along_second(sums, 3)
    sums = sums + along_first(sums, 1) + along_first(sums, 2) + along_first(sums, 3)
    ratio = jnp.sqrt(sums[1, 0]) / jnp.sqrt(sums[0, 0])
    trust_step = ratio * update
    step = (0.02 * ratio).reshape(1, 1)

    here = jnp.concatenate([short, *(along_second(short, -j) for j in (1, 2, 3))])
    near_left = along_first(here, 1)
    near_right = along_first(here, -1)
    far_left = along_first(near_left[: 2 * ROWS], 1)
    far_right = along_first(near_right[2 * ROWS :], -1)
    new_weight = apply_update(
        jnp.concatenate(
            [own_unit(0), other_unit(0), own_unit(-1), own_unit(1), other_unit(-1), other_unit(1)]
        ),
        step,
        weight,
        [here, sibling(here), near_left, near_right, sibling(near_left), sibling(near_right)],
        None,
    )
    new_weight = apply_update(
        jnp.concatenate([own_unit(2), other_unit(2)]),
        step,
        weight,
        [far_left, far_right, sibling(far_left), sibling(far_right)],
        new_weight,
    )
    return (input_grad, new_weight, first_next, second_next, trust_step)


def solution(mesh):
    split = Mesh(mesh.devices.reshape(4, 4, 2, 4), ("x", "z", "c", "y"))
    rows = P(("y", "x", "z", "c"), None)
    return jax.shard_map(
        per_device,
        mesh=split,
        in_specs=(P(DP, "y"), P(DP, None), P("y", None), rows, rows),
        out_specs=(P(DP, "y"), P("y", None), rows, rows, rows),
        check_vma=False,
    )
```

time: 250 us -> 144 us (0.58)
  waiting for transfers between devices: 133 us -> 41.5 us
  blocking collectives: 66.1 us -> 0 us
  starting transfers between devices: 0.08 us -> 38.3 us
  Pallas kernels: 0 us -> 33.5 us
  between operations: 15.4 us -> 2.31 us
  matrix products: 21.7 us -> 11.6 us
  local copies, waits for them, and re-layouts: 8.29 us -> 12.7 us
    reduce_scatter x1 -> x0, waiting for transfers between devices: 94.4 us -> none  [per_device(): lax.psum_scatter(lax.dot_general(hidden, upstream, (((0,), (0,)), ((), ()...]
    psum x1 -> x0, blocking collectives: 66.1 us -> none  [per_device(): weight_sq, update_sq = lax.psum((weight_local, update_local), ('dp', 'mp'))]
    ppermute x0 -> x32, waiting for transfers between devices: none -> 41.5 us  [the longest x11 18.8 us: along_first(): return lax.ppermute(value, DP, shift_first(k))]
    all_gather x1 -> x0, waiting for transfers between devices: 38.4 us -> none  [per_device(): new_weight = lax.all_gather(new_rows, 'dp', axis=0, tiled=True)]
    ppermute x0 -> x32, starting transfers between devices: none -> 38.3 us  [the longest x11 13.6 us: along_first(): return lax.ppermute(value, DP, shift_first(k))]
    pallas_call x0 -> x6, Pallas kernels: none -> 33.5 us  [the longest x2 20.7 us: apply_update(): pl.pallas_call(body, out_shape=jax.ShapeDtypeStruct(weight.shape, jnp.bfl...]
    dot_general x1 -> x0, matrix products: 10.1 us -> none  [per_device(): lax.dot_general(hidden, upstream, (((0,), (0,)), ((), ())), preferred_ele...]
    reduce_sum x1 -> x0, other arithmetic: 3.03 us -> none  [per_device(): update_local = jnp.sum(update * update)]
  transfers between devices with their start and end apart: 2 -> 32, of which waited for: 2 -> 14; matrix products, arithmetic and copies ran while one was open for 5% -> 13% of each run, Pallas kernels for 0% -> 16%
where the time goes in v1:
time: 144 us
  waiting for transfers between devices  41.5 us (29%)
  starting transfers between devices  38.3 us (27%)
  Pallas kernels  33.5 us (23%)
  local copies, waits for them, and re-layouts  12.7 us (9%)
  matrix products  11.6 us (8%)
  other arithmetic  3.8 us (3%)
  between operations  2.31 us (2%)
    pallas_call x2, Pallas kernels, apply_update(): pl.pallas_call(body, out_shape=jax.ShapeDtypeStruct(weight.shape, jnp.bfl...  20.7 us
    ppermute x11, waiting for transfers between devices, along_first(): return lax.ppermute(value, DP, shift_first(k))  18.8 us
    ppermute x9, waiting for transfers between devices, along_second(): return lax.ppermute(value, DP, shift_second(k))  18.6 us
    ppermute x11, starting transfers between devices, along_first(): return lax.ppermute(value, DP, shift_first(k))  13.6 us
    ppermute x9, starting transfers between devices, sibling(): return lax.ppermute(value, 'c', [(0, 1), (1, 0)])  12.7 us
    dot_general x1, matrix products, per_device(): lax.dot_general(upstream, weight, (((1,), (1,)), ((), ())), preferred_ele...  11.6 us
    pallas_call x3, Pallas kernels, partial_terms(): pl.pallas_call(partial_body, out_shape=(stacked, stacked), grid_spec=pltp...  10.7 us
    unnamed x25, local copies, waits for them, and re-layouts  9.67 us
  transfers between devices with their start and end apart: 32, of which 14 were waited for; matrix products, arithmetic and copies ran while one was open for 13% of the time, Pallas kernels for 16%

profile of v1, /device:TPU:1, one launch (start us, length us, event | category | flops | bytes accessed | tf_op | source)
XLA Modules:
  0.0 143.8 jit_solution(2808465599644071063)
XLA Ops:
  0.9 3.1 %copy-done = bf16[448,8192]{1,0:T(8,128)(2,1)S(1)} copy-done((bf16[448,8192]{1,0:T(8,128)(2,1)S(1)}, bf16[448,8192]{1,0:T(8,128)(2,1)}, u32[]{:S(2)}) %copy-start) | copy-done | bytes 7340056
  4.0 1.0 copy-done.2
  5.0 2.9 %partial_terms.5 = (bf16[2048,256]{1,0:T(8,128)(2,1)S(1)}, bf16[2048,256]{1,0:T(8,128)(2,1)S(1)}) custom-call(s32[8]{0:T(128)S(1)} %pad_add_fusion.blocks, bf16[448,8192]{1,0:T(8,128)(2,1)S(1)} %copy-done, bf16[448,8192]{1,0:T(8,128)(2,1)S(1)} %copy-done, bf16[448,512]{1,0:T(8,128)(2,1)S(1)} %copy-done.2), custom_call_target="tpu_custom_call" | custom-call | flops 939524096 | bytes 3932160 | tf_op jit(solution)/shard_map/partial_terms/pallas_call | solution.py:65
  7.9 1.5 %collective-permute-start.2 = (bf16[2048,256]{1,0:T(8,128)(2,1)S(1)}, bf16[2048,256]{1,0:T(8,128)(2,1)S(1)}, u32[]{:S(2)}, u32[]{:S(2)}) collective-permute-start(bf16[2048,256]{1,0:T(8,128)(2,1)S(1)} %get-tuple-element.21), channel_id=1, source_target_pairs={{0,4},{4,0},{1,5},{5,1},{2,6},{6,2},{3,7},{7,3},{8,12},{12,8},{9,1... | collective-permute-start | bytes 3145736 | tf_op jit(solution)/shard_map/ppermute | solution.py:46
  9.4 5.0 %partial_terms.4 = (bf16[4096,256]{1,0:T(8,128)(2,1)S(1)}, bf16[4096,256]{1,0:T(8,128)(2,1)S(1)}) custom-call(s32[16]{0:T(128)S(1)} %pad_add_fusion.2.blocks, bf16[448,8192]{1,0:T(8,128)(2,1)S(1)} %copy-done, bf16[448,8192]{1,0:T(8,128)(2,1)S(1)} %copy-done, bf16[448,512]{1,0:T(8,128)(2,1)S(1)} %copy-done.3), custom_call_target="tpu_custom_call" | custom-call | flops 1879048192 | bytes 7864320 | tf_op jit(solution)/shard_map/partial_terms/pallas_call | solution.py:65
  14.9 3.9 %collective-permute-start.5 = (bf16[1024,256]{1,0:T(8,128)(2,1)S(1)}, bf16[1024,256]{1,0:T(8,128)(2,1)S(1)}, u32[]{:S(2)}, u32[]{:S(2)}) collective-permute-start(bf16[1024,256]{1,0:T(8,128)(2,1)S(1)} %get-tuple-element.38), channel_id=1, source_target_pairs={{0,96},{4,28},{8,104},{12,4},{16,112},{20,12},{24,120},{28,20},{32... | collective-permute-start | bytes 1572872 | tf_op jit(solution)/shard_map/ppermute | solution.py:34
  18.9 2.9 %partial_terms.3 = (bf16[2048,256]{1,0:T(8,128)(2,1)S(1)}, bf16[2048,256]{1,0:T(8,128)(2,1)S(1)}) custom-call(s32[8]{0:T(128)S(1)} %pad_add_fusion.1.blocks, bf16[448,8192]{1,0:T(8,128)(2,1)S(1)} %bitcast.6, bf16[448,8192]{1,0:T(8,128)(2,1)S(1)} %bitcast.6, bf16[448,512]{1,0:T(8,128)(2,1)S(1)} %copy-done.3), custom_call_target="tpu_custom_call" | custom-call | flops 939524096 | bytes 3932160 | tf_op jit(solution)/shard_map/partial_terms/pallas_call | solution.py:65
  21.9 3.1 %collective-permute-done.5 = bf16[1024,256]{1,0:T(8,128)(2,1)S(1)} collective-permute-done((bf16[1024,256]{1,0:T(8,128)(2,1)S(1)}, bf16[1024,256]{1,0:T(8,128)(2,1)S(1)}, u32[]{:S(2)}, u32[]{:S(2)}) %collective-permute-start.5) | collective-permute-done | bytes 524320 | tf_op jit(solution)/shard_map/ppermute | solution.py:34
  25.0 3.4 %collective-permute-done.3 = bf16[1024,256]{1,0:T(8,128)(2,1)S(1)} collective-permute-done((bf16[1024,256]{1,0:T(8,128)(2,1)S(1)}, bf16[1024,256]{1,0:T(8,128)(2,1)S(1)}, u32[]{:S(2)}, u32[]{:S(2)}) %collective-permute-start.3) | collective-permute-done | bytes 524320 | tf_op jit(solution)/shard_map/ppermute | solution.py:34
  29.4 2.7 %collective-permute-start.6 = (bf16[2048,256]{1,0:T(8,128)(2,1)S(1)}, bf16[2048,256]{1,0:T(8,128)(2,1)S(1)}, u32[]{:S(2)}, u32[]{:S(2)}) collective-permute-start(bf16[2048,256]{1,0:T(8,128)(2,1)S(1)} %pad_maximum_fusion.1), channel_id=1, source_target_pairs={{0,96},{4,28},{8,104},{12,4},{16,112},{20,12},{24,120},{28,20},{32... | collective-permute-start | bytes 3145736 | tf_op jit(solution)/shard_map/ppermute | solution.py:34
  32.1 12.3 %collective-permute-done.4.g2 = bf16[2048,256]{1,0:T(8,128)(2,1)S(1)} collective-permute-done((bf16[2048,256]{1,0:T(8,128)(2,1)S(1)}, bf16[2048,256]{1,0:T(8,128)(2,1)S(1)}, u32[]{:S(2)}, u32[]{:S(2)}) %collective-permute-start.4) | collective-permute-done | bytes 1048608 | tf_op jit(solution)/shard_map/ppermute | solution.py:34
  44.9 2.3 %collective-permute-start.9 = (bf16[512,256]{1,0:T(8,128)(2,1)S(1)}, bf16[512,256]{1,0:T(8,128)(2,1)S(1)}, u32[]{:S(2)}, u32[]{:S(2)}) collective-permute-start(bf16[512,256]{1,0:T(8,128)(2,1)S(1)} %get-tuple-element.31), channel_id=1, source_target_pairs={{0,24},{4,100},{8,0},{12,108},{16,8},{20,116},{24,16},{28,124},{32... | collective-permute-start | bytes 786440 | tf_op jit(solution)/shard_map/ppermute | solution.py:38
  48.0 5.3 %collective-permute-done.9.g6 = bf16[512,256]{1,0:T(8,128)(2,1)S(1)} collective-permute-done((bf16[512,256]{1,0:T(8,128)(2,1)S(1)}, bf16[512,256]{1,0:T(8,128)(2,1)S(1)}, u32[]{:S(2)}, u32[]{:S(2)}) %collective-permute-start.9) | collective-permute-done | bytes 262176 | tf_op jit(solution)/shard_map/ppermute | solution.py:38
  54.0 2.9 %collective-permute-done.7.g4 = bf16[512,256]{1,0:T(8,128)(2,1)S(1)} collective-permute-done((bf16[512,256]{1,0:T(8,128)(2,1)S(1)}, bf16[512,256]{1,0:T(8,128)(2,1)S(1)}, u32[]{:S(2)}, u32[]{:S(2)}) %collective-permute-start.7) | collective-permute-done | bytes 262176 | tf_op jit(solution)/shard_map/ppermute | solution.py:38
  57.0 2.0 %update_rows.1 = (f32[256,512]{1,0:T(8,128)}, f32[256,512]{1,0:T(8,128)}, f32[256,512]{1,0:T(8,128)S(1)}, bf16[256,512]{1,0:T(8,128)(2,1)S(1)}, f32[8,128]{1,0:T(8,128)S(1)}) custom-call(s32[1]{0:T(128)S(1)} %bitcast.9, bf16[2048,256]{1,0:T(8,128)(2,1)S(1)} %get-tuple-element.16.g0, bf16[2048,256]{1,0:T(8,128)(2,1)S(1)} %collective-permute-done.g1, ...), custom_call_target="tpu_custom_call" | custom-call | flops 2621440 | bytes 4980736 | tf_op jit(solution)/shard_map/update_rows/pallas_call | solution.py:130
  61.2 3.0 %collective-permute-done.20 = bf16[256,512]{1,0:T(8,128)(2,1)S(1)} collective-permute-done((bf16[256,512]{1,0:T(8,128)(2,1)S(1)}, bf16[256,512]{1,0:T(8,128)(2,1)S(1)}, u32[]{:S(2)}, u32[]{:S(2)}) %collective-permute-start.20) | collective-permute-done | bytes 262176 | tf_op jit(solution)/shard_map/ppermute | solution.py:38
  64.9 1.0 collective-permute-done.21
  66.7 2.3 %collective-permute-done.22 = bf16[256,512]{1,0:T(8,128)(2,1)S(1)} collective-permute-done((bf16[256,512]{1,0:T(8,128)(2,1)S(1)}, bf16[256,512]{1,0:T(8,128)(2,1)S(1)}, u32[]{:S(2)}, u32[]{:S(2)}) %collective-permute-start.22) | collective-permute-done | bytes 262176 | tf_op jit(solution)/shard_map/ppermute | solution.py:38
  69.7 3.1 %collective-permute-start.25 = (bf16[1024,512]{1,0:T(8,128)(2,1)}, bf16[1024,512]{1,0:T(8,128)(2,1)S(1)}, u32[]{:S(2)}, u32[]{:S(2)}) collective-permute-start(bf16[1024,512]{1,0:T(8,128)(2,1)} %constant_dynamic-update-slice_fusion.refs_2_), channel_id=1, source_target_pairs={{0,96},{4,28},{8,104},{12,4},{16,112},{20,12},{24,120},{28,20},{32... | collective-permute-start | bytes 3145736 | tf_op jit(solution)/shard_map/ppermute | solution.py:34
  72.8 5.6 %collective-permute-start.10 = (f32[8,128]{1,0:T(8,128)S(1)}, f32[8,128]{1,0:T(8,128)S(1)}, u32[]{:S(2)}, u32[]{:S(2)}) collective-permute-start(f32[8,128]{1,0:T(8,128)S(1)} %get-tuple-element.22), channel_id=1, source_target_pairs={{0,4},{4,0},{1,5},{5,1},{2,6},{6,2},{3,7},{7,3},{8,12},{12,8},{9,1... | collective-permute-start | bytes 12296 | tf_op jit(solution)/shard_map/ppermute | solution.py:46
  79.2 2.7 %collective-permute-start.13 = (f32[8,128]{1,0:T(8,128)S(1)}, f32[8,128]{1,0:T(8,128)S(1)}, u32[]{:S(2)}, u32[]{:S(2)}) collective-permute-start(f32[8,128]{1,0:T(8,128)S(1)} %add.389), channel_id=1, source_target_pairs={{0,3},{1,0},{2,1},{3,2},{4,7},{5,4},{6,5},{7,6},{8,11},{9,8},{10,9... | collective-permute-start | bytes 12296 | tf_op jit(solution)/shard_map/ppermute | solution.py:42
  83.0 2.9 %collective-permute-done.12 = f32[8,128]{1,0:T(8,128)S(1)} collective-permute-done((f32[8,128]{1,0:T(8,128)S(1)}, f32[8,128]{1,0:T(8,128)S(1)}, u32[]{:S(2)}, u32[]{:S(2)}) %collective-permute-start.12) | collective-permute-done | bytes 4128 | tf_op jit(solution)/shard_map/ppermute | solution.py:42
  86.2 3.0 %collective-permute-start.16 = (f32[8,128]{1,0:T(8,128)S(1)}, f32[8,128]{1,0:T(8,128)S(1)}, u32[]{:S(2)}, u32[]{:S(2)}) collective-permute-start(f32[8,128]{1,0:T(8,128)S(1)} %add_add_fusion.2), channel_id=1, source_target_pairs={{0,24},{4,100},{8,0},{12,108},{16,8},{20,116},{24,16},{28,124},{32... | collective-permute-start | bytes 12296 | tf_op jit(solution)/shard_map/ppermute | solution.py:38
  90.0 3.3 %collective-permute-done.15 = f32[8,128]{1,0:T(8,128)S(1)} collective-permute-done((f32[8,128]{1,0:T(8,128)S(1)}, f32[8,128]{1,0:T(8,128)S(1)}, u32[]{:S(2)}, u32[]{:S(2)}) %collective-permute-start.15) | collective-permute-done | bytes 4128 | tf_op jit(solution)/shard_map/ppermute | solution.py:38
  93.3 1.7 %collective-permute-start.19 = (f32[8,128]{1,0:T(8,128)S(1)}, f32[8,128]{1,0:T(8,128)S(1)}, u32[]{:S(2)}, u32[]{:S(2)}) collective-permute-start(f32[8,128]{1,0:T(8,128)S(1)} %add_add_fusion.1), channel_id=1, source_target_pairs={{0,96},{4,28},{8,104},{12,4},{16,112},{20,12},{24,120},{28,20},{32... | collective-permute-start | bytes 12296 | tf_op jit(solution)/shard_map/ppermute | solution.py:34
  95.6 3.6 %collective-permute-start.29 = (bf16[1024,512]{1,0:T(8,128)(2,1)}, bf16[1024,512]{1,0:T(8,128)(2,1)}, u32[]{:S(2)}, u32[]{:S(2)}) collective-permute-start(bf16[1024,512]{1,0:T(8,128)(2,1)} %constant_dynamic-update-slice_fusion.refs_2_), channel_id=1, source_target_pairs={{0,4},{4,0},{1,5},{5,1},{2,6},{6,2},{3,7},{7,3},{8,12},{12,8},{9,1... | collective-permute-start | bytes 3145736 | tf_op jit(solution)/shard_map/ppermute | solution.py:46
  102.4 1.1 collective-permute-start.31
  103.6 11.6 %select_convert_fusion = bf16[448,8192]{1,0:T(8,128)(2,1)} fusion(bf16[448,8192]{1,0:T(8,128)(2,1)} %other_ref.5, bf16[448,512]{1,0:T(8,128)(2,1)S(1)} %copy-done.3, bf16[8192,512]{1,0:T(8,128)(2,1)} %refs_1_.3), kind=kOutput, calls=%fused_computation | convolution fusion | flops 3769106432 | bytes 23527424 | tf_op jit(solution)/shard_map/dot_general | solution.py:269
  117.8 1.9 %broadcast_multiply_fusion = f32[256,512]{1,0:T(8,128)} fusion(f32[256,512]{1,0:T(8,128)} %copy-done.6, f32[]{:T(128)} %bitcast), kind=kLoop, calls=%fused_computation.11 | loop fusion | flops 131072 | bytes 1048580 | tf_op jit(solution)/shard_map/mul | solution.py:287
  119.7 3.4 %copy-done.1 = bf16[8192,512]{1,0:T(8,128)(2,1)S(1)} copy-done((bf16[8192,512]{1,0:T(8,128)(2,1)S(1)}, bf16[8192,512]{1,0:T(8,128)(2,1)}, u32[]{:S(2)}) %copy-start.1) | copy-done | bytes 8388632
  123.0 14.6 %apply_update.2.refs_6_ = bf16[8192,512]{1,0:T(8,128)(2,1)} custom-call(s32[24]{0:T(128)S(1)} %concatenate.28.blocks, f32[1,1]{1,0:T(1,128)} %bitcast.1.refs_0_, bf16[8192,512]{1,0:T(8,128)(2,1)S(1)} %copy-done.1, bf16[1024,512]{1,0:T(8,128)(2,1)} %constant_dynamic-update-slice_fusion.refs_2_, bf16[1024,512]{1,0:T(8,128)(2,1)} %collective-permute-done.29.refs_3_, ...), custom_call_target="tpu_custom_call" | custom-call | flops 6291456 | bytes 18874368 | tf_op jit(solution)/shard_map/apply_update/pallas_call | solution.py:187
  137.6 6.2 %apply_update.3 = bf16[8192,512]{1,0:T(8,128)(2,1)} custom-call(s32[8]{0:T(128)S(1)} %pad_add_fusion.blocks, f32[1,1]{1,0:T(1,128)} %bitcast.1.refs_0_, bf16[8192,512]{1,0:T(8,128)(2,1)S(1)} %copy-done.1, bf16[512,512]{1,0:T(8,128)(2,1)} %collective-permute-done.24.refs_2_, ...), custom_call_target="tpu_custom_call", output_to_operand_aliasing={{}: (7, {})} | custom-call | flops 2097152 | bytes 6291456 | tf_op jit(solution)/shard_map/apply_update/pallas_call | solution.py:187
  (88 shorter events, 16.3 us)
Async XLA Ops:
  7.9 6.7 %collective-permute-start.2 = (bf16[2048,256]{1,0:T(8,128)(2,1)S(1)}, bf16[2048,256]{1,0:T(8,128)(2,1)S(1)}, u32[]{:S(2)}, u32[]{:S(2)}) collective-permute-start(bf16[2048,256]{1,0:T(8,128)(2,1)S(1)} %get-tuple-element.21), channel_id=1, source_target_pairs={{0,4},{4,0},{1,5},{5,1},{2,6},{6,2},{3,7},{7,3},{8,12},{12,8},{9,1... | collective-permute-start | bytes 3145736 | tf_op jit(solution)/shard_map/ppermute | solution.py:46
  14.4 13.9 %collective-permute-start.1 = (bf16[4096,256]{1,0:T(8,128)(2,1)S(1)}, bf16[4096,256]{1,0:T(8,128)(2,1)S(1)}, u32[]{:S(2)}, u32[]{:S(2)}) collective-permute-start(bf16[4096,256]{1,0:T(8,128)(2,1)S(1)} %get-tuple-element.19), channel_id=1, source_target_pairs={{0,4},{4,0},{1,5},{5,1},{2,6},{6,2},{3,7},{7,3},{8,12},{12,8},{9,1... | collective-permute-start | bytes 6291464 | tf_op jit(solution)/shard_map/ppermute | solution.py:46
  14.9 10.0 %collective-permute-start.5 = (bf16[1024,256]{1,0:T(8,128)(2,1)S(1)}, bf16[1024,256]{1,0:T(8,128)(2,1)S(1)}, u32[]{:S(2)}, u32[]{:S(2)}) collective-permute-start(bf16[1024,256]{1,0:T(8,128)(2,1)S(1)} %get-tuple-element.38), channel_id=1, source_target_pairs={{0,96},{4,28},{8,104},{12,4},{16,112},{20,12},{24,120},{28,20},{32... | collective-permute-start | bytes 1572872 | tf_op jit(solution)/shard_map/ppermute | solution.py:34
  18.9 9.5 %collective-permute-start.3 = (bf16[1024,256]{1,0:T(8,128)(2,1)S(1)}, bf16[1024,256]{1,0:T(8,128)(2,1)S(1)}, u32[]{:S(2)}, u32[]{:S(2)}) collective-permute-start(bf16[1024,256]{1,0:T(8,128)(2,1)S(1)} %get-tuple-element.39), channel_id=1, source_target_pairs={{0,32},{4,12},{8,40},{12,20},{16,48},{20,28},{24,56},{28,4},{32,64... | collective-permute-start | bytes 1572872 | tf_op jit(solution)/shard_map/ppermute | solution.py:34
  21.8 10.3 %collective-permute-start = (bf16[2048,256]{1,0:T(8,128)(2,1)S(1)}, bf16[2048,256]{1,0:T(8,128)(2,1)S(1)}, u32[]{:S(2)}, u32[]{:S(2)}) collective-permute-start(bf16[2048,256]{1,0:T(8,128)(2,1)S(1)} %get-tuple-element.17), channel_id=1, source_target_pairs={{0,4},{4,0},{1,5},{5,1},{2,6},{6,2},{3,7},{7,3},{8,12},{12,8},{9,1... | collective-permute-start | bytes 3145736 | tf_op jit(solution)/shard_map/ppermute | solution.py:46
  29.2 15.2 %collective-permute-start.4 = (bf16[2048,256]{1,0:T(8,128)(2,1)S(1)}, bf16[2048,256]{1,0:T(8,128)(2,1)S(1)}, u32[]{:S(2)}, u32[]{:S(2)}) collective-permute-start(bf16[2048,256]{1,0:T(8,128)(2,1)S(1)} %pad_maximum_fusion), channel_id=1, source_target_pairs={{0,32},{4,12},{8,40},{12,20},{16,48},{20,28},{24,56},{28,4},{32,64... | collective-permute-start | bytes 3145736 | tf_op jit(solution)/shard_map/ppermute | solution.py:34
  29.4 15.1 %collective-permute-start.6 = (bf16[2048,256]{1,0:T(8,128)(2,1)S(1)}, bf16[2048,256]{1,0:T(8,128)(2,1)S(1)}, u32[]{:S(2)}, u32[]{:S(2)}) collective-permute-start(bf16[2048,256]{1,0:T(8,128)(2,1)S(1)} %pad_maximum_fusion.1), channel_id=1, source_target_pairs={{0,96},{4,28},{8,104},{12,4},{16,112},{20,12},{24,120},{28,20},{32... | collective-permute-start | bytes 3145736 | tf_op jit(solution)/shard_map/ppermute | solution.py:34
  44.9 8.4 %collective-permute-start.9 = (bf16[512,256]{1,0:T(8,128)(2,1)S(1)}, bf16[512,256]{1,0:T(8,128)(2,1)S(1)}, u32[]{:S(2)}, u32[]{:S(2)}) collective-permute-start(bf16[512,256]{1,0:T(8,128)(2,1)S(1)} %get-tuple-element.31), channel_id=1, source_target_pairs={{0,24},{4,100},{8,0},{12,108},{16,8},{20,116},{24,16},{28,124},{32... | collective-permute-start | bytes 786440 | tf_op jit(solution)/shard_map/ppermute | solution.py:38
  47.2 6.8 %collective-permute-start.8 = (bf16[512,256]{1,0:T(8,128)(2,1)S(1)}, bf16[512,256]{1,0:T(8,128)(2,1)S(1)}, u32[]{:S(2)}, u32[]{:S(2)}) collective-permute-start(bf16[512,256]{1,0:T(8,128)(2,1)S(1)} %get-tuple-element.32), channel_id=1, source_target_pairs={{0,16},{4,68},{8,24},{12,76},{16,0},{20,84},{24,8},{28,92},{32,48}... | collective-permute-start | bytes 786440 | tf_op jit(solution)/shard_map/ppermute | solution.py:38
  47.4 9.5 %collective-permute-start.7 = (bf16[512,256]{1,0:T(8,128)(2,1)S(1)}, bf16[512,256]{1,0:T(8,128)(2,1)S(1)}, u32[]{:S(2)}, u32[]{:S(2)}) collective-permute-start(bf16[512,256]{1,0:T(8,128)(2,1)S(1)} %get-tuple-element.33), channel_id=1, source_target_pairs={{0,8},{4,36},{8,16},{12,44},{16,24},{20,52},{24,0},{28,60},{32,40}... | collective-permute-start | bytes 786440 | tf_op jit(solution)/shard_map/ppermute | solution.py:38
  59.0 5.2 %collective-permute-start.20 = (bf16[256,512]{1,0:T(8,128)(2,1)S(1)}, bf16[256,512]{1,0:T(8,128)(2,1)S(1)}, u32[]{:S(2)}, u32[]{:S(2)}) collective-permute-start(bf16[256,512]{1,0:T(8,128)(2,1)S(1)} %get-tuple-element.23), channel_id=1, source_target_pairs={{0,24},{4,100},{8,0},{12,108},{16,8},{20,116},{24,16},{28,124},{32... | collective-permute-start | bytes 786440 | tf_op jit(solution)/shard_map/ppermute | solution.py:38
  59.1 6.8 %collective-permute-start.21 = (bf16[256,512]{1,0:T(8,128)(2,1)S(1)}, bf16[256,512]{1,0:T(8,128)(2,1)S(1)}, u32[]{:S(2)}, u32[]{:S(2)}) collective-permute-start(bf16[256,512]{1,0:T(8,128)(2,1)S(1)} %get-tuple-element.23), channel_id=1, source_target_pairs={{0,16},{4,68},{8,24},{12,76},{16,0},{20,84},{24,8},{28,92},{32,48}... | collective-permute-start | bytes 786440 | tf_op jit(solution)/shard_map/ppermute | solution.py:38
  59.6 9.3 %collective-permute-start.22 = (bf16[256,512]{1,0:T(8,128)(2,1)S(1)}, bf16[256,512]{1,0:T(8,128)(2,1)S(1)}, u32[]{:S(2)}, u32[]{:S(2)}) collective-permute-start(bf16[256,512]{1,0:T(8,128)(2,1)S(1)} %get-tuple-element.23), channel_id=1, source_target_pairs={{0,8},{4,36},{8,16},{12,44},{16,24},{20,52},{24,0},{28,60},{32,40}... | collective-permute-start | bytes 786440 | tf_op jit(solution)/shard_map/ppermute | solution.py:38
  69.7 26.0 %collective-permute-start.25 = (bf16[1024,512]{1,0:T(8,128)(2,1)}, bf16[1024,512]{1,0:T(8,128)(2,1)S(1)}, u32[]{:S(2)}, u32[]{:S(2)}) collective-permute-start(bf16[1024,512]{1,0:T(8,128)(2,1)} %constant_dynamic-update-slice_fusion.refs_2_), channel_id=1, source_target_pairs={{0,96},{4,28},{8,104},{12,4},{16,112},{20,12},{24,120},{28,20},{32... | collective-permute-start | bytes 3145736 | tf_op jit(solution)/shard_map/ppermute | solution.py:34
  72.8 27.3 %collective-permute-start.23 = (bf16[1024,512]{1,0:T(8,128)(2,1)}, bf16[1024,512]{1,0:T(8,128)(2,1)S(1)}, u32[]{:S(2)}, u32[]{:S(2)}) collective-permute-start(bf16[1024,512]{1,0:T(8,128)(2,1)} %constant_dynamic-update-slice_fusion.refs_2_), channel_id=1, source_target_pairs={{0,32},{4,12},{8,40},{12,20},{16,48},{20,28},{24,56},{28,4},{32,64... | collective-permute-start | bytes 3145736 | tf_op jit(solution)/shard_map/ppermute | solution.py:34
  72.8 6.4 %collective-permute-start.10 = (f32[8,128]{1,0:T(8,128)S(1)}, f32[8,128]{1,0:T(8,128)S(1)}, u32[]{:S(2)}, u32[]{:S(2)}) collective-permute-start(f32[8,128]{1,0:T(8,128)S(1)} %get-tuple-element.22), channel_id=1, source_target_pairs={{0,4},{4,0},{1,5},{5,1},{2,6},{6,2},{3,7},{7,3},{8,12},{12,8},{9,1... | collective-permute-start | bytes 12296 | tf_op jit(solution)/shard_map/ppermute | solution.py:46
  79.2 3.8 %collective-permute-start.13 = (f32[8,128]{1,0:T(8,128)S(1)}, f32[8,128]{1,0:T(8,128)S(1)}, u32[]{:S(2)}, u32[]{:S(2)}) collective-permute-start(f32[8,128]{1,0:T(8,128)S(1)} %add.389), channel_id=1, source_target_pairs={{0,3},{1,0},{2,1},{3,2},{4,7},{5,4},{6,5},{7,6},{8,11},{9,8},{10,9... | collective-permute-start | bytes 12296 | tf_op jit(solution)/shard_map/ppermute | solution.py:42
  81.9 4.0 %collective-permute-start.12 = (f32[8,128]{1,0:T(8,128)S(1)}, f32[8,128]{1,0:T(8,128)S(1)}, u32[]{:S(2)}, u32[]{:S(2)}) collective-permute-start(f32[8,128]{1,0:T(8,128)S(1)} %add.389), channel_id=1, source_target_pairs={{0,2},{1,3},{2,0},{3,1},{4,6},{5,7},{6,4},{7,5},{8,10},{9,11},{10,... | collective-permute-start | bytes 12296 | tf_op jit(solution)/shard_map/ppermute | solution.py:42
  82.3 4.0 %collective-permute-start.11 = (f32[8,128]{1,0:T(8,128)S(1)}, f32[8,128]{1,0:T(8,128)S(1)}, u32[]{:S(2)}, u32[]{:S(2)}) collective-permute-start(f32[8,128]{1,0:T(8,128)S(1)} %add.389), channel_id=1, source_target_pairs={{0,1},{1,2},{2,3},{3,0},{4,5},{5,6},{6,7},{7,4},{8,9},{9,10},{10,1... | collective-permute-start | bytes 12296 | tf_op jit(solution)/shard_map/ppermute | solution.py:42
  86.2 3.7 %collective-permute-start.16 = (f32[8,128]{1,0:T(8,128)S(1)}, f32[8,128]{1,0:T(8,128)S(1)}, u32[]{:S(2)}, u32[]{:S(2)}) collective-permute-start(f32[8,128]{1,0:T(8,128)S(1)} %add_add_fusion.2), channel_id=1, source_target_pairs={{0,24},{4,100},{8,0},{12,108},{16,8},{20,116},{24,16},{28,124},{32... | collective-permute-start | bytes 12296 | tf_op jit(solution)/shard_map/ppermute | solution.py:38
  89.2 4.1 %collective-permute-start.15 = (f32[8,128]{1,0:T(8,128)S(1)}, f32[8,128]{1,0:T(8,128)S(1)}, u32[]{:S(2)}, u32[]{:S(2)}) collective-permute-start(f32[8,128]{1,0:T(8,128)S(1)} %add_add_fusion.2), channel_id=1, source_target_pairs={{0,16},{4,68},{8,24},{12,76},{16,0},{20,84},{24,8},{28,92},{32,48}... | collective-permute-start | bytes 12296 | tf_op jit(solution)/shard_map/ppermute | solution.py:38
  89.2 4.1 %collective-permute-start.14 = (f32[8,128]{1,0:T(8,128)S(1)}, f32[8,128]{1,0:T(8,128)S(1)}, u32[]{:S(2)}, u32[]{:S(2)}) collective-permute-start(f32[8,128]{1,0:T(8,128)S(1)} %add_add_fusion.2), channel_id=1, source_target_pairs={{0,8},{4,36},{8,16},{12,44},{16,24},{20,52},{24,0},{28,60},{32,40}... | collective-permute-start | bytes 12296 | tf_op jit(solution)/shard_map/ppermute | solution.py:38
  93.3 8.6 %collective-permute-start.19 = (f32[8,128]{1,0:T(8,128)S(1)}, f32[8,128]{1,0:T(8,128)S(1)}, u32[]{:S(2)}, u32[]{:S(2)}) collective-permute-start(f32[8,128]{1,0:T(8,128)S(1)} %add_add_fusion.1), channel_id=1, source_target_pairs={{0,96},{4,28},{8,104},{12,4},{16,112},{20,12},{24,120},{28,20},{32... | collective-permute-start | bytes 12296 | tf_op jit(solution)/shard_map/ppermute | solution.py:34
  95.0 7.5 %collective-permute-start.18 = (f32[8,128]{1,0:T(8,128)S(1)}, f32[8,128]{1,0:T(8,128)S(1)}, u32[]{:S(2)}, u32[]{:S(2)}) collective-permute-start(f32[8,128]{1,0:T(8,128)S(1)} %add_add_fusion.1), channel_id=1, source_target_pairs={{0,64},{4,20},{8,72},{12,28},{16,80},{20,4},{24,88},{28,12},{32,96... | collective-permute-start | bytes 12296 | tf_op jit(solution)/shard_map/ppermute | solution.py:34
  95.0 8.5 %collective-permute-start.17 = (f32[8,128]{1,0:T(8,128)S(1)}, f32[8,128]{1,0:T(8,128)S(1)}, u32[]{:S(2)}, u32[]{:S(2)}) collective-permute-start(f32[8,128]{1,0:T(8,128)S(1)} %add_add_fusion.1), channel_id=1, source_target_pairs={{0,32},{4,12},{8,40},{12,20},{16,48},{20,28},{24,56},{28,4},{32,64... | collective-permute-start | bytes 12296 | tf_op jit(solution)/shard_map/ppermute | solution.py:34
  95.6 24.0 %collective-permute-start.29 = (bf16[1024,512]{1,0:T(8,128)(2,1)}, bf16[1024,512]{1,0:T(8,128)(2,1)}, u32[]{:S(2)}, u32[]{:S(2)}) collective-permute-start(bf16[1024,512]{1,0:T(8,128)(2,1)} %constant_dynamic-update-slice_fusion.refs_2_), channel_id=1, source_target_pairs={{0,4},{4,0},{1,5},{5,1},{2,6},{6,2},{3,7},{7,3},{8,12},{12,8},{9,1... | collective-permute-start | bytes 3145736 | tf_op jit(solution)/shard_map/ppermute | solution.py:46
  100.1 15.2 %collective-permute-start.26 = (bf16[512,512]{1,0:T(8,128)(2,1)}, bf16[512,512]{1,0:T(8,128)(2,1)S(1)}, u32[]{:S(2)}, u32[]{:S(2)}) collective-permute-start(bf16[512,512]{1,0:T(8,128)(2,1)} %slice.124), channel_id=1, source_target_pairs={{0,96},{4,28},{8,104},{12,4},{16,112},{20,12},{24,120},{28,20},{32... | collective-permute-start | bytes 1572872 | tf_op jit(solution)/shard_map/ppermute | solution.py:34
  101.9 13.9 %collective-permute-start.24 = (bf16[512,512]{1,0:T(8,128)(2,1)}, bf16[512,512]{1,0:T(8,128)(2,1)}, u32[]{:S(2)}, u32[]{:S(2)}) collective-permute-start(bf16[512,512]{1,0:T(8,128)(2,1)} %slice.123), channel_id=1, source_target_pairs={{0,32},{4,12},{8,40},{12,20},{16,48},{20,28},{24,56},{28,4},{32,64... | collective-permute-start | bytes 1572872 | tf_op jit(solution)/shard_map/ppermute | solution.py:34
  102.4 17.2 %collective-permute-start.31 = (bf16[1024,512]{1,0:T(8,128)(2,1)S(1)}, bf16[1024,512]{1,0:T(8,128)(2,1)}, u32[]{:S(2)}, u32[]{:S(2)}) collective-permute-start(bf16[1024,512]{1,0:T(8,128)(2,1)S(1)} %collective-permute-done.25.refs_5_), channel_id=1, source_target_pairs={{0,4},{4,0},{1,5},{5,1},{2,6},{6,2},{3,7},{7,3},{8,12},{12,8},{9,1... | collective-permute-start | bytes 3145736 | tf_op jit(solution)/shard_map/ppermute | solution.py:46
  103.5 16.2 %collective-permute-start.30 = (bf16[1024,512]{1,0:T(8,128)(2,1)S(1)}, bf16[1024,512]{1,0:T(8,128)(2,1)}, u32[]{:S(2)}, u32[]{:S(2)}) collective-permute-start(bf16[1024,512]{1,0:T(8,128)(2,1)S(1)} %collective-permute-done.23.refs_4_), channel_id=1, source_target_pairs={{0,4},{4,0},{1,5},{5,1},{2,6},{6,2},{3,7},{7,3},{8,12},{12,8},{9,1... | collective-permute-start | bytes 3145736 | tf_op jit(solution)/shard_map/ppermute | solution.py:46
  115.3 22.3 %collective-permute-start.28 = (bf16[512,512]{1,0:T(8,128)(2,1)S(1)}, bf16[512,512]{1,0:T(8,128)(2,1)}, u32[]{:S(2)}, u32[]{:S(2)}) collective-permute-start(bf16[512,512]{1,0:T(8,128)(2,1)S(1)} %collective-permute-done.26.refs_3_), channel_id=1, source_target_pairs={{0,4},{4,0},{1,5},{5,1},{2,6},{6,2},{3,7},{7,3},{8,12},{12,8},{9,1... | collective-permute-start | bytes 1572872 | tf_op jit(solution)/shard_map/ppermute | solution.py:46
  115.8 21.8 %collective-permute-start.27 = (bf16[512,512]{1,0:T(8,128)(2,1)}, bf16[512,512]{1,0:T(8,128)(2,1)}, u32[]{:S(2)}, u32[]{:S(2)}) collective-permute-start(bf16[512,512]{1,0:T(8,128)(2,1)} %collective-permute-done.24.refs_2_), channel_id=1, source_target_pairs={{0,4},{4,0},{1,5},{5,1},{2,6},{6,2},{3,7},{7,3},{8,12},{12,8},{9,1... | collective-permute-start | bytes 1572872 | tf_op jit(solution)/shard_map/ppermute | solution.py:46
  (11 other events, 187.6 us)

commit v2 on v0

v2 whole, which is shorter than its diff:
```python
import jax
import jax.numpy as jnp
from jax import lax
from jax.experimental import pallas as pl
from jax.experimental.pallas import tpu as pltpu
from jax.sharding import Mesh
from jax.sharding import PartitionSpec as P

STEP = 1000
DP = ("x", "z", "c")
ROWS = 256
D = 512
VMEM = pl.BlockSpec(memory_space=pltpu.VMEM)
SMEM = pl.BlockSpec(memory_space=pltpu.SMEM)
HBM = pl.BlockSpec(memory_space=pltpu.HBM)
SHORT = pl.CostEstimate(flops=2**20, bytes_accessed=2**16, transcendentals=0)
LONG = pl.CostEstimate(flops=2**34, bytes_accessed=2**26, transcendentals=0)


def shift_first(k):
    pairs = []
    for x in range(4):
        for z in range(4):
            pairs.append(((x * 4 + z) * 2, (((x + k) % 4) * 4 + z) * 2))
            pairs.append(((x * 4 + z) * 2 + 1, (x * 4 + (z + k) % 4) * 2 + 1))
    return pairs


def shift_second(k):
    pairs = []
    for x in range(4):
        for z in range(4):
            pairs.append(((x * 4 + z) * 2, (x * 4 + (z + k) % 4) * 2))
            pairs.append(((x * 4 + z) * 2 + 1, (((x + k) % 4) * 4 + z) * 2 + 1))
    return pairs


def along_first(value, k):
    return lax.ppermute(value, DP, shift_first(k))


def along_second(value, k):
    return lax.ppermute(value, DP, shift_second(k))


def paired(value, axes, turn):
    pairs = ((1, 0, 3, 2), (3, 2, 1, 0))[turn]
    if axes == "y":
        return value + lax.ppermute(value, "y", list(enumerate(pairs)))
    moves = []
    for x in range(4):
        for z in range(4):
            for c in range(2):
                along_x = (axes == "first") == (c == 0)
                nx, nz = (pairs[x], z) if along_x else (x, pairs[z])
                moves.append(((x * 4 + z) * 2 + c, (nx * 4 + nz) * 2 + c))
    return value + lax.ppermute(value, DP, moves)


def summed(value, axes):
    return paired(paired(value, axes, 0), axes, 1)


def sibling(value):
    return lax.ppermute(value, "c", [(0, 1), (1, 0)])


def in_hbm(value):
    return pltpu.with_memory_space_constraint(value, pltpu.HBM)


def in_vmem(value):
    return pltpu.with_memory_space_constraint(value, pltpu.VMEM)


def after(value, *others):
    return lax.optimization_barrier((value, *others))[0]


def first_body(picks, blocks, up_ref, pre_ref, out, up_t, columns, arrived, up, up_arrived):
    copies = []
    up_copy = pltpu.make_async_copy(up_ref, up, up_arrived)
    up_copy.start()
    for i, pick in enumerate(picks):
        start = pl.multiple_of(blocks[pick] * ROWS, ROWS)
        copies.append(
            pltpu.make_async_copy(
                pre_ref.at[:, pl.ds(start, ROWS)],
                columns.at[:, pl.ds(i * ROWS, ROWS)],
                arrived.at[i],
            )
        )
        copies[-1].start()
    up_copy.wait()
    up_t[...] = up[...].T
    zero = jnp.zeros((), jnp.bfloat16)
    for i, copy in enumerate(copies):
        copy.wait()
        out[i * D : (i + 1) * D, :] = jnp.dot(
            up_t[...],
            jnp.maximum(columns[:, i * ROWS : (i + 1) * ROWS], zero),
            preferred_element_type=jnp.float32,
        ).astype(jnp.bfloat16)


def first_terms(preactivation, upstream, blocks, picks):
    tokens = preactivation.shape[0]

    def body(*refs):
        first_body(picks, *refs)

    return pl.pallas_call(
        body,
        out_shape=(
            jax.ShapeDtypeStruct((len(picks) * D, ROWS), jnp.bfloat16),
            jax.ShapeDtypeStruct((D, tokens), jnp.bfloat16),
        ),
        in_specs=[SMEM, HBM, HBM],
        out_specs=(VMEM, VMEM),
        scratch_shapes=[
            pltpu.VMEM((tokens, len(picks) * ROWS), jnp.bfloat16),
            pltpu.SemaphoreType.DMA((len(picks),)),
            pltpu.VMEM(upstream.shape, upstream.dtype),
            pltpu.SemaphoreType.DMA,
        ],
        compiler_params=pltpu.CompilerParams(vmem_limit_bytes=16 * 2**20),
        cost_estimate=LONG,
        name="first_terms",
    )(blocks, in_hbm(upstream), in_hbm(preactivation))


def terms_body(picks, parts, adds, blocks, up_ref, pre_ref, *refs):
    ins, outs = refs[: sum(map(len, adds))], refs[sum(map(len, adds)) :]
    zero = jnp.zeros((), jnp.bfloat16)
    picks = list(picks)
    for part, offsets, out in zip(parts, adds, outs):
        mine, ins = ins[: len(offsets)], ins[len(offsets) :]
        for k in range(part):
            start = pl.multiple_of(blocks[picks.pop(0)] * ROWS, ROWS)
            total = jnp.dot(
                up_ref[...],
                jnp.maximum(pre_ref[:, pl.ds(start, ROWS)], zero),
                preferred_element_type=jnp.float32,
            )
            for ref, offset in zip(mine, offsets):
                begin = offset + k * D
                total = total + ref[begin : begin + D, :].astype(jnp.float32)
            out[k * D : (k + 1) * D, :] = total.astype(jnp.bfloat16)


def terms(preactivation, up_t, blocks, picks, parts, adds=None, cost=SHORT):
    adds = adds or [()] * len(parts)
    offsets = [[begin for _, begin in group] for group in adds]

    def body(*refs):
        terms_body(picks, parts, offsets, *refs)

    return pl.pallas_call(
        body,
        out_shape=tuple(jax.ShapeDtypeStruct((p * D, ROWS), jnp.bfloat16) for p in parts),
        in_specs=[SMEM, VMEM, VMEM] + [VMEM] * sum(map(len, adds)),
        out_specs=tuple(VMEM for _ in parts),
        compiler_params=pltpu.CompilerParams(vmem_limit_bytes=16 * 2**20),
        cost_estimate=cost,
        name="terms",
    )(blocks, up_t, in_vmem(preactivation), *(a for group in adds for a, _ in group))


WIDE = 2048


def back_body(lo, count, tokens, up_ref, pre_ref, weight_ref, *refs):
    def step(weight, out):
        back = lax.dot_general(
            up_ref[...], weight[...], (((1,), (1,)), ((), ())), preferred_element_type=jnp.float32
        )
        start = pl.multiple_of((pl.program_id(0) + lo) * WIDE, WIDE)
        out[...] = jnp.where(
            pre_ref[:, pl.ds(start, WIDE)] > 0,
            back.astype(jnp.bfloat16),
            jnp.zeros((), jnp.bfloat16),
        )

    step(weight_ref, refs[-1])


def back_columns(lo, count, upstream, preactivation, weight, before):
    extra = [] if before is None else [before]
    tokens = preactivation.shape[0]

    def body(*refs):
        back_body(lo, count, tokens, *refs)

    return pl.pallas_call(
        body,
        out_shape=jax.ShapeDtypeStruct(preactivation.shape, jnp.bfloat16),
        grid=(count,),
        in_specs=[VMEM, VMEM, pl.BlockSpec((WIDE, D), lambda i: (i + lo, 0))]
        + [pl.BlockSpec(memory_space=pl.ANY)] * len(extra),
        out_specs=pl.BlockSpec((tokens, WIDE), lambda i: (0, i + lo)),
        input_output_aliases={3: 0} if extra else {},
        compiler_params=pltpu.CompilerParams(vmem_limit_bytes=24 * 2**20),
        cost_estimate=LONG,
        name="back_columns",
    )(upstream, in_vmem(preactivation), in_hbm(weight), *map(in_hbm, extra))


def update_body(
    block, g0, g1, g2, g3, g4, g5, first, second, weight,
    first_out, second_out, update_out, short_out, sums_out, own, arrived,
):
    beta_one = 0.9
    beta_two = 0.999
    bias_one = 1.0 - beta_one**STEP
    bias_two = 1.0 - beta_two**STEP
    start = pl.multiple_of(block[0] * ROWS, ROWS)
    fetch = pltpu.make_async_copy(weight.at[pl.ds(start, ROWS)], own, arrived)
    fetch.start()
    update_sq = jnp.zeros((8, 128), jnp.float32)
    weight_sq = jnp.zeros((8, 128), jnp.float32)
    for j in range(D // 128):
        part = slice(j * 128, (j + 1) * 128)
        total = g0[part, :].astype(jnp.float32)
        for ref in (g1, g2, g3, g4, g5):
            total = total + ref[part, :].astype(jnp.float32)
        gradient = total.T
        first_next = beta_one * first[:, part] + (1.0 - beta_one) * gradient
        second_next = beta_two * second[:, part] + (1.0 - beta_two) * gradient * gradient
        if j == 0:
            fetch.wait()
        own_weight = own[:, part].astype(jnp.float32)
        update = (
            first_next * (1.0 / bias_one) / (jnp.sqrt(second_next * (1.0 / bias_two)) + 1e-06)
            + 0.02 * own_weight
        )
        first_out[:, part] = first_next
        second_out[:, part] = second_next
        update_out[:, part] = update
        short_out[:, part] = update.astype(jnp.bfloat16)
        update_sq = update_sq + jnp.sum((update * update).reshape(ROWS // 8, 8, 128), axis=0)
        weight_sq = weight_sq + jnp.sum(
            (own_weight * own_weight).reshape(ROWS // 8, 8, 128), axis=0
        )
    sums_out[0:8, :] = update_sq
    sums_out[8:16, :] = weight_sq


def update_rows(block, parts, first, second, weight):
    long = jax.ShapeDtypeStruct((ROWS, D), jnp.float32)
    return pl.pallas_call(
        update_body,
        out_shape=(
            long,
            long,
            long,
            jax.ShapeDtypeStruct((ROWS, D), jnp.bfloat16),
            jax.ShapeDtypeStruct((16, 128), jnp.float32),
        ),
        in_specs=[SMEM]
        + [VMEM] * 6
        + [VMEM, VMEM, HBM],
        out_specs=(VMEM,) * 5,
        scratch_shapes=[pltpu.VMEM((ROWS, D), jnp.bfloat16), pltpu.SemaphoreType.DMA],
        compiler_params=pltpu.CompilerParams(vmem_limit_bytes=16 * 2**20),
        cost_estimate=SHORT,
        name="update_rows",
    )(block, *parts, first, second, in_hbm(weight))


def apply_body(picks, sizes, trust, blocks, sums_ref, weight, *refs):
    updates = refs[: len(sizes)]
    ready, stored = refs[-2:]
    if trust:
        update_ref, out, trust_out = refs[len(sizes)], refs[-4], refs[-3]
    else:
        out = refs[-3]
    update_sq = jnp.sum(sums_ref[0:8, :], axis=(0, 1), keepdims=True)
    weight_sq = jnp.sum(sums_ref[8:16, :], axis=(0, 1), keepdims=True)
    ratio = jnp.sqrt(weight_sq) / jnp.sqrt(update_sq)
    step = (0.02 * ratio).astype(jnp.bfloat16)
    places = [(update, k) for size, update in zip(sizes, updates) for k in range(size)]
    stores = []
    for i, (update, k) in enumerate(places):
        begin = pl.multiple_of(blocks[picks[i]] * ROWS, ROWS)
        ready[i] = weight[pl.ds(begin, ROWS), :] - step * update[k * ROWS : (k + 1) * ROWS, :]
        stores.append(
            pltpu.make_async_copy(ready.at[i], out.at[pl.ds(begin, ROWS)], stored.at[i])
        )
        stores[-1].start()
    if trust:
        trust_out[...] = ratio * update_ref[...]
    for store in stores:
        store.wait()


def apply_update(blocks, picks, sums, weight, updates, update, before):
    sizes = [u.shape[0] // ROWS for u in updates]
    count = sum(sizes)
    trust = [] if update is None else [update]
    extra = [] if before is None else [before]

    def body(*refs):
        apply_body(picks, sizes, bool(trust), *refs)

    return pl.pallas_call(
        body,
        out_shape=(jax.ShapeDtypeStruct(weight.shape, jnp.bfloat16),)
        + tuple(jax.ShapeDtypeStruct(u.shape, u.dtype) for u in trust),
        in_specs=[SMEM, VMEM, VMEM] + [VMEM] * (len(updates) + len(trust)) + [HBM] * len(extra),
        out_specs=(HBM,) + (VMEM,) * len(trust),
        input_output_aliases={3 + len(updates) + len(trust): 0} if extra else {},
        scratch_shapes=[
            pltpu.VMEM((count, ROWS, D), jnp.bfloat16),
            pltpu.SemaphoreType.DMA((count,)),
        ],
        compiler_params=pltpu.CompilerParams(vmem_limit_bytes=16 * 2**20),
        cost_estimate=SHORT,
        name="apply_update",
    )(blocks, sums, in_vmem(weight), *updates, *trust, *map(in_hbm, extra))


def joined(*values):
    rows = values[0].shape[0]

    def body(*refs):
        for k, ref in enumerate(refs[:-1]):
            refs[-1][k * rows : (k + 1) * rows, :] = ref[...]

    return pl.pallas_call(
        body,
        out_shape=jax.ShapeDtypeStruct((len(values) * rows, D), values[0].dtype),
        in_specs=[VMEM] * len(values),
        out_specs=VMEM,
        compiler_params=pltpu.CompilerParams(vmem_limit_bytes=16 * 2**20),
        cost_estimate=SHORT,
        name="joined",
    )(*values)


def taken(value, begin):
    rows = value.shape[0] // 2

    def body(ref, out):
        out[...] = ref[begin : begin + rows, :]

    return pl.pallas_call(
        body,
        out_shape=jax.ShapeDtypeStruct((rows, value.shape[1]), value.dtype),
        in_specs=[VMEM],
        out_specs=VMEM,
        compiler_params=pltpu.CompilerParams(vmem_limit_bytes=16 * 2**20),
        cost_estimate=SHORT,
        name="taken",
    )(value)


def added(*values):
    total = values[0].astype(jnp.float32)
    for value in values[1:]:
        total = total + value.astype(jnp.float32)
    return total.astype(jnp.bfloat16)


def own_unit(k):
    return [k % 4 * 4 + j for j in range(4)]


def other_unit(k):
    return [16 + k % 4 * 4 + j for j in range(4)]


def per_device(preactivation, upstream, weight, first_moment, second_moment):
    x, z, c = lax.axis_index("x"), lax.axis_index("z"), lax.axis_index("c")
    first = jnp.where(c == 0, x, z)
    second = jnp.where(c == 0, z, x)
    first_stride = jnp.where(c == 0, 8, 2)
    second_stride = jnp.where(c == 0, 2, 8)
    place = jnp.arange(32, dtype=jnp.int32)
    unit, member = (place >> 2) & 3, place & 3
    mine = place < 16
    on_first = (first + jnp.where(mine, unit, member)) & 3
    on_second = (second + jnp.where(mine, member, unit)) & 3
    blocks = on_first * first_stride + on_second * second_stride + jnp.where(mine, c, 1 - c)

    near_free = lambda unit: unit(1)[2:] + unit(-1)[:2]
    near_late = lambda unit: unit(1)[:2] + unit(-1)[2:]

    send_far, up_t = first_terms(preactivation, upstream, blocks, other_unit(2))

    def part(picks, parts, adds=None, then=(), cost=SHORT):
        return terms(preactivation, after(up_t, *then), blocks, picks, parts, adds, cost)

    got_far = sibling(send_far)
    keep_far = part(own_unit(2), (2, 2), then=(send_far,), cost=LONG)
    half = 2 * D
    (send_free,) = part(near_free(other_unit), (4,), then=keep_far)
    keep_far = [after(v, send_free) for v in keep_far]
    far_low = added(keep_far[0], got_far[:half])
    far_high = added(keep_far[1], got_far[half:])
    from_left = along_first(far_low, 1)
    from_right = along_first(far_high, -1)

    got_free = sibling(send_free)
    (send_late,) = part(near_late(other_unit), (4,), then=(far_low, far_high), cost=LONG)
    got_late = sibling(send_late)
    right_high, left_low = part(
        near_free(own_unit), (2, 2), [[(got_free, 0)], [(got_free, half)]], then=(send_late,)
    )
    sum_left_high = along_first(right_high, 1)
    sum_right_low = along_first(left_low, -1)
    (send_here,) = part(other_unit(0), (4,), then=(right_high, left_low), cost=LONG)
    got_here = sibling(send_here)
    right_low, left_high = part(
        near_late(own_unit),
        (2, 2),
        [[(got_late, 0), (from_left, 0)], [(got_late, half), (from_right, 0)]],
        then=(send_here,),
    )
    sum_left_low = along_first(right_low, 1)
    sum_right_high = along_first(left_high, -1)
    input_grad = back_columns(
        0, 2, after(upstream, right_low, left_high), preactivation, weight, None
    )
    (here,) = part(own_unit(0), (4,), [[(got_here, 0)]], then=(input_grad,))
    near = (
        added(here[D:half], sum_left_low[D:], sum_right_low[D:]),
        added(here[half : half + D], sum_left_high[:D], sum_right_high[:D]),
        added(here[half + D :], sum_left_high[D:], sum_right_high[D:]),
    )
    got = [along_second(v, j) for v, j in zip(near, (1, 2, 3))]
    input_grad = back_columns(2, 2, after(upstream, *near), preactivation, weight, input_grad)
    first_next, second_next, update, short, sums = update_rows(
        blocks,
        [here, sum_left_low, sum_right_low, *got],
        first_moment,
        second_moment,
        after(weight, input_grad),
    )

    rows = [along_second(short, -j) for j in (1, 2, 3)]
    sums = summed(sums, "first")
    mine = joined(after(short, sums), *rows)
    mine_other = sibling(mine)
    near_left = along_first(mine, 1)
    near_right = along_first(mine, -1)
    sums = paired(summed(after(sums, mine), "second"), "y", 0)
    near_left = after(near_left, sums, mine_other)
    near_right = after(near_right, sums, mine_other)
    low = taken(near_left, 0)
    high = taken(near_right, 2 * ROWS)
    far_left = along_first(low, 1)
    far_right = along_first(high, -1)
    near_left, near_right = after(near_left, low, high), after(near_right, low, high)
    sums = paired(after(sums, low, high), "y", 1)
    sums = sums + sibling(sums)
    far_left, far_right = after(far_left, sums), after(far_right, sums)
    new_weight, trust_step = apply_update(
        blocks,
        own_unit(0) + other_unit(0) + own_unit(-1) + own_unit(1) + other_unit(-1) + other_unit(1),
        sums,
        weight,
        [mine, mine_other, near_left, near_right, sibling(near_left), sibling(near_right)],
        update,
        None,
    )
    (new_weight,) = apply_update(
        blocks,
        own_unit(2) + other_unit(2),
        sums,
        weight,
        [far_left, far_right, sibling(far_left), sibling(far_right)],
        None,
        new_weight,
    )
    return (input_grad, new_weight, first_next, second_next, trust_step)


def solution(mesh):
    split = Mesh(mesh.devices.reshape(4, 4, 2, 4), ("x", "z", "c", "y"))
    rows = P(("y", "x", "z", "c"), None)
    return jax.shard_map(
        per_device,
        mesh=split,
        in_specs=(P(DP, "y"), P(DP, None), P("y", None), rows, rows),
        out_specs=(P(DP, "y"), P("y", None), rows, rows, rows),
        check_vma=False,
    )
```

time: 250 us -> 104 us (0.42)
  waiting for transfers between devices: 133 us -> 27 us
  blocking collectives: 66.1 us -> 0 us
  starting transfers between devices: 0.08 us -> 41.6 us
  Pallas kernels: 0 us -> 33.4 us
  matrix products: 21.7 us -> 0 us
  between operations: 15.4 us -> 1.07 us
  local copies, waits for them, and re-layouts: 8.29 us -> 0.03 us
  other arithmetic: 4.96 us -> 0.61 us
    reduce_scatter x1 -> x0, waiting for transfers between devices: 94.4 us -> none  [per_device(): lax.psum_scatter(lax.dot_general(hidden, upstream, (((0,), (0,)), ((), ()...]
    psum x1 -> x0, blocking collectives: 66.1 us -> none  [per_device(): weight_sq, update_sq = lax.psum((weight_local, update_local), ('dp', 'mp'))]
    ppermute x0 -> x32, starting transfers between devices: none -> 41.6 us  [the longest x10 16.5 us: along_first(): return lax.ppermute(value, DP, shift_first(k))]
    all_gather x1 -> x0, waiting for transfers between devices: 38.4 us -> none  [per_device(): new_weight = lax.all_gather(new_rows, 'dp', axis=0, tiled=True)]
    pallas_call x0 -> x16, Pallas kernels: none -> 33.4 us  [the longest x2 10.7 us: back_columns(): pl.pallas_call(body, out_shape=jax.ShapeDtypeStruct(preactivation.shape,...]
    ppermute x0 -> x32, waiting for transfers between devices: none -> 27 us  [the longest x4 11.1 us: paired(): return value + lax.ppermute(value, DP, moves)]
    dot_general x2 -> x0, matrix products: 21.7 us -> none  [the longest x1 11.6 us: per_device(): lax.dot_general(upstream, weight, (((1,), (1,)), ((), ())), preferred_ele...]
    unnamed x7 -> x12, local copies, waits for them, and re-layouts: 8.29 us -> 0.03 us
  transfers between devices with their start and end apart: 2 -> 32, of which waited for: 2 -> 15; matrix products, arithmetic and copies ran while one was open for 5% -> 0% of each run, Pallas kernels for 0% -> 23%
where the time goes in v2:
time: 104 us
  starting transfers between devices  41.6 us (40%)
  Pallas kernels  33.4 us (32%)
  waiting for transfers between devices  27 us (26%)
  between operations  1.07 us (1%)
    ppermute x10, starting transfers between devices, along_first(): return lax.ppermute(value, DP, shift_first(k))  16.5 us
    ppermute x10, starting transfers between devices, sibling(): return lax.ppermute(value, 'c', [(0, 1), (1, 0)])  11.9 us
    ppermute x4, waiting for transfers between devices, paired(): return value + lax.ppermute(value, DP, moves)  11.1 us
    pallas_call x2, Pallas kernels, back_columns(): pl.pallas_call(body, out_shape=jax.ShapeDtypeStruct(preactivation.shape,...  10.7 us
    pallas_call x7, Pallas kernels, terms(): pl.pallas_call(body, out_shape=tuple((jax.ShapeDtypeStruct((p * D, ROWS),...  8.94 us
    ppermute x10, waiting for transfers between devices, along_first(): return lax.ppermute(value, DP, shift_first(k))  8.56 us
    pallas_call x2, Pallas kernels, apply_update(): pl.pallas_call(body, out_shape=(jax.ShapeDtypeStruct(weight.shape, jnp.bf...  6.4 us
    ppermute x6, starting transfers between devices, along_second(): return lax.ppermute(value, DP, shift_second(k))  6.37 us
  transfers between devices with their start and end apart: 32, of which 15 were waited for; matrix products, arithmetic and copies ran while one was open for 0% of the time, Pallas kernels for 23%

profile of v2, /device:TPU:1, one launch (start us, length us, event | category | flops | bytes accessed | tf_op | source)
XLA Modules:
  0.0 103.7 jit_solution(16287903370394963102)
XLA Ops:
  0.7 4.1 %first_terms.1 = (bf16[2048,256]{1,0:T(8,128)(2,1)S(1)}, bf16[512,448]{1,0:T(8,128)(2,1)S(1)}) custom-call(s32[32]{0:T(128)S(1)} %fusion.3.refs_0_.block, bf16[448,512]{1,0:T(8,128)(2,1)} %refs_0_.1, bf16[448,8192]{1,0:T(8,128)(2,1)} %refs_1_.5), custom_call_target="tpu_custom_call" | custom-call | flops 17179869184 | bytes 67108864 | tf_op jit(solution)/shard_map/first_terms/pallas_call | solution.py:112
  4.8 1.5 %collective-permute-start = (bf16[2048,256]{1,0:T(8,128)(2,1)S(1)}, bf16[2048,256]{1,0:T(8,128)(2,1)S(1)}, u32[]{:S(2)}, u32[]{:S(2)}) collective-permute-start(bf16[2048,256]{1,0:T(8,128)(2,1)S(1)} %get-tuple-element.42), channel_id=1, source_target_pairs={{0,4},{4,0},{1,5},{5,1},{2,6},{6,2},{3,7},{7,3},{8,12},{12,8},{9,1... | collective-permute-start | bytes 3145736 | tf_op jit(solution)/shard_map/ppermute | solution.py:65
  6.3 1.3 %terms.7 = (bf16[1024,256]{1,0:T(8,128)(2,1)S(1)}, bf16[1024,256]{1,0:T(8,128)(2,1)S(1)}) custom-call(s32[32]{0:T(128)S(1)} %fusion.3.refs_0_.block, bf16[512,448]{1,0:T(8,128)(2,1)S(1)} %get-tuple-element.58.refs_1_, bf16[448,8192]{1,0:T(8,128)(2,1)S(1)} %copy-done), custom_call_target="tpu_custom_call" | custom-call | flops 17179869184 | bytes 67108864 | tf_op jit(solution)/shard_map/terms/pallas_call | solution.py:158
  9.2 3.9 %collective-permute-start.4 = (bf16[1024,256]{1,0:T(8,128)(2,1)S(1)}, bf16[1024,256]{1,0:T(8,128)(2,1)S(1)}, u32[]{:S(2)}, u32[]{:S(2)}) collective-permute-start(bf16[1024,256]{1,0:T(8,128)(2,1)S(1)} %get-tuple-element.80), channel_id=1, source_target_pairs={{0,96},{4,28},{8,104},{12,4},{16,112},{20,12},{24,120},{28,20},{32... | collective-permute-start | bytes 1572872 | tf_op jit(solution)/shard_map/ppermute | solution.py:39
  14.4 1.3 %terms.10 = (bf16[1024,256]{1,0:T(8,128)(2,1)S(1)}, bf16[1024,256]{1,0:T(8,128)(2,1)S(1)}) custom-call(s32[32]{0:T(128)S(1)} %fusion.3.refs_0_.block, bf16[512,448]{1,0:T(8,128)(2,1)S(1)} %get-tuple-element.58.refs_1_, bf16[448,8192]{1,0:T(8,128)(2,1)S(1)} %copy-done, bf16[2048,256]{1,0:T(8,128)(2,1)S(1)} %collective-permute-done.1.refs_3_.refs_4_, ...), custom_call_target="tpu_custom_call" | custom-call | flops 1048576 | bytes 65536 | tf_op jit(solution)/shard_map/terms/pallas_call | solution.py:158
  15.8 2.7 %collective-permute-start.7 = (bf16[1024,256]{1,0:T(8,128)(2,1)S(1)}, bf16[1024,256]{1,0:T(8,128)(2,1)S(1)}, u32[]{:S(2)}, u32[]{:S(2)}) collective-permute-start(bf16[1024,256]{1,0:T(8,128)(2,1)S(1)} %get-tuple-element.52), channel_id=1, source_target_pairs={{0,96},{4,28},{8,104},{12,4},{16,112},{20,12},{24,120},{28,20},{32... | collective-permute-start | bytes 1572872 | tf_op jit(solution)/shard_map/ppermute | solution.py:39
  18.6 1.3 %terms.11 = bf16[2048,256]{1,0:T(8,128)(2,1)S(1)} custom-call(s32[32]{0:T(128)S(1)} %fusion.3.refs_0_.block, bf16[512,448]{1,0:T(8,128)(2,1)S(1)} %get-tuple-element.58.refs_1_, bf16[448,8192]{1,0:T(8,128)(2,1)S(1)} %copy-done), custom_call_target="tpu_custom_call" | custom-call | flops 17179869184 | bytes 67108864 | tf_op jit(solution)/shard_map/terms/pallas_call | solution.py:158
  20.4 2.3 %collective-permute-done.3.refs_4_ = bf16[1024,256]{1,0:T(8,128)(2,1)S(1)} collective-permute-done((bf16[1024,256]{1,0:T(8,128)(2,1)S(1)}, bf16[1024,256]{1,0:T(8,128)(2,1)S(1)}, u32[]{:S(2)}, u32[]{:S(2)}) %collective-permute-start.3) | collective-permute-done | bytes 524320 | tf_op jit(solution)/shard_map/ppermute | solution.py:39
  22.7 1.3 %terms.12 = (bf16[1024,256]{1,0:T(8,128)(2,1)S(1)}, bf16[1024,256]{1,0:T(8,128)(2,1)S(1)}) custom-call(s32[32]{0:T(128)S(1)} %fusion.3.refs_0_.block, bf16[512,448]{1,0:T(8,128)(2,1)S(1)} %get-tuple-element.58.refs_1_, bf16[448,8192]{1,0:T(8,128)(2,1)S(1)} %copy-done, bf16[2048,256]{1,0:T(8,128)(2,1)S(1)} %collective-permute-done.2.refs_3_.refs_5_, ...), custom_call_target="tpu_custom_call" | custom-call | flops 1048576 | bytes 65536 | tf_op jit(solution)/shard_map/terms/pallas_call | solution.py:158
  24.1 2.7 %collective-permute-start.9 = (bf16[1024,256]{1,0:T(8,128)(2,1)S(1)}, bf16[1024,256]{1,0:T(8,128)(2,1)S(1)}, u32[]{:S(2)}, u32[]{:S(2)}) collective-permute-start(bf16[1024,256]{1,0:T(8,128)(2,1)S(1)} %get-tuple-element.56), channel_id=1, source_target_pairs={{0,96},{4,28},{8,104},{12,4},{16,112},{20,12},{24,120},{28,20},{32... | collective-permute-start | bytes 1572872 | tf_op jit(solution)/shard_map/ppermute | solution.py:39
  26.8 5.1 %back_columns.2.refs_3_ = bf16[448,8192]{1,0:T(8,128)(2,1)} custom-call(bf16[448,512]{1,0:T(8,128)(2,1)S(1)} %copy-done.3, bf16[448,8192]{1,0:T(8,128)(2,1)S(1)} %copy-done, bf16[8192,512]{1,0:T(8,128)(2,1)} %refs_2_.23), custom_call_target="tpu_custom_call" | custom-call | flops 17179869184 | bytes 67108864 | tf_op jit(solution)/shard_map/back_columns/pallas_call | solution.py:194
  34.2 2.5 %collective-permute-start.12 = (bf16[512,256]{1,0:T(8,128)(2,1)S(1)}, bf16[512,256]{1,0:T(8,128)(2,1)S(1)}, u32[]{:S(2)}, u32[]{:S(2)}) collective-permute-start(bf16[512,256]{1,0:T(8,128)(2,1)S(1)} %get-tuple-element.77), channel_id=1, source_target_pairs={{0,24},{4,100},{8,0},{12,108},{16,8},{20,116},{24,16},{28,124},{32... | collective-permute-start | bytes 786440 | tf_op jit(solution)/shard_map/ppermute | solution.py:43
  37.8 5.6 %back_columns.3 = bf16[448,8192]{1,0:T(8,128)(2,1)} custom-call(bf16[448,512]{1,0:T(8,128)(2,1)S(1)} %copy-done.3, bf16[448,8192]{1,0:T(8,128)(2,1)S(1)} %copy-done, bf16[8192,512]{1,0:T(8,128)(2,1)} %refs_2_.23, bf16[448,8192]{1,0:T(8,128)(2,1)} %back_columns.2.refs_3_), custom_call_target="tpu_custom_call", output_to_operand_aliasing={{}: (3, {})} | custom-call | flops 17179869184 | bytes 67108864 | tf_op jit(solution)/shard_map/back_columns/pallas_call | solution.py:194
  43.6 3.0 %collective-permute-done.10.g3 = bf16[512,256]{1,0:T(8,128)(2,1)S(1)} collective-permute-done((bf16[512,256]{1,0:T(8,128)(2,1)S(1)}, bf16[512,256]{1,0:T(8,128)(2,1)S(1)}, u32[]{:S(2)}, u32[]{:S(2)}) %collective-permute-start.10) | collective-permute-done | bytes 262176 | tf_op jit(solution)/shard_map/ppermute | solution.py:43
  46.6 3.1 %update_rows.1 = (f32[256,512]{1,0:T(8,128)}, f32[256,512]{1,0:T(8,128)}, f32[256,512]{1,0:T(8,128)S(1)}, bf16[256,512]{1,0:T(8,128)(2,1)S(1)}, f32[16,128]{1,0:T(8,128)S(1)}) custom-call(s32[32]{0:T(128)S(1)} %fusion.3.refs_0_.block, bf16[2048,256]{1,0:T(8,128)(2,1)S(1)} %terms.13.g0, bf16[1024,256]{1,0:T(8,128)(2,1)S(1)} %collective-permute-done.6.g1, ...), custom_call_target="tpu_custom_call" | custom-call | flops 1048576 | bytes 65536 | tf_op jit(solution)/shard_map/update_rows/pallas_call | solution.py:250
  49.8 1.5 %collective-permute-start.16 = (bf16[256,512]{1,0:T(8,128)(2,1)S(1)}, bf16[256,512]{1,0:T(8,128)(2,1)S(1)}, u32[]{:S(2)}, u32[]{:S(2)}) collective-permute-start(bf16[256,512]{1,0:T(8,128)(2,1)S(1)} %get-tuple-element.63.refs_0_), channel_id=1, source_target_pairs={{0,16},{4,68},{8,24},{12,76},{16,0},{20,84},{24,8},{28,92},{32,48}... | collective-permute-start | bytes 786440 | tf_op jit(solution)/shard_map/ppermute | solution.py:43
  52.4 2.5 %collective-permute-done.13 = f32[16,128]{1,0:T(8,128)S(1)} collective-permute-done((f32[16,128]{1,0:T(8,128)S(1)}, f32[16,128]{1,0:T(8,128)S(1)}, u32[]{:S(2)}, u32[]{:S(2)}) %collective-permute-start.13) | collective-permute-done | bytes 8224 | tf_op jit(solution)/shard_map/ppermute | solution.py:57
  54.9 2.8 %collective-permute-start.14 = (f32[16,128]{1,0:T(8,128)S(1)}, f32[16,128]{1,0:T(8,128)S(1)}, u32[]{:S(2)}, u32[]{:S(2)}) collective-permute-start(f32[16,128]{1,0:T(8,128)S(1)} %add.77), channel_id=1, source_target_pairs={{0,96},{4,28},{8,104},{12,20},{16,112},{20,12},{24,120},{28,4},{32... | collective-permute-start | bytes 24584 | tf_op jit(solution)/shard_map/ppermute | solution.py:57
  57.7 1.5 %collective-permute-done.14 = f32[16,128]{1,0:T(8,128)S(1)} collective-permute-done((f32[16,128]{1,0:T(8,128)S(1)}, f32[16,128]{1,0:T(8,128)S(1)}, u32[]{:S(2)}, u32[]{:S(2)}) %collective-permute-start.14) | collective-permute-done | bytes 8224 | tf_op jit(solution)/shard_map/ppermute | solution.py:57
  60.1 3.9 %collective-permute-start.23 = (bf16[1024,512]{1,0:T(8,128)(2,1)S(1)}, bf16[1024,512]{1,0:T(8,128)(2,1)S(1)}, u32[]{:S(2)}, u32[]{:S(2)}) collective-permute-start(bf16[1024,512]{1,0:T(8,128)(2,1)S(1)} %joined.1.refs_3_), channel_id=1, source_target_pairs={{0,96},{4,28},{8,104},{12,4},{16,112},{20,12},{24,120},{28,20},{32... | collective-permute-start | bytes 3145736 | tf_op jit(solution)/shard_map/ppermute | solution.py:39
  64.0 5.8 %collective-permute-start.22 = (bf16[1024,512]{1,0:T(8,128)(2,1)S(1)}, bf16[1024,512]{1,0:T(8,128)(2,1)S(1)}, u32[]{:S(2)}, u32[]{:S(2)}) collective-permute-start(bf16[1024,512]{1,0:T(8,128)(2,1)S(1)} %joined.1.refs_3_), channel_id=1, source_target_pairs={{0,4},{4,0},{1,5},{5,1},{2,6},{6,2},{3,7},{7,3},{8,12},{12,8},{9,1... | collective-permute-start | bytes 3145736 | tf_op jit(solution)/shard_map/ppermute | solution.py:65
  70.2 2.9 %collective-permute-done.18 = f32[16,128]{1,0:T(8,128)S(1)} collective-permute-done((f32[16,128]{1,0:T(8,128)S(1)}, f32[16,128]{1,0:T(8,128)S(1)}, u32[]{:S(2)}, u32[]{:S(2)}) %collective-permute-start.18) | collective-permute-done | bytes 8224 | tf_op jit(solution)/shard_map/ppermute | solution.py:57
  73.1 4.2 %collective-permute-done.19 = f32[16,128]{1,0:T(8,128)S(1)} collective-permute-done((f32[16,128]{1,0:T(8,128)S(1)}, f32[16,128]{1,0:T(8,128)S(1)}, u32[]{:S(2)}, u32[]{:S(2)}) %collective-permute-start.19) | collective-permute-done | bytes 8224 | tf_op jit(solution)/shard_map/ppermute | solution.py:57
  77.3 1.3 %collective-permute-start.20 = (f32[16,128]{1,0:T(8,128)S(1)}, f32[16,128]{1,0:T(8,128)S(1)}, u32[]{:S(2)}, u32[]{:S(2)}) collective-permute-start(f32[16,128]{1,0:T(8,128)S(1)} %add.80), channel_id=1, source_target_pairs={{0,1},{1,0},{2,3},{3,2},{4,5},{5,4},{6,7},{7,6},{8,9},{9,8},{10,11... | collective-permute-start | bytes 24584 | tf_op jit(solution)/shard_map/ppermute | solution.py:49
  78.6 1.5 %collective-permute-done.20 = f32[16,128]{1,0:T(8,128)S(1)} collective-permute-done((f32[16,128]{1,0:T(8,128)S(1)}, f32[16,128]{1,0:T(8,128)S(1)}, u32[]{:S(2)}, u32[]{:S(2)}) %collective-permute-start.20) | collective-permute-done | bytes 8224 | tf_op jit(solution)/shard_map/ppermute | solution.py:49
  80.1 2.4 %collective-permute-start.27 = (bf16[512,512]{1,0:T(8,128)(2,1)S(1)}, bf16[512,512]{1,0:T(8,128)(2,1)S(1)}, u32[]{:S(2)}, u32[]{:S(2)}) collective-permute-start(bf16[512,512]{1,0:T(8,128)(2,1)S(1)} %taken.3), channel_id=1, source_target_pairs={{0,96},{4,28},{8,104},{12,4},{16,112},{20,12},{24,120},{28,20},{32... | collective-permute-start | bytes 1572872 | tf_op jit(solution)/shard_map/ppermute | solution.py:39
  82.5 2.5 %collective-permute-done.21.ref.refs_5_ = bf16[1024,512]{1,0:T(8,128)(2,1)S(1)} collective-permute-done((bf16[1024,512]{1,0:T(8,128)(2,1)S(1)}, bf16[1024,512]{1,0:T(8,128)(2,1)S(1)}, u32[]{:S(2)}, u32[]{:S(2)}) %collective-permute-start.21) | collective-permute-done | bytes 1048608 | tf_op jit(solution)/shard_map/ppermute | solution.py:39
  86.6 2.7 %collective-permute-start.24 = (f32[16,128]{1,0:T(8,128)S(1)}, f32[16,128]{1,0:T(8,128)S(1)}, u32[]{:S(2)}, u32[]{:S(2)}) collective-permute-start(f32[16,128]{1,0:T(8,128)S(1)} %add.81), channel_id=1, source_target_pairs={{0,3},{1,2},{2,1},{3,0},{4,7},{5,6},{6,5},{7,4},{8,11},{9,10},{10,... | collective-permute-start | bytes 24584 | tf_op jit(solution)/shard_map/ppermute | solution.py:49
  92.7 3.1 %collective-permute-done.26.refs_3_ = bf16[512,512]{1,0:T(8,128)(2,1)S(1)} collective-permute-done((bf16[512,512]{1,0:T(8,128)(2,1)S(1)}, bf16[512,512]{1,0:T(8,128)(2,1)S(1)}, u32[]{:S(2)}, u32[]{:S(2)}) %collective-permute-start.26) | collective-permute-done | bytes 524320 | tf_op jit(solution)/shard_map/ppermute | solution.py:39
  95.8 1.3 %collective-permute-start.28 = (bf16[512,512]{1,0:T(8,128)(2,1)S(1)}, bf16[512,512]{1,0:T(8,128)(2,1)S(1)}, u32[]{:S(2)}, u32[]{:S(2)}) collective-permute-start(bf16[512,512]{1,0:T(8,128)(2,1)S(1)} %collective-permute-done.26.refs_3_), channel_id=1, source_target_pairs={{0,4},{4,0},{1,5},{5,1},{2,6},{6,2},{3,7},{7,3},{8,12},{12,8},{9,1... | collective-permute-start | bytes 1572872 | tf_op jit(solution)/shard_map/ppermute | solution.py:65
  97.1 4.3 %apply_update.2 = (bf16[8192,512]{1,0:T(8,128)(2,1)}, f32[256,512]{1,0:T(8,128)}) custom-call(s32[32]{0:T(128)S(1)} %fusion.3.refs_0_.block, f32[16,128]{1,0:T(8,128)S(1)} %add.83.refs_1_, bf16[8192,512]{1,0:T(8,128)(2,1)S(1)} %bitcast.1, bf16[1024,512]{1,0:T(8,128)(2,1)S(1)} %joined.1.refs_3_, bf16[1024,512]{1,0:T(8,128)(2,1)S(1)} %collective-permute-done.22.refs_4_, ...), custom_call_target="tpu_custom_call" | custom-call | flops 1048576 | bytes 65536 | tf_op jit(solution)/shard_map/apply_update/pallas_call | solution.py:305
  101.4 2.1 %apply_update.3 = bf16[8192,512]{1,0:T(8,128)(2,1)} custom-call(s32[32]{0:T(128)S(1)} %fusion.3.refs_0_.block, f32[16,128]{1,0:T(8,128)S(1)} %add.83.refs_1_, bf16[8192,512]{1,0:T(8,128)(2,1)S(1)} %bitcast.1, bf16[512,512]{1,0:T(8,128)(2,1)S(1)} %collective-permute-done.26.refs_3_, ...), custom_call_target="tpu_custom_call", output_to_operand_aliasing={{}: (7, {})} | custom-call | flops 1048576 | bytes 65536 | tf_op jit(solution)/shard_map/apply_update/pallas_call | solution.py:305
  (71 shorter events, 14.7 us)
Async XLA Ops:
  4.8 4.1 %collective-permute-start = (bf16[2048,256]{1,0:T(8,128)(2,1)S(1)}, bf16[2048,256]{1,0:T(8,128)(2,1)S(1)}, u32[]{:S(2)}, u32[]{:S(2)}) collective-permute-start(bf16[2048,256]{1,0:T(8,128)(2,1)S(1)} %get-tuple-element.42), channel_id=1, source_target_pairs={{0,4},{4,0},{1,5},{5,1},{2,6},{6,2},{3,7},{7,3},{8,12},{12,8},{9,1... | collective-permute-start | bytes 3145736 | tf_op jit(solution)/shard_map/ppermute | solution.py:65
  8.8 5.6 %collective-permute-start.1 = (bf16[2048,256]{1,0:T(8,128)(2,1)S(1)}, bf16[2048,256]{1,0:T(8,128)(2,1)S(1)}, u32[]{:S(2)}, u32[]{:S(2)}) collective-permute-start(bf16[2048,256]{1,0:T(8,128)(2,1)S(1)} %terms.8), channel_id=1, source_target_pairs={{0,4},{4,0},{1,5},{5,1},{2,6},{6,2},{3,7},{7,3},{8,12},{12,8},{9,1... | collective-permute-start | bytes 3145736 | tf_op jit(solution)/shard_map/ppermute | solution.py:65
  9.2 10.6 %collective-permute-start.4 = (bf16[1024,256]{1,0:T(8,128)(2,1)S(1)}, bf16[1024,256]{1,0:T(8,128)(2,1)S(1)}, u32[]{:S(2)}, u32[]{:S(2)}) collective-permute-start(bf16[1024,256]{1,0:T(8,128)(2,1)S(1)} %get-tuple-element.80), channel_id=1, source_target_pairs={{0,96},{4,28},{8,104},{12,4},{16,112},{20,12},{24,120},{28,20},{32... | collective-permute-start | bytes 1572872 | tf_op jit(solution)/shard_map/ppermute | solution.py:39
  13.1 9.5 %collective-permute-start.3 = (bf16[1024,256]{1,0:T(8,128)(2,1)S(1)}, bf16[1024,256]{1,0:T(8,128)(2,1)S(1)}, u32[]{:S(2)}, u32[]{:S(2)}) collective-permute-start(bf16[1024,256]{1,0:T(8,128)(2,1)S(1)} %get-tuple-element.81), channel_id=1, source_target_pairs={{0,32},{4,12},{8,40},{12,20},{16,48},{20,28},{24,56},{28,4},{32,64... | collective-permute-start | bytes 1572872 | tf_op jit(solution)/shard_map/ppermute | solution.py:39
  15.7 17.5 %collective-permute-start.8 = (bf16[1024,256]{1,0:T(8,128)(2,1)S(1)}, bf16[1024,256]{1,0:T(8,128)(2,1)S(1)}, u32[]{:S(2)}, u32[]{:S(2)}) collective-permute-start(bf16[1024,256]{1,0:T(8,128)(2,1)S(1)} %get-tuple-element.51), channel_id=1, source_target_pairs={{0,32},{4,12},{8,40},{12,20},{16,48},{20,28},{24,56},{28,4},{32,64... | collective-permute-start | bytes 1572872 | tf_op jit(solution)/shard_map/ppermute | solution.py:39
  15.8 17.4 %collective-permute-start.7 = (bf16[1024,256]{1,0:T(8,128)(2,1)S(1)}, bf16[1024,256]{1,0:T(8,128)(2,1)S(1)}, u32[]{:S(2)}, u32[]{:S(2)}) collective-permute-start(bf16[1024,256]{1,0:T(8,128)(2,1)S(1)} %get-tuple-element.52), channel_id=1, source_target_pairs={{0,96},{4,28},{8,104},{12,4},{16,112},{20,12},{24,120},{28,20},{32... | collective-permute-start | bytes 1572872 | tf_op jit(solution)/shard_map/ppermute | solution.py:39
  18.5 4.1 %collective-permute-start.2 = (bf16[2048,256]{1,0:T(8,128)(2,1)S(1)}, bf16[2048,256]{1,0:T(8,128)(2,1)S(1)}, u32[]{:S(2)}, u32[]{:S(2)}) collective-permute-start(bf16[2048,256]{1,0:T(8,128)(2,1)S(1)} %terms.9), channel_id=1, source_target_pairs={{0,4},{4,0},{1,5},{5,1},{2,6},{6,2},{3,7},{7,3},{8,12},{12,8},{9,1... | collective-permute-start | bytes 3145736 | tf_op jit(solution)/shard_map/ppermute | solution.py:65
  19.9 12.0 %collective-permute-start.5 = (bf16[2048,256]{1,0:T(8,128)(2,1)S(1)}, bf16[2048,256]{1,0:T(8,128)(2,1)S(1)}, u32[]{:S(2)}, u32[]{:S(2)}) collective-permute-start(bf16[2048,256]{1,0:T(8,128)(2,1)S(1)} %terms.11), channel_id=1, source_target_pairs={{0,4},{4,0},{1,5},{5,1},{2,6},{6,2},{3,7},{7,3},{8,12},{12,8},{9,1... | collective-permute-start | bytes 3145736 | tf_op jit(solution)/shard_map/ppermute | solution.py:65
  24.0 9.9 %collective-permute-start.6 = (bf16[1024,256]{1,0:T(8,128)(2,1)S(1)}, bf16[1024,256]{1,0:T(8,128)(2,1)S(1)}, u32[]{:S(2)}, u32[]{:S(2)}) collective-permute-start(bf16[1024,256]{1,0:T(8,128)(2,1)S(1)} %get-tuple-element.55), channel_id=1, source_target_pairs={{0,32},{4,12},{8,40},{12,20},{16,48},{20,28},{24,56},{28,4},{32,64... | collective-permute-start | bytes 1572872 | tf_op jit(solution)/shard_map/ppermute | solution.py:39
  24.1 9.8 %collective-permute-start.9 = (bf16[1024,256]{1,0:T(8,128)(2,1)S(1)}, bf16[1024,256]{1,0:T(8,128)(2,1)S(1)}, u32[]{:S(2)}, u32[]{:S(2)}) collective-permute-start(bf16[1024,256]{1,0:T(8,128)(2,1)S(1)} %get-tuple-element.56), channel_id=1, source_target_pairs={{0,96},{4,28},{8,104},{12,4},{16,112},{20,12},{24,120},{28,20},{32... | collective-permute-start | bytes 1572872 | tf_op jit(solution)/shard_map/ppermute | solution.py:39
  34.2 9.2 %collective-permute-start.12 = (bf16[512,256]{1,0:T(8,128)(2,1)S(1)}, bf16[512,256]{1,0:T(8,128)(2,1)S(1)}, u32[]{:S(2)}, u32[]{:S(2)}) collective-permute-start(bf16[512,256]{1,0:T(8,128)(2,1)S(1)} %get-tuple-element.77), channel_id=1, source_target_pairs={{0,24},{4,100},{8,0},{12,108},{16,8},{20,116},{24,16},{28,124},{32... | collective-permute-start | bytes 786440 | tf_op jit(solution)/shard_map/ppermute | solution.py:43
  36.8 6.8 %collective-permute-start.11 = (bf16[512,256]{1,0:T(8,128)(2,1)S(1)}, bf16[512,256]{1,0:T(8,128)(2,1)S(1)}, u32[]{:S(2)}, u32[]{:S(2)}) collective-permute-start(bf16[512,256]{1,0:T(8,128)(2,1)S(1)} %get-tuple-element.78), channel_id=1, source_target_pairs={{0,16},{4,68},{8,24},{12,76},{16,0},{20,84},{24,8},{28,92},{32,48}... | collective-permute-start | bytes 786440 | tf_op jit(solution)/shard_map/ppermute | solution.py:43
  37.0 9.6 %collective-permute-start.10 = (bf16[512,256]{1,0:T(8,128)(2,1)S(1)}, bf16[512,256]{1,0:T(8,128)(2,1)S(1)}, u32[]{:S(2)}, u32[]{:S(2)}) collective-permute-start(bf16[512,256]{1,0:T(8,128)(2,1)S(1)} %get-tuple-element.79), channel_id=1, source_target_pairs={{0,8},{4,36},{8,16},{12,44},{16,24},{20,52},{24,0},{28,60},{32,40}... | collective-permute-start | bytes 786440 | tf_op jit(solution)/shard_map/ppermute | solution.py:43
  49.7 9.6 %collective-permute-start.17 = (bf16[256,512]{1,0:T(8,128)(2,1)S(1)}, bf16[256,512]{1,0:T(8,128)(2,1)S(1)}, u32[]{:S(2)}, u32[]{:S(2)}) collective-permute-start(bf16[256,512]{1,0:T(8,128)(2,1)S(1)} %get-tuple-element.63.refs_0_), channel_id=1, source_target_pairs={{0,8},{4,36},{8,16},{12,44},{16,24},{20,52},{24,0},{28,60},{32,40}... | collective-permute-start | bytes 786440 | tf_op jit(solution)/shard_map/ppermute | solution.py:43
  49.8 9.5 %collective-permute-start.16 = (bf16[256,512]{1,0:T(8,128)(2,1)S(1)}, bf16[256,512]{1,0:T(8,128)(2,1)S(1)}, u32[]{:S(2)}, u32[]{:S(2)}) collective-permute-start(bf16[256,512]{1,0:T(8,128)(2,1)S(1)} %get-tuple-element.63.refs_0_), channel_id=1, source_target_pairs={{0,16},{4,68},{8,24},{12,76},{16,0},{20,84},{24,8},{28,92},{32,48}... | collective-permute-start | bytes 786440 | tf_op jit(solution)/shard_map/ppermute | solution.py:43
  51.3 8.7 %collective-permute-start.15 = (bf16[256,512]{1,0:T(8,128)(2,1)S(1)}, bf16[256,512]{1,0:T(8,128)(2,1)S(1)}, u32[]{:S(2)}, u32[]{:S(2)}) collective-permute-start(bf16[256,512]{1,0:T(8,128)(2,1)S(1)} %get-tuple-element.63.refs_0_), channel_id=1, source_target_pairs={{0,24},{4,100},{8,0},{12,108},{16,8},{20,116},{24,16},{28,124},{32... | collective-permute-start | bytes 786440 | tf_op jit(solution)/shard_map/ppermute | solution.py:43
  52.4 2.5 %collective-permute-start.13 = (f32[16,128]{1,0:T(8,128)S(1)}, f32[16,128]{1,0:T(8,128)S(1)}, u32[]{:S(2)}, u32[]{:S(2)}) collective-permute-start(f32[16,128]{1,0:T(8,128)S(1)} %get-tuple-element.61), channel_id=1, source_target_pairs={{0,32},{4,12},{8,40},{12,4},{16,48},{20,28},{24,56},{28,20},{32,0}... | collective-permute-start | bytes 24584 | tf_op jit(solution)/shard_map/ppermute | solution.py:57
  54.9 4.2 %collective-permute-start.14 = (f32[16,128]{1,0:T(8,128)S(1)}, f32[16,128]{1,0:T(8,128)S(1)}, u32[]{:S(2)}, u32[]{:S(2)}) collective-permute-start(f32[16,128]{1,0:T(8,128)S(1)} %add.77), channel_id=1, source_target_pairs={{0,96},{4,28},{8,104},{12,20},{16,112},{20,12},{24,120},{28,4},{32... | collective-permute-start | bytes 24584 | tf_op jit(solution)/shard_map/ppermute | solution.py:57
  60.1 20.0 %collective-permute-start.23 = (bf16[1024,512]{1,0:T(8,128)(2,1)S(1)}, bf16[1024,512]{1,0:T(8,128)(2,1)S(1)}, u32[]{:S(2)}, u32[]{:S(2)}) collective-permute-start(bf16[1024,512]{1,0:T(8,128)(2,1)S(1)} %joined.1.refs_3_), channel_id=1, source_target_pairs={{0,96},{4,28},{8,104},{12,4},{16,112},{20,12},{24,120},{28,20},{32... | collective-permute-start | bytes 3145736 | tf_op jit(solution)/shard_map/ppermute | solution.py:39
  64.0 16.1 %collective-permute-start.22 = (bf16[1024,512]{1,0:T(8,128)(2,1)S(1)}, bf16[1024,512]{1,0:T(8,128)(2,1)S(1)}, u32[]{:S(2)}, u32[]{:S(2)}) collective-permute-start(bf16[1024,512]{1,0:T(8,128)(2,1)S(1)} %joined.1.refs_3_), channel_id=1, source_target_pairs={{0,4},{4,0},{1,5},{5,1},{2,6},{6,2},{3,7},{7,3},{8,12},{12,8},{9,1... | collective-permute-start | bytes 3145736 | tf_op jit(solution)/shard_map/ppermute | solution.py:65
  69.8 15.2 %collective-permute-start.21 = (bf16[1024,512]{1,0:T(8,128)(2,1)S(1)}, bf16[1024,512]{1,0:T(8,128)(2,1)S(1)}, u32[]{:S(2)}, u32[]{:S(2)}) collective-permute-start(bf16[1024,512]{1,0:T(8,128)(2,1)S(1)} %joined.1.refs_3_), channel_id=1, source_target_pairs={{0,32},{4,12},{8,40},{12,20},{16,48},{20,28},{24,56},{28,4},{32,64... | collective-permute-start | bytes 3145736 | tf_op jit(solution)/shard_map/ppermute | solution.py:39
  70.2 2.9 %collective-permute-start.18 = (f32[16,128]{1,0:T(8,128)S(1)}, f32[16,128]{1,0:T(8,128)S(1)}, u32[]{:S(2)}, u32[]{:S(2)}) collective-permute-start(f32[16,128]{1,0:T(8,128)S(1)} %add.78), channel_id=1, source_target_pairs={{0,8},{4,36},{8,0},{12,44},{16,24},{20,52},{24,16},{28,60},{32,40}... | collective-permute-start | bytes 24584 | tf_op jit(solution)/shard_map/ppermute | solution.py:57
  73.1 4.2 %collective-permute-start.19 = (f32[16,128]{1,0:T(8,128)S(1)}, f32[16,128]{1,0:T(8,128)S(1)}, u32[]{:S(2)}, u32[]{:S(2)}) collective-permute-start(f32[16,128]{1,0:T(8,128)S(1)} %add.79), channel_id=1, source_target_pairs={{0,24},{4,100},{8,16},{12,108},{16,8},{20,116},{24,0},{28,124},{32... | collective-permute-start | bytes 24584 | tf_op jit(solution)/shard_map/ppermute | solution.py:57
  77.3 2.8 %collective-permute-start.20 = (f32[16,128]{1,0:T(8,128)S(1)}, f32[16,128]{1,0:T(8,128)S(1)}, u32[]{:S(2)}, u32[]{:S(2)}) collective-permute-start(f32[16,128]{1,0:T(8,128)S(1)} %add.80), channel_id=1, source_target_pairs={{0,1},{1,0},{2,3},{3,2},{4,5},{5,4},{6,7},{7,6},{8,9},{9,8},{10,11... | collective-permute-start | bytes 24584 | tf_op jit(solution)/shard_map/ppermute | solution.py:49
  80.1 12.2 %collective-permute-start.27 = (bf16[512,512]{1,0:T(8,128)(2,1)S(1)}, bf16[512,512]{1,0:T(8,128)(2,1)S(1)}, u32[]{:S(2)}, u32[]{:S(2)}) collective-permute-start(bf16[512,512]{1,0:T(8,128)(2,1)S(1)} %taken.3), channel_id=1, source_target_pairs={{0,96},{4,28},{8,104},{12,4},{16,112},{20,12},{24,120},{28,20},{32... | collective-permute-start | bytes 1572872 | tf_op jit(solution)/shard_map/ppermute | solution.py:39
  85.1 12.0 %collective-permute-start.30 = (bf16[1024,512]{1,0:T(8,128)(2,1)S(1)}, bf16[1024,512]{1,0:T(8,128)(2,1)S(1)}, u32[]{:S(2)}, u32[]{:S(2)}) collective-permute-start(bf16[1024,512]{1,0:T(8,128)(2,1)S(1)} %collective-permute-done.21.ref.refs_5_), channel_id=1, source_target_pairs={{0,4},{4,0},{1,5},{5,1},{2,6},{6,2},{3,7},{7,3},{8,12},{12,8},{9,1... | collective-permute-start | bytes 3145736 | tf_op jit(solution)/shard_map/ppermute | solution.py:65
  86.1 10.9 %collective-permute-start.31 = (bf16[1024,512]{1,0:T(8,128)(2,1)S(1)}, bf16[1024,512]{1,0:T(8,128)(2,1)S(1)}, u32[]{:S(2)}, u32[]{:S(2)}) collective-permute-start(bf16[1024,512]{1,0:T(8,128)(2,1)S(1)} %collective-permute-done.23.ref.refs_6_), channel_id=1, source_target_pairs={{0,4},{4,0},{1,5},{5,1},{2,6},{6,2},{3,7},{7,3},{8,12},{12,8},{9,1... | collective-permute-start | bytes 3145736 | tf_op jit(solution)/shard_map/ppermute | solution.py:65
  86.2 9.5 %collective-permute-start.26 = (bf16[512,512]{1,0:T(8,128)(2,1)S(1)}, bf16[512,512]{1,0:T(8,128)(2,1)S(1)}, u32[]{:S(2)}, u32[]{:S(2)}) collective-permute-start(bf16[512,512]{1,0:T(8,128)(2,1)S(1)} %taken.2), channel_id=1, source_target_pairs={{0,32},{4,12},{8,40},{12,20},{16,48},{20,28},{24,56},{28,4},{32,64... | collective-permute-start | bytes 1572872 | tf_op jit(solution)/shard_map/ppermute | solution.py:39
  86.6 3.8 %collective-permute-start.24 = (f32[16,128]{1,0:T(8,128)S(1)}, f32[16,128]{1,0:T(8,128)S(1)}, u32[]{:S(2)}, u32[]{:S(2)}) collective-permute-start(f32[16,128]{1,0:T(8,128)S(1)} %add.81), channel_id=1, source_target_pairs={{0,3},{1,2},{2,1},{3,0},{4,7},{5,6},{6,5},{7,4},{8,11},{9,10},{10,... | collective-permute-start | bytes 24584 | tf_op jit(solution)/shard_map/ppermute | solution.py:49
  90.4 2.0 %collective-permute-start.25 = (f32[16,128]{1,0:T(8,128)S(1)}, f32[16,128]{1,0:T(8,128)S(1)}, u32[]{:S(2)}, u32[]{:S(2)}) collective-permute-start(f32[16,128]{1,0:T(8,128)S(1)} %add.82), channel_id=1, source_target_pairs={{0,4},{4,0},{1,5},{5,1},{2,6},{6,2},{3,7},{7,3},{8,12},{12,8},{9,1... | collective-permute-start | bytes 24584 | tf_op jit(solution)/shard_map/ppermute | solution.py:65
  92.3 9.1 %collective-permute-start.29 = (bf16[512,512]{1,0:T(8,128)(2,1)S(1)}, bf16[512,512]{1,0:T(8,128)(2,1)S(1)}, u32[]{:S(2)}, u32[]{:S(2)}) collective-permute-start(bf16[512,512]{1,0:T(8,128)(2,1)S(1)} %collective-permute-done.27.refs_4_), channel_id=1, source_target_pairs={{0,4},{4,0},{1,5},{5,1},{2,6},{6,2},{3,7},{7,3},{8,12},{12,8},{9,1... | collective-permute-start | bytes 1572872 | tf_op jit(solution)/shard_map/ppermute | solution.py:65
  95.8 5.7 %collective-permute-start.28 = (bf16[512,512]{1,0:T(8,128)(2,1)S(1)}, bf16[512,512]{1,0:T(8,128)(2,1)S(1)}, u32[]{:S(2)}, u32[]{:S(2)}) collective-permute-start(bf16[512,512]{1,0:T(8,128)(2,1)S(1)} %collective-permute-done.26.refs_3_), channel_id=1, source_target_pairs={{0,4},{4,0},{1,5},{5,1},{2,6},{6,2},{3,7},{7,3},{8,12},{12,8},{9,1... | collective-permute-start | bytes 1572872 | tf_op jit(solution)/shard_map/ppermute | solution.py:65
  (6 other events, 151.9 us)

commit v3 on v2

--- a/solution.py
+++ b/solution.py
@@ -17,48 +17,27 @@
 LONG = pl.CostEstimate(flops=2**34, bytes_accessed=2**26, transcendentals=0)
 
 
-def shift_first(k):
+def exchanges(axis, k):
     pairs = []
     for x in range(4):
         for z in range(4):
-            pairs.append(((x * 4 + z) * 2, (((x + k) % 4) * 4 + z) * 2))
-            pairs.append(((x * 4 + z) * 2 + 1, (x * 4 + (z + k) % 4) * 2 + 1))
+            for c in range(2):
+                along_x = (axis == "first") == (c == 0)
+                to_x, to_z = (x ^ k, z) if along_x else (x, z ^ k)
+                pairs.append(((x * 4 + z) * 2 + c, (to_x * 4 + to_z) * 2 + c))
     return pairs
 
 
-def shift_second(k):
-    pairs = []
-    for x in range(4):
-        for z in range(4):
-            pairs.append(((x * 4 + z) * 2, (x * 4 + (z + k) % 4) * 2))
-            pairs.append(((x * 4 + z) * 2 + 1, (((x + k) % 4) * 4 + z) * 2 + 1))
-    return pairs
-
-
 def along_first(value, k):
-    return lax.ppermute(value, DP, shift_first(k))
+    return lax.ppermute(value, DP, exchanges("first", k))
 
 
 def along_second(value, k):
-    return lax.ppermute(value, DP, shift_second(k))
-
-
-def paired(value, axes, turn):
-    pairs = ((1, 0, 3, 2), (3, 2, 1, 0))[turn]
-    if axes == "y":
-        return value + lax.ppermute(value, "y", list(enumerate(pairs)))
-    moves = []
-    for x in range(4):
-        for z in range(4):
-            for c in range(2):
-                along_x = (axes == "first") == (c == 0)
-                nx, nz = (pairs[x], z) if along_x else (x, pairs[z])
-                moves.append(((x * 4 + z) * 2 + c, (nx * 4 + nz) * 2 + c))
-    return value + lax.ppermute(value, DP, moves)
-
-
-def summed(value, axes):
-    return paired(paired(value, axes, 0), axes, 1)
+    return lax.ppermute(value, DP, exchanges("second", k))
+
+
+def along_y(value, k):
+    return lax.ppermute(value, "y", [(y, y ^ k) for y in range(4)])
 
 
 def sibling(value):
@@ -169,19 +148,14 @@
 WIDE = 2048
 
 
-def back_body(lo, count, tokens, up_ref, pre_ref, weight_ref, *refs):
-    def step(weight, out):
-        back = lax.dot_general(
-            up_ref[...], weight[...], (((1,), (1,)), ((), ())), preferred_element_type=jnp.float32
-        )
-        start = pl.multiple_of((pl.program_id(0) + lo) * WIDE, WIDE)
-        out[...] = jnp.where(
-            pre_ref[:, pl.ds(start, WIDE)] > 0,
-            back.astype(jnp.bfloat16),
-            jnp.zeros((), jnp.bfloat16),
-        )
-
-    step(weight_ref, refs[-1])
+def back_body(lo, up_ref, pre_ref, weight_ref, *refs):
+    here = pl.ds(pl.multiple_of((pl.program_id(0) + lo) * WIDE, WIDE), WIDE)
+    back = lax.dot_general(
+        up_ref[...], weight_ref[here, :], (((1,), (1,)), ((), ())), preferred_element_type=jnp.float32
+    )
+    refs[-1][...] = jnp.where(
+        pre_ref[:, here] > 0, back.astype(jnp.bfloat16), jnp.zeros((), jnp.bfloat16)
+    )
 
 
 def back_columns(lo, count, upstream, preactivation, weight, before):
@@ -189,33 +163,32 @@
     tokens = preactivation.shape[0]
 
     def body(*refs):
-        back_body(lo, count, tokens, *refs)
+        back_body(lo, *refs)
 
     return pl.pallas_call(
         body,
         out_shape=jax.ShapeDtypeStruct(preactivation.shape, jnp.bfloat16),
         grid=(count,),
-        in_specs=[VMEM, VMEM, pl.BlockSpec((WIDE, D), lambda i: (i + lo, 0))]
+        in_specs=[VMEM, VMEM, VMEM]
         + [pl.BlockSpec(memory_space=pl.ANY)] * len(extra),
         out_specs=pl.BlockSpec((tokens, WIDE), lambda i: (0, i + lo)),
         input_output_aliases={3: 0} if extra else {},
         compiler_params=pltpu.CompilerParams(vmem_limit_bytes=24 * 2**20),
         cost_estimate=LONG,
         name="back_columns",
-    )(upstream, in_vmem(preactivation), in_hbm(weight), *map(in_hbm, extra))
+    )(upstream, in_vmem(preactivation), in_vmem(weight), *map(in_hbm, extra))
 
 
 def update_body(
     block, g0, g1, g2, g3, g4, g5, first, second, weight,
-    first_out, second_out, update_out, short_out, sums_out, own, arrived,
+    first_out, second_out, update_out, short_out,
 ):
     beta_one = 0.9
     beta_two = 0.999
     bias_one = 1.0 - beta_one**STEP
     bias_two = 1.0 - beta_two**STEP
     start = pl.multiple_of(block[0] * ROWS, ROWS)
-    fetch = pltpu.make_async_copy(weight.at[pl.ds(start, ROWS)], own, arrived)
-    fetch.start()
+    own = pl.ds(start, ROWS)
     update_sq = jnp.zeros((8, 128), jnp.float32)
     weight_sq = jnp.zeros((8, 128), jnp.float32)
     for j in range(D // 128):
@@ -226,9 +199,7 @@
         gradient = total.T
         first_next = beta_one * first[:, part] + (1.0 - beta_one) * gradient
         second_next = beta_two * second[:, part] + (1.0 - beta_two) * gradient * gradient
-        if j == 0:
-            fetch.wait()
-        own_weight = own[:, part].astype(jnp.float32)
+        own_weight = weight[own, part].astype(jnp.float32)
         update = (
             first_next * (1.0 / bias_one) / (jnp.sqrt(second_next * (1.0 / bias_two)) + 1e-06)
             + 0.02 * own_weight
@@ -236,13 +207,18 @@
         first_out[:, part] = first_next
         second_out[:, part] = second_next
         update_out[:, part] = update
-        short_out[:, part] = update.astype(jnp.bfloat16)
+        short_out[0:ROWS, part] = update.astype(jnp.bfloat16)
         update_sq = update_sq + jnp.sum((update * update).reshape(ROWS // 8, 8, 128), axis=0)
         weight_sq = weight_sq + jnp.sum(
             (own_weight * own_weight).reshape(ROWS // 8, 8, 128), axis=0
         )
-    sums_out[0:8, :] = update_sq
-    sums_out[8:16, :] = weight_sq
+    for k, norm in enumerate((update_sq, weight_sq)):
+        lines = slice(ROWS + 8 * k, ROWS + 8 * k + 8)
+        for j in range(3):
+            piece = norm.astype(jnp.bfloat16)
+            short_out[lines, j * 128 : (j + 1) * 128] = piece
+            norm = norm - piece.astype(jnp.float32)
+        short_out[lines, 384:512] = jnp.zeros((8, 128), jnp.bfloat16)
 
 
 def update_rows(block, parts, first, second, weight):
@@ -253,18 +229,14 @@
             long,
             long,
             long,
-            jax.ShapeDtypeStruct((ROWS, D), jnp.bfloat16),
-            jax.ShapeDtypeStruct((16, 128), jnp.float32),
+            jax.ShapeDtypeStruct((ROWS + 16, D), jnp.bfloat16),
         ),
-        in_specs=[SMEM]
-        + [VMEM] * 6
-        + [VMEM, VMEM, HBM],
-        out_specs=(VMEM,) * 5,
-        scratch_shapes=[pltpu.VMEM((ROWS, D), jnp.bfloat16), pltpu.SemaphoreType.DMA],
+        in_specs=[SMEM] + [VMEM] * 9,
+        out_specs=(VMEM,) * 4,
         compiler_params=pltpu.CompilerParams(vmem_limit_bytes=16 * 2**20),
         cost_estimate=SHORT,
         name="update_rows",
-    )(block, *parts, first, second, in_hbm(weight))
+    )(block, *parts, first, second, in_vmem(weight))
 
 
 def apply_body(picks, sizes, trust, blocks, sums_ref, weight, *refs):
@@ -320,17 +292,23 @@
 
 
 def joined(*values):
-    rows = values[0].shape[0]
-
     def body(*refs):
-        for k, ref in enumerate(refs[:-1]):
-            refs[-1][k * rows : (k + 1) * rows, :] = ref[...]
-
-    return pl.pallas_call(
-        body,
-        out_shape=jax.ShapeDtypeStruct((len(values) * rows, D), values[0].dtype),
+        rows_out, sums_out = refs[-2:]
+        total = jnp.zeros((16, 128), jnp.float32)
+        for k, ref in enumerate(refs[:-2]):
+            rows_out[k * ROWS : (k + 1) * ROWS, :] = ref[0:ROWS, :]
+            for j in range(3):
+                total = total + ref[ROWS : ROWS + 16, j * 128 : (j + 1) * 128].astype(jnp.float32)
+        sums_out[...] = total
+
+    return pl.pallas_call(
+        body,
+        out_shape=(
+            jax.ShapeDtypeStruct((len(values) * ROWS, D), jnp.bfloat16),
+            jax.ShapeDtypeStruct((16, 128), jnp.float32),
+        ),
         in_specs=[VMEM] * len(values),
-        out_specs=VMEM,
+        out_specs=(VMEM, VMEM),
         compiler_params=pltpu.CompilerParams(vmem_limit_bytes=16 * 2**20),
         cost_estimate=SHORT,
         name="joined",
@@ -362,11 +340,11 @@
 
 
 def own_unit(k):
-    return [k % 4 * 4 + j for j in range(4)]
+    return [k * 4 + j for j in range(4)]
 
 
 def other_unit(k):
-    return [16 + k % 4 * 4 + j for j in range(4)]
+    return [16 + k * 4 + j for j in range(4)]
 
 
 def per_device(preactivation, upstream, weight, first_moment, second_moment):
@@ -378,12 +356,12 @@
     place = jnp.arange(32, dtype=jnp.int32)
     unit, member = (place >> 2) & 3, place & 3
     mine = place < 16
-    on_first = (first + jnp.where(mine, unit, member)) & 3
-    on_second = (second + jnp.where(mine, member, unit)) & 3
+    on_first = first ^ jnp.where(mine, unit, member)
+    on_second = second ^ jnp.where(mine, member, unit)
     blocks = on_first * first_stride + on_second * second_stride + jnp.where(mine, c, 1 - c)
 
-    near_free = lambda unit: unit(1)[2:] + unit(-1)[:2]
-    near_late = lambda unit: unit(1)[:2] + unit(-1)[2:]
+    near_free = lambda unit: unit(1)[:2] + unit(3)[2:]
+    near_late = lambda unit: unit(1)[2:] + unit(3)[:2]
 
     send_far, up_t = first_terms(preactivation, upstream, blocks, other_unit(2))
 
@@ -397,78 +375,75 @@
     keep_far = [after(v, send_free) for v in keep_far]
     far_low = added(keep_far[0], got_far[:half])
     far_high = added(keep_far[1], got_far[half:])
-    from_left = along_first(far_low, 1)
-    from_right = along_first(far_high, -1)
+    from_one = along_first(far_low, 1)
+    from_three = along_first(far_high, 3)
 
     got_free = sibling(send_free)
     (send_late,) = part(near_late(other_unit), (4,), then=(far_low, far_high), cost=LONG)
     got_late = sibling(send_late)
-    right_high, left_low = part(
+    one_low, three_high = part(
         near_free(own_unit), (2, 2), [[(got_free, 0)], [(got_free, half)]], then=(send_late,)
     )
-    sum_left_high = along_first(right_high, 1)
-    sum_right_low = along_first(left_low, -1)
-    (send_here,) = part(other_unit(0), (4,), then=(right_high, left_low), cost=LONG)
+    sum_one_low = along_first(one_low, 1)
+    sum_three_high = along_first(three_high, 3)
+    (send_here,) = part(other_unit(0), (4,), then=(one_low, three_high), cost=LONG)
     got_here = sibling(send_here)
-    right_low, left_high = part(
+    one_high, three_low = part(
         near_late(own_unit),
         (2, 2),
-        [[(got_late, 0), (from_left, 0)], [(got_late, half), (from_right, 0)]],
+        [[(got_late, 0), (from_three, 0)], [(got_late, half), (from_one, 0)]],
         then=(send_here,),
     )
-    sum_left_low = along_first(right_low, 1)
-    sum_right_high = along_first(left_high, -1)
+    sum_one_high = along_first(one_high, 1)
+    sum_three_low = along_first(three_low, 3)
     input_grad = back_columns(
-        0, 2, after(upstream, right_low, left_high), preactivation, weight, None
+        0, 2, after(upstream, one_high, three_low), preactivation, weight, None
     )
     (here,) = part(own_unit(0), (4,), [[(got_here, 0)]], then=(input_grad,))
     near = (
-        added(here[D:half], sum_left_low[D:], sum_right_low[D:]),
-        added(here[half : half + D], sum_left_high[:D], sum_right_high[:D]),
-        added(here[half + D :], sum_left_high[D:], sum_right_high[D:]),
-    )
-    got = [along_second(v, j) for v, j in zip(near, (1, 2, 3))]
+        added(here[D:half], sum_one_low[D:], sum_three_low[D:]),
+        added(here[half : half + D], sum_one_high[:D], sum_three_high[:D]),
+        added(here[half + D :], sum_one_high[D:], sum_three_high[D:]),
+    )
+    got = [along_second(v, k) for v, k in zip(near, (1, 2, 3))]
     input_grad = back_columns(2, 2, after(upstream, *near), preactivation, weight, input_grad)
-    first_next, second_next, update, short, sums = update_rows(
+    first_next, second_next, update, short = update_rows(
         blocks,
-        [here, sum_left_low, sum_right_low, *got],
+        [here, sum_one_low, sum_three_low, *got],
         first_moment,
         second_moment,
         after(weight, input_grad),
     )
 
-    rows = [along_second(short, -j) for j in (1, 2, 3)]
-    sums = summed(sums, "first")
-    mine = joined(after(short, sums), *rows)
-    mine_other = sibling(mine)
-    near_left = along_first(mine, 1)
-    near_right = along_first(mine, -1)
-    sums = paired(summed(after(sums, mine), "second"), "y", 0)
-    near_left = after(near_left, sums, mine_other)
-    near_right = after(near_right, sums, mine_other)
-    low = taken(near_left, 0)
-    high = taken(near_right, 2 * ROWS)
-    far_left = along_first(low, 1)
-    far_right = along_first(high, -1)
-    near_left, near_right = after(near_left, low, high), after(near_right, low, high)
-    sums = paired(after(sums, low, high), "y", 1)
+    mine, sums = joined(short, *(along_second(short, k) for k in (1, 2, 3)))
+    near_one = along_first(mine, 1)
+    near_three = along_first(mine, 3)
+    sums = sums + along_y(sums, 1)
+    sums = sums + along_y(sums, 3)
+    sums = sums + along_first(sums, 1) + along_first(sums, 2) + along_first(sums, 3)
+    low = taken(after(near_one, sums), 0)
+    high = taken(after(near_three, sums), 2 * ROWS)
+    far_low = along_first(low, 3)
+    far_high = along_first(high, 1)
+    sums = after(sums, low, high)
+    near_one, near_three = after(near_one, low, high), after(near_three, low, high)
+    others = [sibling(v) for v in (after(mine, low, high), near_one, near_three)]
     sums = sums + sibling(sums)
-    far_left, far_right = after(far_left, sums), after(far_right, sums)
     new_weight, trust_step = apply_update(
         blocks,
-        own_unit(0) + other_unit(0) + own_unit(-1) + own_unit(1) + other_unit(-1) + other_unit(1),
+        own_unit(0) + own_unit(1) + own_unit(3) + own_unit(2),
         sums,
         weight,
-        [mine, mine_other, near_left, near_right, sibling(near_left), sibling(near_right)],
+        [mine, near_one, near_three, far_low, far_high],
         update,
         None,
     )
     (new_weight,) = apply_update(
         blocks,
-        own_unit(2) + other_unit(2),
+        other_unit(0) + other_unit(1) + other_unit(3) + other_unit(2),
         sums,
         weight,
-        [far_left, far_right, sibling(far_left), sibling(far_right)],
+        [*others, sibling(far_low), sibling(far_high)],
         None,
         new_weight,
     )

time: 104 us -> 96.2 us (0.925)
  Pallas kernels: 33.4 us -> 29.1 us
  starting transfers between devices: 41.6 us -> 37.6 us
    pallas_call x2, Pallas kernels: 10.7 us -> 7.31 us  [back_columns(): pl.pallas_call(body, out_shape=jax.ShapeDtypeStruct(preactivation.shape,...]
    ppermute x10, starting transfers between devices: 11.9 us -> 8.88 us  [sibling(): return lax.ppermute(value, 'c', [(0, 1), (1, 0)])]
    ppermute x22 -> x21, waiting for transfers between devices: 26.2 us -> 27.7 us  [the longest x13 14.8 us: along_first(): return lax.ppermute(value, DP, exchanges('first', k))]
    ppermute x22 -> x21, starting transfers between devices: 29.6 us -> 28.7 us  [the longest x13 18.1 us: along_first(): return lax.ppermute(value, DP, exchanges('first', k))]
  transfers between devices with their start and end apart: 32 -> 31, of which waited for: 15 -> 14; matrix products, arithmetic and copies ran while one was open for 0% -> 0% of each run, Pallas kernels for 23% -> 21%
where the time goes in v3:
time: 96.2 us; the launch traced here: 96.1 us
  starting transfers between devices  37.6 us (39%)
  Pallas kernels  29.1 us (30%)
  waiting for transfers between devices  27.7 us (29%)
  between operations  1.04 us (1%)
    ppermute x13, starting transfers between devices, along_first(): return lax.ppermute(value, DP, exchanges('first', k))  18.1 us
    ppermute x13, waiting for transfers between devices, along_first(): return lax.ppermute(value, DP, exchanges('first', k))  14.8 us
    ppermute x6, waiting for transfers between devices, along_second(): return lax.ppermute(value, DP, exchanges('second', k))  10.4 us
    pallas_call x7, Pallas kernels, terms(): pl.pallas_call(body, out_shape=tuple((jax.ShapeDtypeStruct((p * D, ROWS),...  8.95 us
    ppermute x10, starting transfers between devices, sibling(): return lax.ppermute(value, 'c', [(0, 1), (1, 0)])  8.88 us
    pallas_call x2, Pallas kernels, back_columns(): pl.pallas_call(body, out_shape=jax.ShapeDtypeStruct(preactivation.shape,...  7.31 us
    ppermute x6, starting transfers between devices, along_second(): return lax.ppermute(value, DP, exchanges('second', k))  6.59 us
    pallas_call x2, Pallas kernels, apply_update(): pl.pallas_call(body, out_shape=(jax.ShapeDtypeStruct(weight.shape, jnp.bf...  6.45 us
  transfers between devices with their start and end apart: 31, of which 14 were waited for; matrix products, arithmetic and copies ran while one was open for 0% of the time, Pallas kernels for 21%

profile of v3, /device:TPU:1, one launch (start us, length us, event | category | flops | bytes accessed | tf_op | source)
XLA Modules:
  0.0 96.1 jit_solution(8334003026497340165)
XLA Ops:
  0.7 4.1 %first_terms.1 = (bf16[2048,256]{1,0:T(8,128)(2,1)S(1)}, bf16[512,448]{1,0:T(8,128)(2,1)S(1)}) custom-call(s32[32]{0:T(128)S(1)} %fusion.3.refs_0_.block, bf16[448,512]{1,0:T(8,128)(2,1)} %refs_0_.1, bf16[448,8192]{1,0:T(8,128)(2,1)} %refs_1_.5), custom_call_target="tpu_custom_call" | custom-call | flops 17179869184 | bytes 67108864 | tf_op jit(solution)/shard_map/first_terms/pallas_call | solution.py:91
  4.8 1.5 %collective-permute-start = (bf16[2048,256]{1,0:T(8,128)(2,1)S(1)}, bf16[2048,256]{1,0:T(8,128)(2,1)S(1)}, u32[]{:S(2)}, u32[]{:S(2)}) collective-permute-start(bf16[2048,256]{1,0:T(8,128)(2,1)S(1)} %get-tuple-element.40), channel_id=1, source_target_pairs={{0,4},{4,0},{1,5},{5,1},{2,6},{6,2},{3,7},{7,3},{8,12},{12,8},{9,1... | collective-permute-start | bytes 3145736 | tf_op jit(solution)/shard_map/ppermute | solution.py:44
  6.3 1.3 %terms.7 = (bf16[1024,256]{1,0:T(8,128)(2,1)S(1)}, bf16[1024,256]{1,0:T(8,128)(2,1)S(1)}) custom-call(s32[32]{0:T(128)S(1)} %fusion.3.refs_0_.block, bf16[512,448]{1,0:T(8,128)(2,1)S(1)} %get-tuple-element.56.refs_1_, bf16[448,8192]{1,0:T(8,128)(2,1)S(1)} %copy-done), custom_call_target="tpu_custom_call" | custom-call | flops 17179869184 | bytes 67108864 | tf_op jit(solution)/shard_map/terms/pallas_call | solution.py:137
  7.6 1.3 %terms.8 = bf16[2048,256]{1,0:T(8,128)(2,1)S(1)} custom-call(s32[32]{0:T(128)S(1)} %fusion.3.refs_0_.block, bf16[512,448]{1,0:T(8,128)(2,1)S(1)} %get-tuple-element.56.refs_1_, bf16[448,8192]{1,0:T(8,128)(2,1)S(1)} %copy-done), custom_call_target="tpu_custom_call" | custom-call | flops 1048576 | bytes 65536 | tf_op jit(solution)/shard_map/terms/pallas_call | solution.py:137
  9.2 3.9 %collective-permute-start.3 = (bf16[1024,256]{1,0:T(8,128)(2,1)S(1)}, bf16[1024,256]{1,0:T(8,128)(2,1)S(1)}, u32[]{:S(2)}, u32[]{:S(2)}) collective-permute-start(bf16[1024,256]{1,0:T(8,128)(2,1)S(1)} %get-tuple-element.76), channel_id=1, source_target_pairs={{0,96},{4,28},{8,104},{12,20},{16,112},{20,12},{24,120},{28,4},{32... | collective-permute-start | bytes 1572872 | tf_op jit(solution)/shard_map/ppermute | solution.py:32
  13.1 1.3 %terms.9 = bf16[2048,256]{1,0:T(8,128)(2,1)S(1)} custom-call(s32[32]{0:T(128)S(1)} %fusion.3.refs_0_.block, bf16[512,448]{1,0:T(8,128)(2,1)S(1)} %get-tuple-element.56.refs_1_, bf16[448,8192]{1,0:T(8,128)(2,1)S(1)} %copy-done), custom_call_target="tpu_custom_call" | custom-call | flops 17179869184 | bytes 67108864 | tf_op jit(solution)/shard_map/terms/pallas_call | solution.py:137
  14.4 1.3 %terms.10 = (bf16[1024,256]{1,0:T(8,128)(2,1)S(1)}, bf16[1024,256]{1,0:T(8,128)(2,1)S(1)}) custom-call(s32[32]{0:T(128)S(1)} %fusion.3.refs_0_.block, bf16[512,448]{1,0:T(8,128)(2,1)S(1)} %get-tuple-element.56.refs_1_, bf16[448,8192]{1,0:T(8,128)(2,1)S(1)} %copy-done, bf16[2048,256]{1,0:T(8,128)(2,1)S(1)} %collective-permute-done.1.refs_3_.refs_4_, ...), custom_call_target="tpu_custom_call" | custom-call | flops 1048576 | bytes 65536 | tf_op jit(solution)/shard_map/terms/pallas_call | solution.py:137
  15.7 1.5 %collective-permute-start.6 = (bf16[1024,256]{1,0:T(8,128)(2,1)S(1)}, bf16[1024,256]{1,0:T(8,128)(2,1)S(1)}, u32[]{:S(2)}, u32[]{:S(2)}) collective-permute-start(bf16[1024,256]{1,0:T(8,128)(2,1)S(1)} %get-tuple-element.49), channel_id=1, source_target_pairs={{0,32},{4,12},{8,40},{12,4},{16,48},{20,28},{24,56},{28,20},{32,0}... | collective-permute-start | bytes 1572872 | tf_op jit(solution)/shard_map/ppermute | solution.py:32
  20.2 1.3 %collective-permute-done.4.refs_6_ = bf16[1024,256]{1,0:T(8,128)(2,1)S(1)} collective-permute-done((bf16[1024,256]{1,0:T(8,128)(2,1)S(1)}, bf16[1024,256]{1,0:T(8,128)(2,1)S(1)}, u32[]{:S(2)}, u32[]{:S(2)}) %collective-permute-start.4) | collective-permute-done | bytes 524320 | tf_op jit(solution)/shard_map/ppermute | solution.py:32
  21.5 1.4 %terms.12 = (bf16[1024,256]{1,0:T(8,128)(2,1)S(1)}, bf16[1024,256]{1,0:T(8,128)(2,1)S(1)}) custom-call(s32[32]{0:T(128)S(1)} %fusion.3.refs_0_.block, bf16[512,448]{1,0:T(8,128)(2,1)S(1)} %get-tuple-element.56.refs_1_, bf16[448,8192]{1,0:T(8,128)(2,1)S(1)} %copy-done, bf16[2048,256]{1,0:T(8,128)(2,1)S(1)} %collective-permute-done.2.refs_3_.refs_5_, ...), custom_call_target="tpu_custom_call" | custom-call | flops 1048576 | bytes 65536 | tf_op jit(solution)/shard_map/terms/pallas_call | solution.py:137
  23.4 2.3 %collective-permute-start.7 = (bf16[1024,256]{1,0:T(8,128)(2,1)S(1)}, bf16[1024,256]{1,0:T(8,128)(2,1)S(1)}, u32[]{:S(2)}, u32[]{:S(2)}) collective-permute-start(bf16[1024,256]{1,0:T(8,128)(2,1)S(1)} %get-tuple-element.54), channel_id=1, source_target_pairs={{0,96},{4,28},{8,104},{12,20},{16,112},{20,12},{24,120},{28,4},{32... | collective-permute-start | bytes 1572872 | tf_op jit(solution)/shard_map/ppermute | solution.py:32
  25.6 3.7 %back_columns.2.refs_3_ = bf16[448,8192]{1,0:T(8,128)(2,1)} custom-call(bf16[448,512]{1,0:T(8,128)(2,1)S(1)} %copy-done.3, bf16[448,8192]{1,0:T(8,128)(2,1)S(1)} %copy-done, bf16[8192,512]{1,0:T(8,128)(2,1)S(1)} %bitcast.1), custom_call_target="tpu_custom_call" | custom-call | flops 17179869184 | bytes 67108864 | tf_op jit(solution)/shard_map/back_columns/pallas_call | solution.py:168
  30.6 2.1 %collective-permute-done.8 = bf16[1024,256]{1,0:T(8,128)(2,1)S(1)} collective-permute-done((bf16[1024,256]{1,0:T(8,128)(2,1)S(1)}, bf16[1024,256]{1,0:T(8,128)(2,1)S(1)}, u32[]{:S(2)}, u32[]{:S(2)}) %collective-permute-start.8) | collective-permute-done | bytes 524320 | tf_op jit(solution)/shard_map/ppermute | solution.py:32
  33.2 2.3 %collective-permute-start.12 = (bf16[512,256]{1,0:T(8,128)(2,1)S(1)}, bf16[512,256]{1,0:T(8,128)(2,1)S(1)}, u32[]{:S(2)}, u32[]{:S(2)}) collective-permute-start(bf16[512,256]{1,0:T(8,128)(2,1)S(1)} %get-tuple-element.73), channel_id=1, source_target_pairs={{0,24},{4,100},{8,16},{12,108},{16,8},{20,116},{24,0},{28,124},{32... | collective-permute-start | bytes 786440 | tf_op jit(solution)/shard_map/ppermute | solution.py:36
  36.5 3.6 %back_columns.3 = bf16[448,8192]{1,0:T(8,128)(2,1)} custom-call(bf16[448,512]{1,0:T(8,128)(2,1)S(1)} %copy-done.3, bf16[448,8192]{1,0:T(8,128)(2,1)S(1)} %copy-done, bf16[8192,512]{1,0:T(8,128)(2,1)S(1)} %bitcast.1, bf16[448,8192]{1,0:T(8,128)(2,1)} %back_columns.2.refs_3_), custom_call_target="tpu_custom_call", output_to_operand_aliasing={{}: (3, {})} | custom-call | flops 17179869184 | bytes 67108864 | tf_op jit(solution)/shard_map/back_columns/pallas_call | solution.py:168
  40.2 2.3 %collective-permute-done.12.g5 = bf16[512,256]{1,0:T(8,128)(2,1)S(1)} collective-permute-done((bf16[512,256]{1,0:T(8,128)(2,1)S(1)}, bf16[512,256]{1,0:T(8,128)(2,1)S(1)}, u32[]{:S(2)}, u32[]{:S(2)}) %collective-permute-start.12) | collective-permute-done | bytes 262176 | tf_op jit(solution)/shard_map/ppermute | solution.py:36
  43.4 2.1 %update_rows.1 = (f32[256,512]{1,0:T(8,128)}, f32[256,512]{1,0:T(8,128)}, f32[256,512]{1,0:T(8,128)S(1)}, bf16[272,512]{1,0:T(8,128)(2,1)S(1)}) custom-call(s32[32]{0:T(128)S(1)} %fusion.3.refs_0_.block, bf16[2048,256]{1,0:T(8,128)(2,1)S(1)} %terms.13.g0, bf16[1024,256]{1,0:T(8,128)(2,1)S(1)} %collective-permute-done.6.g1, ...), custom_call_target="tpu_custom_call" | custom-call | flops 1048576 | bytes 65536 | tf_op jit(solution)/shard_map/update_rows/pallas_call | solution.py:226
  45.6 2.2 %collective-permute-start.15 = (bf16[272,512]{1,0:T(8,128)(2,1)S(1)}, bf16[272,512]{1,0:T(8,128)(2,1)S(1)}, u32[]{:S(2)}, u32[]{:S(2)}) collective-permute-start(bf16[272,512]{1,0:T(8,128)(2,1)S(1)} %get-tuple-element.59.refs_0_), channel_id=1, source_target_pairs={{0,24},{4,100},{8,16},{12,108},{16,8},{20,116},{24,0},{28,124},{32... | collective-permute-start | bytes 835592 | tf_op jit(solution)/shard_map/ppermute | solution.py:36
  48.8 6.6 %collective-permute-done.15.refs_3_ = bf16[272,512]{1,0:T(8,128)(2,1)S(1)} collective-permute-done((bf16[272,512]{1,0:T(8,128)(2,1)S(1)}, bf16[272,512]{1,0:T(8,128)(2,1)S(1)}, u32[]{:S(2)}, u32[]{:S(2)}) %collective-permute-start.15) | collective-permute-done | bytes 278560 | tf_op jit(solution)/shard_map/ppermute | solution.py:36
  56.0 2.5 %collective-permute-start.22 = (bf16[1024,512]{1,0:T(8,128)(2,1)S(1)}, bf16[1024,512]{1,0:T(8,128)(2,1)S(1)}, u32[]{:S(2)}, u32[]{:S(2)}) collective-permute-start(bf16[1024,512]{1,0:T(8,128)(2,1)S(1)} %get-tuple-element.65.refs_3_), channel_id=1, source_target_pairs={{0,96},{4,28},{8,104},{12,20},{16,112},{20,12},{24,120},{28,4},{32... | collective-permute-start | bytes 3145736 | tf_op jit(solution)/shard_map/ppermute | solution.py:32
  58.5 1.3 %collective-permute-start.16 = (f32[16,128]{1,0:T(8,128)S(1)}, f32[16,128]{1,0:T(8,128)S(1)}, u32[]{:S(2)}, u32[]{:S(2)}) collective-permute-start(f32[16,128]{1,0:T(8,128)S(1)} %get-tuple-element.60), channel_id=1, source_target_pairs={{0,1},{1,0},{2,3},{3,2},{4,5},{5,4},{6,7},{7,6},{8,9},{9,8},{10,11... | collective-permute-start | bytes 24584 | tf_op jit(solution)/shard_map/ppermute | solution.py:40
  61.0 2.7 %collective-permute-start.17 = (f32[16,128]{1,0:T(8,128)S(1)}, f32[16,128]{1,0:T(8,128)S(1)}, u32[]{:S(2)}, u32[]{:S(2)}) collective-permute-start(f32[16,128]{1,0:T(8,128)S(1)} %add.58), channel_id=1, source_target_pairs={{0,3},{1,2},{2,1},{3,0},{4,7},{5,6},{6,5},{7,4},{8,11},{9,10},{10,... | collective-permute-start | bytes 24584 | tf_op jit(solution)/shard_map/ppermute | solution.py:40
  63.7 1.3 %collective-permute-done.17 = f32[16,128]{1,0:T(8,128)S(1)} collective-permute-done((f32[16,128]{1,0:T(8,128)S(1)}, f32[16,128]{1,0:T(8,128)S(1)}, u32[]{:S(2)}, u32[]{:S(2)}) %collective-permute-start.17) | collective-permute-done | bytes 8224 | tf_op jit(solution)/shard_map/ppermute | solution.py:40
  65.4 2.9 %collective-permute-start.19 = (f32[16,128]{1,0:T(8,128)S(1)}, f32[16,128]{1,0:T(8,128)S(1)}, u32[]{:S(2)}, u32[]{:S(2)}) collective-permute-start(f32[16,128]{1,0:T(8,128)S(1)} %add.59), channel_id=1, source_target_pairs={{0,64},{4,20},{8,72},{12,28},{16,80},{20,4},{24,88},{28,12},{32,96... | collective-permute-start | bytes 24584 | tf_op jit(solution)/shard_map/ppermute | solution.py:32
  68.3 3.0 %collective-permute-done.20 = f32[16,128]{1,0:T(8,128)S(1)} collective-permute-done((f32[16,128]{1,0:T(8,128)S(1)}, f32[16,128]{1,0:T(8,128)S(1)}, u32[]{:S(2)}, u32[]{:S(2)}) %collective-permute-start.20) | collective-permute-done | bytes 8224 | tf_op jit(solution)/shard_map/ppermute | solution.py:32
  71.4 2.0 %collective-permute-done.19 = f32[16,128]{1,0:T(8,128)S(1)} collective-permute-done((f32[16,128]{1,0:T(8,128)S(1)}, f32[16,128]{1,0:T(8,128)S(1)}, u32[]{:S(2)}, u32[]{:S(2)}) %collective-permute-start.19) | collective-permute-done | bytes 8224 | tf_op jit(solution)/shard_map/ppermute | solution.py:32
  73.5 4.7 %collective-permute-start.23 = (f32[16,128]{1,0:T(8,128)S(1)}, f32[16,128]{1,0:T(8,128)S(1)}, u32[]{:S(2)}, u32[]{:S(2)}) collective-permute-start(f32[16,128]{1,0:T(8,128)S(1)} %add_add_fusion), channel_id=1, source_target_pairs={{0,4},{4,0},{1,5},{5,1},{2,6},{6,2},{3,7},{7,3},{8,12},{12,8},{9,1... | collective-permute-start | bytes 24584 | tf_op jit(solution)/shard_map/ppermute | solution.py:44
  79.0 3.3 %collective-permute-start.27 = (bf16[512,512]{1,0:T(8,128)(2,1)S(1)}, bf16[512,512]{1,0:T(8,128)(2,1)S(1)}, u32[]{:S(2)}, u32[]{:S(2)}) collective-permute-start(bf16[512,512]{1,0:T(8,128)(2,1)S(1)} %taken.2), channel_id=1, source_target_pairs={{0,96},{4,28},{8,104},{12,20},{16,112},{20,12},{24,120},{28,4},{32... | collective-permute-start | bytes 1572872 | tf_op jit(solution)/shard_map/ppermute | solution.py:32
  82.8 3.7 %collective-permute-done.29.refs_7_ = bf16[512,512]{1,0:T(8,128)(2,1)S(1)} collective-permute-done((bf16[512,512]{1,0:T(8,128)(2,1)S(1)}, bf16[512,512]{1,0:T(8,128)(2,1)S(1)}, u32[]{:S(2)}, u32[]{:S(2)}) %collective-permute-start.29) | collective-permute-done | bytes 524320 | tf_op jit(solution)/shard_map/ppermute | solution.py:32
  87.4 1.6 %collective-permute-done.27.refs_6_ = bf16[512,512]{1,0:T(8,128)(2,1)S(1)} collective-permute-done((bf16[512,512]{1,0:T(8,128)(2,1)S(1)}, bf16[512,512]{1,0:T(8,128)(2,1)S(1)}, u32[]{:S(2)}, u32[]{:S(2)}) %collective-permute-start.27) | collective-permute-done | bytes 524320 | tf_op jit(solution)/shard_map/ppermute | solution.py:32
  89.4 3.6 %apply_update.2 = (bf16[8192,512]{1,0:T(8,128)(2,1)}, f32[256,512]{1,0:T(8,128)}) custom-call(s32[32]{0:T(128)S(1)} %fusion.3.refs_0_.block, f32[16,128]{1,0:T(8,128)S(1)} %add.63.refs_1_, bf16[8192,512]{1,0:T(8,128)(2,1)S(1)} %bitcast.1, bf16[1024,512]{1,0:T(8,128)(2,1)S(1)} %get-tuple-element.65.refs_3_, ...), custom_call_target="tpu_custom_call" | custom-call | flops 1048576 | bytes 65536 | tf_op jit(solution)/shard_map/apply_update/pallas_call | solution.py:277
  93.1 2.8 %apply_update.3 = bf16[8192,512]{1,0:T(8,128)(2,1)} custom-call(s32[32]{0:T(128)S(1)} %fusion.3.refs_0_.block, f32[16,128]{1,0:T(8,128)S(1)} %add.63.refs_1_, bf16[8192,512]{1,0:T(8,128)(2,1)S(1)} %bitcast.1, bf16[1024,512]{1,0:T(8,128)(2,1)S(1)} %collective-permute-done.24.refs_3_, ...), custom_call_target="tpu_custom_call", output_to_operand_aliasing={{}: (8, {})} | custom-call | flops 1048576 | bytes 65536 | tf_op jit(solution)/shard_map/apply_update/pallas_call | solution.py:277
  (66 shorter events, 13.5 us)
Async XLA Ops:
  4.8 4.1 %collective-permute-start = (bf16[2048,256]{1,0:T(8,128)(2,1)S(1)}, bf16[2048,256]{1,0:T(8,128)(2,1)S(1)}, u32[]{:S(2)}, u32[]{:S(2)}) collective-permute-start(bf16[2048,256]{1,0:T(8,128)(2,1)S(1)} %get-tuple-element.40), channel_id=1, source_target_pairs={{0,4},{4,0},{1,5},{5,1},{2,6},{6,2},{3,7},{7,3},{8,12},{12,8},{9,1... | collective-permute-start | bytes 3145736 | tf_op jit(solution)/shard_map/ppermute | solution.py:44
  8.8 5.6 %collective-permute-start.1 = (bf16[2048,256]{1,0:T(8,128)(2,1)S(1)}, bf16[2048,256]{1,0:T(8,128)(2,1)S(1)}, u32[]{:S(2)}, u32[]{:S(2)}) collective-permute-start(bf16[2048,256]{1,0:T(8,128)(2,1)S(1)} %terms.8), channel_id=1, source_target_pairs={{0,4},{4,0},{1,5},{5,1},{2,6},{6,2},{3,7},{7,3},{8,12},{12,8},{9,1... | collective-permute-start | bytes 3145736 | tf_op jit(solution)/shard_map/ppermute | solution.py:44
  9.2 10.6 %collective-permute-start.3 = (bf16[1024,256]{1,0:T(8,128)(2,1)S(1)}, bf16[1024,256]{1,0:T(8,128)(2,1)S(1)}, u32[]{:S(2)}, u32[]{:S(2)}) collective-permute-start(bf16[1024,256]{1,0:T(8,128)(2,1)S(1)} %get-tuple-element.76), channel_id=1, source_target_pairs={{0,96},{4,28},{8,104},{12,20},{16,112},{20,12},{24,120},{28,4},{32... | collective-permute-start | bytes 1572872 | tf_op jit(solution)/shard_map/ppermute | solution.py:32
  13.1 8.3 %collective-permute-start.4 = (bf16[1024,256]{1,0:T(8,128)(2,1)S(1)}, bf16[1024,256]{1,0:T(8,128)(2,1)S(1)}, u32[]{:S(2)}, u32[]{:S(2)}) collective-permute-start(bf16[1024,256]{1,0:T(8,128)(2,1)S(1)} %get-tuple-element.77), channel_id=1, source_target_pairs={{0,32},{4,12},{8,40},{12,4},{16,48},{20,28},{24,56},{28,20},{32,0}... | collective-permute-start | bytes 1572872 | tf_op jit(solution)/shard_map/ppermute | solution.py:32
  15.7 14.8 %collective-permute-start.6 = (bf16[1024,256]{1,0:T(8,128)(2,1)S(1)}, bf16[1024,256]{1,0:T(8,128)(2,1)S(1)}, u32[]{:S(2)}, u32[]{:S(2)}) collective-permute-start(bf16[1024,256]{1,0:T(8,128)(2,1)S(1)} %get-tuple-element.49), channel_id=1, source_target_pairs={{0,32},{4,12},{8,40},{12,4},{16,48},{20,28},{24,56},{28,20},{32,0}... | collective-permute-start | bytes 1572872 | tf_op jit(solution)/shard_map/ppermute | solution.py:32
  17.3 8.4 %slice-start.1 = ((s8[8388608]{0:T(1024)(128)(4,1)}), s8[4194304]{0:T(1024)(128)(4,1)S(1)}, s32[]{:S(2)}) async-start(s8[8388608]{0:T(1024)(128)(4,1)} %bitcast), calls=%async_computation.1 | async-start | bytes 8388608
  17.3 13.3 %collective-permute-start.9 = (bf16[1024,256]{1,0:T(8,128)(2,1)S(1)}, bf16[1024,256]{1,0:T(8,128)(2,1)S(1)}, u32[]{:S(2)}, u32[]{:S(2)}) collective-permute-start(bf16[1024,256]{1,0:T(8,128)(2,1)S(1)} %get-tuple-element.50), channel_id=1, source_target_pairs={{0,96},{4,28},{8,104},{12,20},{16,112},{20,12},{24,120},{28,4},{32... | collective-permute-start | bytes 1572872 | tf_op jit(solution)/shard_map/ppermute | solution.py:32
  17.3 4.1 %collective-permute-start.2 = (bf16[2048,256]{1,0:T(8,128)(2,1)S(1)}, bf16[2048,256]{1,0:T(8,128)(2,1)S(1)}, u32[]{:S(2)}, u32[]{:S(2)}) collective-permute-start(bf16[2048,256]{1,0:T(8,128)(2,1)S(1)} %terms.9), channel_id=1, source_target_pairs={{0,4},{4,0},{1,5},{5,1},{2,6},{6,2},{3,7},{7,3},{8,12},{12,8},{9,1... | collective-permute-start | bytes 3145736 | tf_op jit(solution)/shard_map/ppermute | solution.py:44
  19.8 9.5 %collective-permute-start.5 = (bf16[2048,256]{1,0:T(8,128)(2,1)S(1)}, bf16[2048,256]{1,0:T(8,128)(2,1)S(1)}, u32[]{:S(2)}, u32[]{:S(2)}) collective-permute-start(bf16[2048,256]{1,0:T(8,128)(2,1)S(1)} %terms.11), channel_id=1, source_target_pairs={{0,4},{4,0},{1,5},{5,1},{2,6},{6,2},{3,7},{7,3},{8,12},{12,8},{9,1... | collective-permute-start | bytes 3145736 | tf_op jit(solution)/shard_map/ppermute | solution.py:44
  22.8 9.9 %collective-permute-start.8 = (bf16[1024,256]{1,0:T(8,128)(2,1)S(1)}, bf16[1024,256]{1,0:T(8,128)(2,1)S(1)}, u32[]{:S(2)}, u32[]{:S(2)}) collective-permute-start(bf16[1024,256]{1,0:T(8,128)(2,1)S(1)} %get-tuple-element.53), channel_id=1, source_target_pairs={{0,32},{4,12},{8,40},{12,4},{16,48},{20,28},{24,56},{28,20},{32,0}... | collective-permute-start | bytes 1572872 | tf_op jit(solution)/shard_map/ppermute | solution.py:32
  23.4 9.5 %collective-permute-start.7 = (bf16[1024,256]{1,0:T(8,128)(2,1)S(1)}, bf16[1024,256]{1,0:T(8,128)(2,1)S(1)}, u32[]{:S(2)}, u32[]{:S(2)}) collective-permute-start(bf16[1024,256]{1,0:T(8,128)(2,1)S(1)} %get-tuple-element.54), channel_id=1, source_target_pairs={{0,96},{4,28},{8,104},{12,20},{16,112},{20,12},{24,120},{28,4},{32... | collective-permute-start | bytes 1572872 | tf_op jit(solution)/shard_map/ppermute | solution.py:32
  33.2 9.3 %collective-permute-start.12 = (bf16[512,256]{1,0:T(8,128)(2,1)S(1)}, bf16[512,256]{1,0:T(8,128)(2,1)S(1)}, u32[]{:S(2)}, u32[]{:S(2)}) collective-permute-start(bf16[512,256]{1,0:T(8,128)(2,1)S(1)} %get-tuple-element.73), channel_id=1, source_target_pairs={{0,24},{4,100},{8,16},{12,108},{16,8},{20,116},{24,0},{28,124},{32... | collective-permute-start | bytes 786440 | tf_op jit(solution)/shard_map/ppermute | solution.py:36
  35.4 7.1 %collective-permute-start.11 = (bf16[512,256]{1,0:T(8,128)(2,1)S(1)}, bf16[512,256]{1,0:T(8,128)(2,1)S(1)}, u32[]{:S(2)}, u32[]{:S(2)}) collective-permute-start(bf16[512,256]{1,0:T(8,128)(2,1)S(1)} %get-tuple-element.74), channel_id=1, source_target_pairs={{0,16},{4,68},{8,24},{12,76},{16,0},{20,84},{24,8},{28,92},{32,48}... | collective-permute-start | bytes 786440 | tf_op jit(solution)/shard_map/ppermute | solution.py:36
  36.0 7.4 %collective-permute-start.10 = (bf16[512,256]{1,0:T(8,128)(2,1)S(1)}, bf16[512,256]{1,0:T(8,128)(2,1)S(1)}, u32[]{:S(2)}, u32[]{:S(2)}) collective-permute-start(bf16[512,256]{1,0:T(8,128)(2,1)S(1)} %get-tuple-element.75), channel_id=1, source_target_pairs={{0,8},{4,36},{8,0},{12,44},{16,24},{20,52},{24,16},{28,60},{32,40}... | collective-permute-start | bytes 786440 | tf_op jit(solution)/shard_map/ppermute | solution.py:36
  45.6 9.9 %collective-permute-start.15 = (bf16[272,512]{1,0:T(8,128)(2,1)S(1)}, bf16[272,512]{1,0:T(8,128)(2,1)S(1)}, u32[]{:S(2)}, u32[]{:S(2)}) collective-permute-start(bf16[272,512]{1,0:T(8,128)(2,1)S(1)} %get-tuple-element.59.refs_0_), channel_id=1, source_target_pairs={{0,24},{4,100},{8,16},{12,108},{16,8},{20,116},{24,0},{28,124},{32... | collective-permute-start | bytes 835592 | tf_op jit(solution)/shard_map/ppermute | solution.py:36
  47.8 7.7 %collective-permute-start.14 = (bf16[272,512]{1,0:T(8,128)(2,1)S(1)}, bf16[272,512]{1,0:T(8,128)(2,1)S(1)}, u32[]{:S(2)}, u32[]{:S(2)}) collective-permute-start(bf16[272,512]{1,0:T(8,128)(2,1)S(1)} %get-tuple-element.59.refs_0_), channel_id=1, source_target_pairs={{0,16},{4,68},{8,24},{12,76},{16,0},{20,84},{24,8},{28,92},{32,48}... | collective-permute-start | bytes 835592 | tf_op jit(solution)/shard_map/ppermute | solution.py:36
  48.3 7.7 %collective-permute-start.13 = (bf16[272,512]{1,0:T(8,128)(2,1)S(1)}, bf16[272,512]{1,0:T(8,128)(2,1)S(1)}, u32[]{:S(2)}, u32[]{:S(2)}) collective-permute-start(bf16[272,512]{1,0:T(8,128)(2,1)S(1)} %get-tuple-element.59.refs_0_), channel_id=1, source_target_pairs={{0,8},{4,36},{8,0},{12,44},{16,24},{20,52},{24,16},{28,60},{32,40}... | collective-permute-start | bytes 835592 | tf_op jit(solution)/shard_map/ppermute | solution.py:36
  56.0 17.3 %collective-permute-start.22 = (bf16[1024,512]{1,0:T(8,128)(2,1)S(1)}, bf16[1024,512]{1,0:T(8,128)(2,1)S(1)}, u32[]{:S(2)}, u32[]{:S(2)}) collective-permute-start(bf16[1024,512]{1,0:T(8,128)(2,1)S(1)} %get-tuple-element.65.refs_3_), channel_id=1, source_target_pairs={{0,96},{4,28},{8,104},{12,20},{16,112},{20,12},{24,120},{28,4},{32... | collective-permute-start | bytes 3145736 | tf_op jit(solution)/shard_map/ppermute | solution.py:32
  58.5 14.9 %collective-permute-start.21 = (bf16[1024,512]{1,0:T(8,128)(2,1)S(1)}, bf16[1024,512]{1,0:T(8,128)(2,1)S(1)}, u32[]{:S(2)}, u32[]{:S(2)}) collective-permute-start(bf16[1024,512]{1,0:T(8,128)(2,1)S(1)} %get-tuple-element.65.refs_3_), channel_id=1, source_target_pairs={{0,32},{4,12},{8,40},{12,4},{16,48},{20,28},{24,56},{28,20},{32,0}... | collective-permute-start | bytes 3145736 | tf_op jit(solution)/shard_map/ppermute | solution.py:32
  58.5 2.5 %collective-permute-start.16 = (f32[16,128]{1,0:T(8,128)S(1)}, f32[16,128]{1,0:T(8,128)S(1)}, u32[]{:S(2)}, u32[]{:S(2)}) collective-permute-start(f32[16,128]{1,0:T(8,128)S(1)} %get-tuple-element.60), channel_id=1, source_target_pairs={{0,1},{1,0},{2,3},{3,2},{4,5},{5,4},{6,7},{7,6},{8,9},{9,8},{10,11... | collective-permute-start | bytes 24584 | tf_op jit(solution)/shard_map/ppermute | solution.py:40
  61.0 4.1 %collective-permute-start.17 = (f32[16,128]{1,0:T(8,128)S(1)}, f32[16,128]{1,0:T(8,128)S(1)}, u32[]{:S(2)}, u32[]{:S(2)}) collective-permute-start(f32[16,128]{1,0:T(8,128)S(1)} %add.58), channel_id=1, source_target_pairs={{0,3},{1,2},{2,1},{3,0},{4,7},{5,6},{6,5},{7,4},{8,11},{9,10},{10,... | collective-permute-start | bytes 24584 | tf_op jit(solution)/shard_map/ppermute | solution.py:40
  65.1 6.3 %collective-permute-start.20 = (f32[16,128]{1,0:T(8,128)S(1)}, f32[16,128]{1,0:T(8,128)S(1)}, u32[]{:S(2)}, u32[]{:S(2)}) collective-permute-start(f32[16,128]{1,0:T(8,128)S(1)} %add.59), channel_id=1, source_target_pairs={{0,96},{4,28},{8,104},{12,20},{16,112},{20,12},{24,120},{28,4},{32... | collective-permute-start | bytes 24584 | tf_op jit(solution)/shard_map/ppermute | solution.py:32
  65.4 8.0 %collective-permute-start.19 = (f32[16,128]{1,0:T(8,128)S(1)}, f32[16,128]{1,0:T(8,128)S(1)}, u32[]{:S(2)}, u32[]{:S(2)}) collective-permute-start(f32[16,128]{1,0:T(8,128)S(1)} %add.59), channel_id=1, source_target_pairs={{0,64},{4,20},{8,72},{12,28},{16,80},{20,4},{24,88},{28,12},{32,96... | collective-permute-start | bytes 24584 | tf_op jit(solution)/shard_map/ppermute | solution.py:32
  68.3 5.0 %collective-permute-start.18 = (f32[16,128]{1,0:T(8,128)S(1)}, f32[16,128]{1,0:T(8,128)S(1)}, u32[]{:S(2)}, u32[]{:S(2)}) collective-permute-start(f32[16,128]{1,0:T(8,128)S(1)} %add.59), channel_id=1, source_target_pairs={{0,32},{4,12},{8,40},{12,4},{16,48},{20,28},{24,56},{28,20},{32,0}... | collective-permute-start | bytes 24584 | tf_op jit(solution)/shard_map/ppermute | solution.py:32
  73.5 9.3 %collective-permute-start.23 = (f32[16,128]{1,0:T(8,128)S(1)}, f32[16,128]{1,0:T(8,128)S(1)}, u32[]{:S(2)}, u32[]{:S(2)}) collective-permute-start(f32[16,128]{1,0:T(8,128)S(1)} %add_add_fusion), channel_id=1, source_target_pairs={{0,4},{4,0},{1,5},{5,1},{2,6},{6,2},{3,7},{7,3},{8,12},{12,8},{9,1... | collective-permute-start | bytes 24584 | tf_op jit(solution)/shard_map/ppermute | solution.py:44
  78.2 8.3 %collective-permute-start.29 = (bf16[512,512]{1,0:T(8,128)(2,1)S(1)}, bf16[512,512]{1,0:T(8,128)(2,1)S(1)}, u32[]{:S(2)}, u32[]{:S(2)}) collective-permute-start(bf16[512,512]{1,0:T(8,128)(2,1)S(1)} %taken.3), channel_id=1, source_target_pairs={{0,32},{4,12},{8,40},{12,4},{16,48},{20,28},{24,56},{28,20},{32,0}... | collective-permute-start | bytes 1572872 | tf_op jit(solution)/shard_map/ppermute | solution.py:32
  79.0 10.1 %collective-permute-start.27 = (bf16[512,512]{1,0:T(8,128)(2,1)S(1)}, bf16[512,512]{1,0:T(8,128)(2,1)S(1)}, u32[]{:S(2)}, u32[]{:S(2)}) collective-permute-start(bf16[512,512]{1,0:T(8,128)(2,1)S(1)} %taken.2), channel_id=1, source_target_pairs={{0,96},{4,28},{8,104},{12,20},{16,112},{20,12},{24,120},{28,4},{32... | collective-permute-start | bytes 1572872 | tf_op jit(solution)/shard_map/ppermute | solution.py:32
  82.2 10.8 %collective-permute-start.24 = (bf16[1024,512]{1,0:T(8,128)(2,1)S(1)}, bf16[1024,512]{1,0:T(8,128)(2,1)S(1)}, u32[]{:S(2)}, u32[]{:S(2)}) collective-permute-start(bf16[1024,512]{1,0:T(8,128)(2,1)S(1)} %get-tuple-element.65.refs_3_), channel_id=1, source_target_pairs={{0,4},{4,0},{1,5},{5,1},{2,6},{6,2},{3,7},{7,3},{8,12},{12,8},{9,1... | collective-permute-start | bytes 3145736 | tf_op jit(solution)/shard_map/ppermute | solution.py:44
  82.2 10.8 %collective-permute-start.25 = (bf16[1024,512]{1,0:T(8,128)(2,1)S(1)}, bf16[1024,512]{1,0:T(8,128)(2,1)S(1)}, u32[]{:S(2)}, u32[]{:S(2)}) collective-permute-start(bf16[1024,512]{1,0:T(8,128)(2,1)S(1)} %collective-permute-done.21.ref.refs_4_), channel_id=1, source_target_pairs={{0,4},{4,0},{1,5},{5,1},{2,6},{6,2},{3,7},{7,3},{8,12},{12,8},{9,1... | collective-permute-start | bytes 3145736 | tf_op jit(solution)/shard_map/ppermute | solution.py:44
  82.8 10.3 %collective-permute-start.26 = (bf16[1024,512]{1,0:T(8,128)(2,1)S(1)}, bf16[1024,512]{1,0:T(8,128)(2,1)S(1)}, u32[]{:S(2)}, u32[]{:S(2)}) collective-permute-start(bf16[1024,512]{1,0:T(8,128)(2,1)S(1)} %collective-permute-done.22.ref.refs_5_), channel_id=1, source_target_pairs={{0,4},{4,0},{1,5},{5,1},{2,6},{6,2},{3,7},{7,3},{8,12},{12,8},{9,1... | collective-permute-start | bytes 3145736 | tf_op jit(solution)/shard_map/ppermute | solution.py:44
  86.5 6.6 %collective-permute-start.30 = (bf16[512,512]{1,0:T(8,128)(2,1)S(1)}, bf16[512,512]{1,0:T(8,128)(2,1)S(1)}, u32[]{:S(2)}, u32[]{:S(2)}) collective-permute-start(bf16[512,512]{1,0:T(8,128)(2,1)S(1)} %collective-permute-done.29.refs_7_), channel_id=1, source_target_pairs={{0,4},{4,0},{1,5},{5,1},{2,6},{6,2},{3,7},{7,3},{8,12},{12,8},{9,1... | collective-permute-start | bytes 1572872 | tf_op jit(solution)/shard_map/ppermute | solution.py:44
  89.0 4.0 %collective-permute-start.28 = (bf16[512,512]{1,0:T(8,128)(2,1)S(1)}, bf16[512,512]{1,0:T(8,128)(2,1)S(1)}, u32[]{:S(2)}, u32[]{:S(2)}) collective-permute-start(bf16[512,512]{1,0:T(8,128)(2,1)S(1)} %collective-permute-done.27.refs_6_), channel_id=1, source_target_pairs={{0,4},{4,0},{1,5},{5,1},{2,6},{6,2},{3,7},{7,3},{8,12},{12,8},{9,1... | collective-permute-start | bytes 1572872 | tf_op jit(solution)/shard_map/ppermute | solution.py:44
  (5 other events, 35.5 us)

commit v4 on v3

--- a/solution.py
+++ b/solution.py
@@ -428,22 +428,23 @@
     sums = after(sums, low, high)
     near_one, near_three = after(near_one, low, high), after(near_three, low, high)
     others = [sibling(v) for v in (after(mine, low, high), near_one, near_three)]
-    sums = sums + sibling(sums)
+    sums = sums + sibling(after(sums, others[0]))
     new_weight, trust_step = apply_update(
         blocks,
-        own_unit(0) + own_unit(1) + own_unit(3) + own_unit(2),
+        own_unit(0) + own_unit(1) + own_unit(3) + other_unit(0) + other_unit(1) + other_unit(3),
         sums,
         weight,
-        [mine, near_one, near_three, far_low, far_high],
+        [mine, near_one, near_three, *others],
         update,
         None,
     )
+    far_low, far_high = after(far_low, new_weight), after(far_high, new_weight)
     (new_weight,) = apply_update(
         blocks,
-        other_unit(0) + other_unit(1) + other_unit(3) + other_unit(2),
+        own_unit(2) + other_unit(2),
         sums,
         weight,
-        [*others, sibling(far_low), sibling(far_high)],
+        [far_low, far_high, sibling(far_low), sibling(far_high)],
         None,
         new_weight,
     )

time: 96.2 us -> 94.5 us (0.982)
    ppermute x13, waiting for transfers between devices: 14.8 us -> 10.8 us  [along_first(): return lax.ppermute(value, DP, exchanges('first', k))]
    ppermute x10, waiting for transfers between devices: 0.03 us -> 3.36 us  [sibling(): return lax.ppermute(value, 'c', [(0, 1), (1, 0)])]
  transfers between devices with their start and end apart: 31 -> 31, of which waited for: 14 -> 16; matrix products, arithmetic and copies ran while one was open for 0% -> 0% of each run, Pallas kernels for 21% -> 22%
where the time goes in v4:
time: 94.5 us; the launch traced here: 94.4 us
  starting transfers between devices  36.7 us (39%)
  Pallas kernels  28.9 us (31%)
  waiting for transfers between devices  27.2 us (29%)
  between operations  1.02 us (1%)
    ppermute x13, starting transfers between devices, along_first(): return lax.ppermute(value, DP, exchanges('first', k))  18.1 us
    ppermute x13, waiting for transfers between devices, along_first(): return lax.ppermute(value, DP, exchanges('first', k))  10.8 us
    ppermute x6, waiting for transfers between devices, along_second(): return lax.ppermute(value, DP, exchanges('second', k))  10.5 us
    pallas_call x7, Pallas kernels, terms(): pl.pallas_call(body, out_shape=tuple((jax.ShapeDtypeStruct((p * D, ROWS),...  8.95 us
    ppermute x10, starting transfers between devices, sibling(): return lax.ppermute(value, 'c', [(0, 1), (1, 0)])  8.04 us
    pallas_call x2, Pallas kernels, back_columns(): pl.pallas_call(body, out_shape=jax.ShapeDtypeStruct(preactivation.shape,...  7.12 us
    ppermute x6, starting transfers between devices, along_second(): return lax.ppermute(value, DP, exchanges('second', k))  6.59 us
    pallas_call x2, Pallas kernels, apply_update(): pl.pallas_call(body, out_shape=(jax.ShapeDtypeStruct(weight.shape, jnp.bf...  6.4 us
  transfers between devices with their start and end apart: 31, of which 16 were waited for; matrix products, arithmetic and copies ran while one was open for 0% of the time, Pallas kernels for 22%

profile of v4, /device:TPU:1, one launch (start us, length us, event | category | flops | bytes accessed | tf_op | source)
XLA Modules:
  0.0 94.4 jit_solution(13806915361492177004)
XLA Ops:
  0.7 4.1 %first_terms.1 = (bf16[2048,256]{1,0:T(8,128)(2,1)S(1)}, bf16[512,448]{1,0:T(8,128)(2,1)S(1)}) custom-call(s32[32]{0:T(128)S(1)} %fusion.3.refs_0_.block, bf16[448,512]{1,0:T(8,128)(2,1)} %refs_0_.1, bf16[448,8192]{1,0:T(8,128)(2,1)} %refs_1_.5), custom_call_target="tpu_custom_call" | custom-call | flops 17179869184 | bytes 67108864 | tf_op jit(solution)/shard_map/first_terms/pallas_call | solution.py:91
  4.8 1.5 %collective-permute-start = (bf16[2048,256]{1,0:T(8,128)(2,1)S(1)}, bf16[2048,256]{1,0:T(8,128)(2,1)S(1)}, u32[]{:S(2)}, u32[]{:S(2)}) collective-permute-start(bf16[2048,256]{1,0:T(8,128)(2,1)S(1)} %get-tuple-element.43), channel_id=1, source_target_pairs={{0,4},{4,0},{1,5},{5,1},{2,6},{6,2},{3,7},{7,3},{8,12},{12,8},{9,1... | collective-permute-start | bytes 3145736 | tf_op jit(solution)/shard_map/ppermute | solution.py:44
  6.3 1.3 %terms.7 = (bf16[1024,256]{1,0:T(8,128)(2,1)S(1)}, bf16[1024,256]{1,0:T(8,128)(2,1)S(1)}) custom-call(s32[32]{0:T(128)S(1)} %fusion.3.refs_0_.block, bf16[512,448]{1,0:T(8,128)(2,1)S(1)} %get-tuple-element.59.refs_1_, bf16[448,8192]{1,0:T(8,128)(2,1)S(1)} %copy-done), custom_call_target="tpu_custom_call" | custom-call | flops 17179869184 | bytes 67108864 | tf_op jit(solution)/shard_map/terms/pallas_call | solution.py:137
  7.6 1.3 %terms.8 = bf16[2048,256]{1,0:T(8,128)(2,1)S(1)} custom-call(s32[32]{0:T(128)S(1)} %fusion.3.refs_0_.block, bf16[512,448]{1,0:T(8,128)(2,1)S(1)} %get-tuple-element.59.refs_1_, bf16[448,8192]{1,0:T(8,128)(2,1)S(1)} %copy-done), custom_call_target="tpu_custom_call" | custom-call | flops 1048576 | bytes 65536 | tf_op jit(solution)/shard_map/terms/pallas_call | solution.py:137
  9.2 3.9 %collective-permute-start.3 = (bf16[1024,256]{1,0:T(8,128)(2,1)S(1)}, bf16[1024,256]{1,0:T(8,128)(2,1)S(1)}, u32[]{:S(2)}, u32[]{:S(2)}) collective-permute-start(bf16[1024,256]{1,0:T(8,128)(2,1)S(1)} %get-tuple-element.82), channel_id=1, source_target_pairs={{0,96},{4,28},{8,104},{12,20},{16,112},{20,12},{24,120},{28,4},{32... | collective-permute-start | bytes 1572872 | tf_op jit(solution)/shard_map/ppermute | solution.py:32
  13.1 1.3 %terms.9 = bf16[2048,256]{1,0:T(8,128)(2,1)S(1)} custom-call(s32[32]{0:T(128)S(1)} %fusion.3.refs_0_.block, bf16[512,448]{1,0:T(8,128)(2,1)S(1)} %get-tuple-element.59.refs_1_, bf16[448,8192]{1,0:T(8,128)(2,1)S(1)} %copy-done), custom_call_target="tpu_custom_call" | custom-call | flops 17179869184 | bytes 67108864 | tf_op jit(solution)/shard_map/terms/pallas_call | solution.py:137
  14.4 1.3 %terms.10 = (bf16[1024,256]{1,0:T(8,128)(2,1)S(1)}, bf16[1024,256]{1,0:T(8,128)(2,1)S(1)}) custom-call(s32[32]{0:T(128)S(1)} %fusion.3.refs_0_.block, bf16[512,448]{1,0:T(8,128)(2,1)S(1)} %get-tuple-element.59.refs_1_, bf16[448,8192]{1,0:T(8,128)(2,1)S(1)} %copy-done, bf16[2048,256]{1,0:T(8,128)(2,1)S(1)} %collective-permute-done.1.refs_3_.refs_4_, ...), custom_call_target="tpu_custom_call" | custom-call | flops 1048576 | bytes 65536 | tf_op jit(solution)/shard_map/terms/pallas_call | solution.py:137
  15.7 1.5 %collective-permute-start.6 = (bf16[1024,256]{1,0:T(8,128)(2,1)S(1)}, bf16[1024,256]{1,0:T(8,128)(2,1)S(1)}, u32[]{:S(2)}, u32[]{:S(2)}) collective-permute-start(bf16[1024,256]{1,0:T(8,128)(2,1)S(1)} %get-tuple-element.52), channel_id=1, source_target_pairs={{0,32},{4,12},{8,40},{12,4},{16,48},{20,28},{24,56},{28,20},{32,0}... | collective-permute-start | bytes 1572872 | tf_op jit(solution)/shard_map/ppermute | solution.py:32
  20.2 1.3 %collective-permute-done.4.refs_6_ = bf16[1024,256]{1,0:T(8,128)(2,1)S(1)} collective-permute-done((bf16[1024,256]{1,0:T(8,128)(2,1)S(1)}, bf16[1024,256]{1,0:T(8,128)(2,1)S(1)}, u32[]{:S(2)}, u32[]{:S(2)}) %collective-permute-start.4) | collective-permute-done | bytes 524320 | tf_op jit(solution)/shard_map/ppermute | solution.py:32
  21.5 1.4 %terms.12 = (bf16[1024,256]{1,0:T(8,128)(2,1)S(1)}, bf16[1024,256]{1,0:T(8,128)(2,1)S(1)}) custom-call(s32[32]{0:T(128)S(1)} %fusion.3.refs_0_.block, bf16[512,448]{1,0:T(8,128)(2,1)S(1)} %get-tuple-element.59.refs_1_, bf16[448,8192]{1,0:T(8,128)(2,1)S(1)} %copy-done, bf16[2048,256]{1,0:T(8,128)(2,1)S(1)} %collective-permute-done.2.refs_3_.refs_5_, ...), custom_call_target="tpu_custom_call" | custom-call | flops 1048576 | bytes 65536 | tf_op jit(solution)/shard_map/terms/pallas_call | solution.py:137
  23.3 2.2 %collective-permute-start.7 = (bf16[1024,256]{1,0:T(8,128)(2,1)S(1)}, bf16[1024,256]{1,0:T(8,128)(2,1)S(1)}, u32[]{:S(2)}, u32[]{:S(2)}) collective-permute-start(bf16[1024,256]{1,0:T(8,128)(2,1)S(1)} %get-tuple-element.57), channel_id=1, source_target_pairs={{0,96},{4,28},{8,104},{12,20},{16,112},{20,12},{24,120},{28,4},{32... | collective-permute-start | bytes 1572872 | tf_op jit(solution)/shard_map/ppermute | solution.py:32
  25.6 3.6 %back_columns.2.refs_3_ = bf16[448,8192]{1,0:T(8,128)(2,1)} custom-call(bf16[448,512]{1,0:T(8,128)(2,1)S(1)} %copy-done.3, bf16[448,8192]{1,0:T(8,128)(2,1)S(1)} %copy-done, bf16[8192,512]{1,0:T(8,128)(2,1)S(1)} %bitcast.1), custom_call_target="tpu_custom_call" | custom-call | flops 17179869184 | bytes 67108864 | tf_op jit(solution)/shard_map/back_columns/pallas_call | solution.py:168
  29.2 1.3 %terms.13.g0 = bf16[2048,256]{1,0:T(8,128)(2,1)S(1)} custom-call(s32[32]{0:T(128)S(1)} %fusion.3.refs_0_.block, bf16[512,448]{1,0:T(8,128)(2,1)S(1)} %get-tuple-element.59.refs_1_, bf16[448,8192]{1,0:T(8,128)(2,1)S(1)} %copy-done, bf16[2048,256]{1,0:T(8,128)(2,1)S(1)} %collective-permute-done.5.refs_3_), custom_call_target="tpu_custom_call" | custom-call | flops 1048576 | bytes 65536 | tf_op jit(solution)/shard_map/terms/pallas_call | solution.py:137
  30.5 2.2 %collective-permute-done.8 = bf16[1024,256]{1,0:T(8,128)(2,1)S(1)} collective-permute-done((bf16[1024,256]{1,0:T(8,128)(2,1)S(1)}, bf16[1024,256]{1,0:T(8,128)(2,1)S(1)}, u32[]{:S(2)}, u32[]{:S(2)}) %collective-permute-start.8) | collective-permute-done | bytes 524320 | tf_op jit(solution)/shard_map/ppermute | solution.py:32
  33.2 2.3 %collective-permute-start.12 = (bf16[512,256]{1,0:T(8,128)(2,1)S(1)}, bf16[512,256]{1,0:T(8,128)(2,1)S(1)}, u32[]{:S(2)}, u32[]{:S(2)}) collective-permute-start(bf16[512,256]{1,0:T(8,128)(2,1)S(1)} %get-tuple-element.79), channel_id=1, source_target_pairs={{0,24},{4,100},{8,16},{12,108},{16,8},{20,116},{24,0},{28,124},{32... | collective-permute-start | bytes 786440 | tf_op jit(solution)/shard_map/ppermute | solution.py:36
  36.5 3.5 %back_columns.3 = bf16[448,8192]{1,0:T(8,128)(2,1)} custom-call(bf16[448,512]{1,0:T(8,128)(2,1)S(1)} %copy-done.3, bf16[448,8192]{1,0:T(8,128)(2,1)S(1)} %copy-done, bf16[8192,512]{1,0:T(8,128)(2,1)S(1)} %bitcast.1, bf16[448,8192]{1,0:T(8,128)(2,1)} %back_columns.2.refs_3_), custom_call_target="tpu_custom_call", output_to_operand_aliasing={{}: (3, {})} | custom-call | flops 17179869184 | bytes 67108864 | tf_op jit(solution)/shard_map/back_columns/pallas_call | solution.py:168
  40.1 2.4 %collective-permute-done.12.g5 = bf16[512,256]{1,0:T(8,128)(2,1)S(1)} collective-permute-done((bf16[512,256]{1,0:T(8,128)(2,1)S(1)}, bf16[512,256]{1,0:T(8,128)(2,1)S(1)}, u32[]{:S(2)}, u32[]{:S(2)}) %collective-permute-start.12) | collective-permute-done | bytes 262176 | tf_op jit(solution)/shard_map/ppermute | solution.py:36
  43.4 2.1 %update_rows.1 = (f32[256,512]{1,0:T(8,128)}, f32[256,512]{1,0:T(8,128)}, f32[256,512]{1,0:T(8,128)S(1)}, bf16[272,512]{1,0:T(8,128)(2,1)S(1)}) custom-call(s32[32]{0:T(128)S(1)} %fusion.3.refs_0_.block, bf16[2048,256]{1,0:T(8,128)(2,1)S(1)} %terms.13.g0, bf16[1024,256]{1,0:T(8,128)(2,1)S(1)} %collective-permute-done.6.g1, ...), custom_call_target="tpu_custom_call" | custom-call | flops 1048576 | bytes 65536 | tf_op jit(solution)/shard_map/update_rows/pallas_call | solution.py:226
  45.6 2.2 %collective-permute-start.15 = (bf16[272,512]{1,0:T(8,128)(2,1)S(1)}, bf16[272,512]{1,0:T(8,128)(2,1)S(1)}, u32[]{:S(2)}, u32[]{:S(2)}) collective-permute-start(bf16[272,512]{1,0:T(8,128)(2,1)S(1)} %get-tuple-element.62.refs_0_), channel_id=1, source_target_pairs={{0,24},{4,100},{8,16},{12,108},{16,8},{20,116},{24,0},{28,124},{32... | collective-permute-start | bytes 835592 | tf_op jit(solution)/shard_map/ppermute | solution.py:36
  48.8 6.6 %collective-permute-done.15.refs_3_ = bf16[272,512]{1,0:T(8,128)(2,1)S(1)} collective-permute-done((bf16[272,512]{1,0:T(8,128)(2,1)S(1)}, bf16[272,512]{1,0:T(8,128)(2,1)S(1)}, u32[]{:S(2)}, u32[]{:S(2)}) %collective-permute-start.15) | collective-permute-done | bytes 278560 | tf_op jit(solution)/shard_map/ppermute | solution.py:36
  56.0 2.5 %collective-permute-start.22 = (bf16[1024,512]{1,0:T(8,128)(2,1)S(1)}, bf16[1024,512]{1,0:T(8,128)(2,1)S(1)}, u32[]{:S(2)}, u32[]{:S(2)}) collective-permute-start(bf16[1024,512]{1,0:T(8,128)(2,1)S(1)} %get-tuple-element.68.refs_3_), channel_id=1, source_target_pairs={{0,96},{4,28},{8,104},{12,20},{16,112},{20,12},{24,120},{28,4},{32... | collective-permute-start | bytes 3145736 | tf_op jit(solution)/shard_map/ppermute | solution.py:32
  58.5 1.3 %collective-permute-start.16 = (f32[16,128]{1,0:T(8,128)S(1)}, f32[16,128]{1,0:T(8,128)S(1)}, u32[]{:S(2)}, u32[]{:S(2)}) collective-permute-start(f32[16,128]{1,0:T(8,128)S(1)} %get-tuple-element.63), channel_id=1, source_target_pairs={{0,1},{1,0},{2,3},{3,2},{4,5},{5,4},{6,7},{7,6},{8,9},{9,8},{10,11... | collective-permute-start | bytes 24584 | tf_op jit(solution)/shard_map/ppermute | solution.py:40
  61.0 2.7 %collective-permute-start.17 = (f32[16,128]{1,0:T(8,128)S(1)}, f32[16,128]{1,0:T(8,128)S(1)}, u32[]{:S(2)}, u32[]{:S(2)}) collective-permute-start(f32[16,128]{1,0:T(8,128)S(1)} %add.58), channel_id=1, source_target_pairs={{0,3},{1,2},{2,1},{3,0},{4,7},{5,6},{6,5},{7,4},{8,11},{9,10},{10,... | collective-permute-start | bytes 24584 | tf_op jit(solution)/shard_map/ppermute | solution.py:40
  63.7 1.3 %collective-permute-done.17 = f32[16,128]{1,0:T(8,128)S(1)} collective-permute-done((f32[16,128]{1,0:T(8,128)S(1)}, f32[16,128]{1,0:T(8,128)S(1)}, u32[]{:S(2)}, u32[]{:S(2)}) %collective-permute-start.17) | collective-permute-done | bytes 8224 | tf_op jit(solution)/shard_map/ppermute | solution.py:40
  65.4 2.9 %collective-permute-start.19 = (f32[16,128]{1,0:T(8,128)S(1)}, f32[16,128]{1,0:T(8,128)S(1)}, u32[]{:S(2)}, u32[]{:S(2)}) collective-permute-start(f32[16,128]{1,0:T(8,128)S(1)} %add.59), channel_id=1, source_target_pairs={{0,64},{4,20},{8,72},{12,28},{16,80},{20,4},{24,88},{28,12},{32,96... | collective-permute-start | bytes 24584 | tf_op jit(solution)/shard_map/ppermute | solution.py:32
  68.3 3.0 %collective-permute-done.20 = f32[16,128]{1,0:T(8,128)S(1)} collective-permute-done((f32[16,128]{1,0:T(8,128)S(1)}, f32[16,128]{1,0:T(8,128)S(1)}, u32[]{:S(2)}, u32[]{:S(2)}) %collective-permute-start.20) | collective-permute-done | bytes 8224 | tf_op jit(solution)/shard_map/ppermute | solution.py:32
  71.3 2.0 %collective-permute-done.19 = f32[16,128]{1,0:T(8,128)S(1)} collective-permute-done((f32[16,128]{1,0:T(8,128)S(1)}, f32[16,128]{1,0:T(8,128)S(1)}, u32[]{:S(2)}, u32[]{:S(2)}) %collective-permute-start.19) | collective-permute-done | bytes 8224 | tf_op jit(solution)/shard_map/ppermute | solution.py:32
  73.5 4.7 %collective-permute-start.23 = (bf16[1024,512]{1,0:T(8,128)(2,1)S(1)}, bf16[1024,512]{1,0:T(8,128)(2,1)S(1)}, u32[]{:S(2)}, u32[]{:S(2)}) collective-permute-start(bf16[1024,512]{1,0:T(8,128)(2,1)S(1)} %get-tuple-element.68.refs_3_), channel_id=1, source_target_pairs={{0,4},{4,0},{1,5},{5,1},{2,6},{6,2},{3,7},{7,3},{8,12},{12,8},{9,1... | collective-permute-start | bytes 3145736 | tf_op jit(solution)/shard_map/ppermute | solution.py:44
  79.5 3.3 %collective-permute-start.25 = (bf16[512,512]{1,0:T(8,128)(2,1)S(1)}, bf16[512,512]{1,0:T(8,128)(2,1)S(1)}, u32[]{:S(2)}, u32[]{:S(2)}) collective-permute-start(bf16[512,512]{1,0:T(8,128)(2,1)S(1)} %taken.2), channel_id=1, source_target_pairs={{0,96},{4,28},{8,104},{12,20},{16,112},{20,12},{24,120},{28,4},{32... | collective-permute-start | bytes 1572872 | tf_op jit(solution)/shard_map/ppermute | solution.py:32
  83.9 4.3 %apply_update.2 = (bf16[8192,512]{1,0:T(8,128)(2,1)}, f32[256,512]{1,0:T(8,128)}) custom-call(s32[32]{0:T(128)S(1)} %fusion.3.refs_0_.block, f32[16,128]{1,0:T(8,128)S(1)} %add.63.refs_1_, bf16[8192,512]{1,0:T(8,128)(2,1)S(1)} %bitcast.1, bf16[1024,512]{1,0:T(8,128)(2,1)S(1)} %get-tuple-element.68.refs_3_, ...), custom_call_target="tpu_custom_call" | custom-call | flops 1048576 | bytes 65536 | tf_op jit(solution)/shard_map/apply_update/pallas_call | solution.py:277
  90.0 1.4 %collective-permute-done.29.refs_5_ = bf16[512,512]{1,0:T(8,128)(2,1)S(1)} collective-permute-done((bf16[512,512]{1,0:T(8,128)(2,1)S(1)}, bf16[512,512]{1,0:T(8,128)(2,1)S(1)}, u32[]{:S(2)}, u32[]{:S(2)}) %collective-permute-start.29) | collective-permute-done | bytes 524320 | tf_op jit(solution)/shard_map/ppermute | solution.py:44
  92.2 2.1 %apply_update.3 = bf16[8192,512]{1,0:T(8,128)(2,1)} custom-call(s32[32]{0:T(128)S(1)} %fusion.3.refs_0_.block, f32[16,128]{1,0:T(8,128)S(1)} %add.63.refs_1_, bf16[8192,512]{1,0:T(8,128)(2,1)S(1)} %bitcast.1, bf16[512,512]{1,0:T(8,128)(2,1)S(1)} %collective-permute-done.25.refs_3_, ...), custom_call_target="tpu_custom_call", output_to_operand_aliasing={{}: (7, {})} | custom-call | flops 1048576 | bytes 65536 | tf_op jit(solution)/shard_map/apply_update/pallas_call | solution.py:277
  (66 shorter events, 14.6 us)
Async XLA Ops:
  4.8 4.2 %collective-permute-start = (bf16[2048,256]{1,0:T(8,128)(2,1)S(1)}, bf16[2048,256]{1,0:T(8,128)(2,1)S(1)}, u32[]{:S(2)}, u32[]{:S(2)}) collective-permute-start(bf16[2048,256]{1,0:T(8,128)(2,1)S(1)} %get-tuple-element.43), channel_id=1, source_target_pairs={{0,4},{4,0},{1,5},{5,1},{2,6},{6,2},{3,7},{7,3},{8,12},{12,8},{9,1... | collective-permute-start | bytes 3145736 | tf_op jit(solution)/shard_map/ppermute | solution.py:44
  8.8 5.6 %collective-permute-start.1 = (bf16[2048,256]{1,0:T(8,128)(2,1)S(1)}, bf16[2048,256]{1,0:T(8,128)(2,1)S(1)}, u32[]{:S(2)}, u32[]{:S(2)}) collective-permute-start(bf16[2048,256]{1,0:T(8,128)(2,1)S(1)} %terms.8), channel_id=1, source_target_pairs={{0,4},{4,0},{1,5},{5,1},{2,6},{6,2},{3,7},{7,3},{8,12},{12,8},{9,1... | collective-permute-start | bytes 3145736 | tf_op jit(solution)/shard_map/ppermute | solution.py:44
  9.2 10.6 %collective-permute-start.3 = (bf16[1024,256]{1,0:T(8,128)(2,1)S(1)}, bf16[1024,256]{1,0:T(8,128)(2,1)S(1)}, u32[]{:S(2)}, u32[]{:S(2)}) collective-permute-start(bf16[1024,256]{1,0:T(8,128)(2,1)S(1)} %get-tuple-element.82), channel_id=1, source_target_pairs={{0,96},{4,28},{8,104},{12,20},{16,112},{20,12},{24,120},{28,4},{32... | collective-permute-start | bytes 1572872 | tf_op jit(solution)/shard_map/ppermute | solution.py:32
  13.1 8.3 %collective-permute-start.4 = (bf16[1024,256]{1,0:T(8,128)(2,1)S(1)}, bf16[1024,256]{1,0:T(8,128)(2,1)S(1)}, u32[]{:S(2)}, u32[]{:S(2)}) collective-permute-start(bf16[1024,256]{1,0:T(8,128)(2,1)S(1)} %get-tuple-element.83), channel_id=1, source_target_pairs={{0,32},{4,12},{8,40},{12,4},{16,48},{20,28},{24,56},{28,20},{32,0}... | collective-permute-start | bytes 1572872 | tf_op jit(solution)/shard_map/ppermute | solution.py:32
  15.7 14.8 %collective-permute-start.6 = (bf16[1024,256]{1,0:T(8,128)(2,1)S(1)}, bf16[1024,256]{1,0:T(8,128)(2,1)S(1)}, u32[]{:S(2)}, u32[]{:S(2)}) collective-permute-start(bf16[1024,256]{1,0:T(8,128)(2,1)S(1)} %get-tuple-element.52), channel_id=1, source_target_pairs={{0,32},{4,12},{8,40},{12,4},{16,48},{20,28},{24,56},{28,20},{32,0}... | collective-permute-start | bytes 1572872 | tf_op jit(solution)/shard_map/ppermute | solution.py:32
  17.2 8.4 %slice-start.1 = ((s8[8388608]{0:T(1024)(128)(4,1)}), s8[4194304]{0:T(1024)(128)(4,1)S(1)}, s32[]{:S(2)}) async-start(s8[8388608]{0:T(1024)(128)(4,1)} %bitcast), calls=%async_computation.1 | async-start | bytes 8388608
  17.2 13.2 %collective-permute-start.9 = (bf16[1024,256]{1,0:T(8,128)(2,1)S(1)}, bf16[1024,256]{1,0:T(8,128)(2,1)S(1)}, u32[]{:S(2)}, u32[]{:S(2)}) collective-permute-start(bf16[1024,256]{1,0:T(8,128)(2,1)S(1)} %get-tuple-element.53), channel_id=1, source_target_pairs={{0,96},{4,28},{8,104},{12,20},{16,112},{20,12},{24,120},{28,4},{32... | collective-permute-start | bytes 1572872 | tf_op jit(solution)/shard_map/ppermute | solution.py:32
  17.3 4.1 %collective-permute-start.2 = (bf16[2048,256]{1,0:T(8,128)(2,1)S(1)}, bf16[2048,256]{1,0:T(8,128)(2,1)S(1)}, u32[]{:S(2)}, u32[]{:S(2)}) collective-permute-start(bf16[2048,256]{1,0:T(8,128)(2,1)S(1)} %terms.9), channel_id=1, source_target_pairs={{0,4},{4,0},{1,5},{5,1},{2,6},{6,2},{3,7},{7,3},{8,12},{12,8},{9,1... | collective-permute-start | bytes 3145736 | tf_op jit(solution)/shard_map/ppermute | solution.py:44
  19.8 9.4 %collective-permute-start.5 = (bf16[2048,256]{1,0:T(8,128)(2,1)S(1)}, bf16[2048,256]{1,0:T(8,128)(2,1)S(1)}, u32[]{:S(2)}, u32[]{:S(2)}) collective-permute-start(bf16[2048,256]{1,0:T(8,128)(2,1)S(1)} %terms.11), channel_id=1, source_target_pairs={{0,4},{4,0},{1,5},{5,1},{2,6},{6,2},{3,7},{7,3},{8,12},{12,8},{9,1... | collective-permute-start | bytes 3145736 | tf_op jit(solution)/shard_map/ppermute | solution.py:44
  22.8 9.9 %collective-permute-start.8 = (bf16[1024,256]{1,0:T(8,128)(2,1)S(1)}, bf16[1024,256]{1,0:T(8,128)(2,1)S(1)}, u32[]{:S(2)}, u32[]{:S(2)}) collective-permute-start(bf16[1024,256]{1,0:T(8,128)(2,1)S(1)} %get-tuple-element.56), channel_id=1, source_target_pairs={{0,32},{4,12},{8,40},{12,4},{16,48},{20,28},{24,56},{28,20},{32,0}... | collective-permute-start | bytes 1572872 | tf_op jit(solution)/shard_map/ppermute | solution.py:32
  23.3 9.5 %collective-permute-start.7 = (bf16[1024,256]{1,0:T(8,128)(2,1)S(1)}, bf16[1024,256]{1,0:T(8,128)(2,1)S(1)}, u32[]{:S(2)}, u32[]{:S(2)}) collective-permute-start(bf16[1024,256]{1,0:T(8,128)(2,1)S(1)} %get-tuple-element.57), channel_id=1, source_target_pairs={{0,96},{4,28},{8,104},{12,20},{16,112},{20,12},{24,120},{28,4},{32... | collective-permute-start | bytes 1572872 | tf_op jit(solution)/shard_map/ppermute | solution.py:32
  33.2 9.3 %collective-permute-start.12 = (bf16[512,256]{1,0:T(8,128)(2,1)S(1)}, bf16[512,256]{1,0:T(8,128)(2,1)S(1)}, u32[]{:S(2)}, u32[]{:S(2)}) collective-permute-start(bf16[512,256]{1,0:T(8,128)(2,1)S(1)} %get-tuple-element.79), channel_id=1, source_target_pairs={{0,24},{4,100},{8,16},{12,108},{16,8},{20,116},{24,0},{28,124},{32... | collective-permute-start | bytes 786440 | tf_op jit(solution)/shard_map/ppermute | solution.py:36
  35.4 7.1 %collective-permute-start.11 = (bf16[512,256]{1,0:T(8,128)(2,1)S(1)}, bf16[512,256]{1,0:T(8,128)(2,1)S(1)}, u32[]{:S(2)}, u32[]{:S(2)}) collective-permute-start(bf16[512,256]{1,0:T(8,128)(2,1)S(1)} %get-tuple-element.80), channel_id=1, source_target_pairs={{0,16},{4,68},{8,24},{12,76},{16,0},{20,84},{24,8},{28,92},{32,48}... | collective-permute-start | bytes 786440 | tf_op jit(solution)/shard_map/ppermute | solution.py:36
  36.0 7.5 %collective-permute-start.10 = (bf16[512,256]{1,0:T(8,128)(2,1)S(1)}, bf16[512,256]{1,0:T(8,128)(2,1)S(1)}, u32[]{:S(2)}, u32[]{:S(2)}) collective-permute-start(bf16[512,256]{1,0:T(8,128)(2,1)S(1)} %get-tuple-element.81), channel_id=1, source_target_pairs={{0,8},{4,36},{8,0},{12,44},{16,24},{20,52},{24,16},{28,60},{32,40}... | collective-permute-start | bytes 786440 | tf_op jit(solution)/shard_map/ppermute | solution.py:36
  45.6 9.9 %collective-permute-start.15 = (bf16[272,512]{1,0:T(8,128)(2,1)S(1)}, bf16[272,512]{1,0:T(8,128)(2,1)S(1)}, u32[]{:S(2)}, u32[]{:S(2)}) collective-permute-start(bf16[272,512]{1,0:T(8,128)(2,1)S(1)} %get-tuple-element.62.refs_0_), channel_id=1, source_target_pairs={{0,24},{4,100},{8,16},{12,108},{16,8},{20,116},{24,0},{28,124},{32... | collective-permute-start | bytes 835592 | tf_op jit(solution)/shard_map/ppermute | solution.py:36
  47.7 7.7 %collective-permute-start.14 = (bf16[272,512]{1,0:T(8,128)(2,1)S(1)}, bf16[272,512]{1,0:T(8,128)(2,1)S(1)}, u32[]{:S(2)}, u32[]{:S(2)}) collective-permute-start(bf16[272,512]{1,0:T(8,128)(2,1)S(1)} %get-tuple-element.62.refs_0_), channel_id=1, source_target_pairs={{0,16},{4,68},{8,24},{12,76},{16,0},{20,84},{24,8},{28,92},{32,48}... | collective-permute-start | bytes 835592 | tf_op jit(solution)/shard_map/ppermute | solution.py:36
  48.3 7.7 %collective-permute-start.13 = (bf16[272,512]{1,0:T(8,128)(2,1)S(1)}, bf16[272,512]{1,0:T(8,128)(2,1)S(1)}, u32[]{:S(2)}, u32[]{:S(2)}) collective-permute-start(bf16[272,512]{1,0:T(8,128)(2,1)S(1)} %get-tuple-element.62.refs_0_), channel_id=1, source_target_pairs={{0,8},{4,36},{8,0},{12,44},{16,24},{20,52},{24,16},{28,60},{32,40}... | collective-permute-start | bytes 835592 | tf_op jit(solution)/shard_map/ppermute | solution.py:36
  56.0 17.3 %collective-permute-start.22 = (bf16[1024,512]{1,0:T(8,128)(2,1)S(1)}, bf16[1024,512]{1,0:T(8,128)(2,1)S(1)}, u32[]{:S(2)}, u32[]{:S(2)}) collective-permute-start(bf16[1024,512]{1,0:T(8,128)(2,1)S(1)} %get-tuple-element.68.refs_3_), channel_id=1, source_target_pairs={{0,96},{4,28},{8,104},{12,20},{16,112},{20,12},{24,120},{28,4},{32... | collective-permute-start | bytes 3145736 | tf_op jit(solution)/shard_map/ppermute | solution.py:32
  58.5 14.9 %collective-permute-start.21 = (bf16[1024,512]{1,0:T(8,128)(2,1)S(1)}, bf16[1024,512]{1,0:T(8,128)(2,1)S(1)}, u32[]{:S(2)}, u32[]{:S(2)}) collective-permute-start(bf16[1024,512]{1,0:T(8,128)(2,1)S(1)} %get-tuple-element.68.refs_3_), channel_id=1, source_target_pairs={{0,32},{4,12},{8,40},{12,4},{16,48},{20,28},{24,56},{28,20},{32,0}... | collective-permute-start | bytes 3145736 | tf_op jit(solution)/shard_map/ppermute | solution.py:32
  58.5 2.5 %collective-permute-start.16 = (f32[16,128]{1,0:T(8,128)S(1)}, f32[16,128]{1,0:T(8,128)S(1)}, u32[]{:S(2)}, u32[]{:S(2)}) collective-permute-start(f32[16,128]{1,0:T(8,128)S(1)} %get-tuple-element.63), channel_id=1, source_target_pairs={{0,1},{1,0},{2,3},{3,2},{4,5},{5,4},{6,7},{7,6},{8,9},{9,8},{10,11... | collective-permute-start | bytes 24584 | tf_op jit(solution)/shard_map/ppermute | solution.py:40
  61.0 4.1 %collective-permute-start.17 = (f32[16,128]{1,0:T(8,128)S(1)}, f32[16,128]{1,0:T(8,128)S(1)}, u32[]{:S(2)}, u32[]{:S(2)}) collective-permute-start(f32[16,128]{1,0:T(8,128)S(1)} %add.58), channel_id=1, source_target_pairs={{0,3},{1,2},{2,1},{3,0},{4,7},{5,6},{6,5},{7,4},{8,11},{9,10},{10,... | collective-permute-start | bytes 24584 | tf_op jit(solution)/shard_map/ppermute | solution.py:40
  65.0 6.3 %collective-permute-start.20 = (f32[16,128]{1,0:T(8,128)S(1)}, f32[16,128]{1,0:T(8,128)S(1)}, u32[]{:S(2)}, u32[]{:S(2)}) collective-permute-start(f32[16,128]{1,0:T(8,128)S(1)} %add.59), channel_id=1, source_target_pairs={{0,96},{4,28},{8,104},{12,20},{16,112},{20,12},{24,120},{28,4},{32... | collective-permute-start | bytes 24584 | tf_op jit(solution)/shard_map/ppermute | solution.py:32
  65.4 8.0 %collective-permute-start.19 = (f32[16,128]{1,0:T(8,128)S(1)}, f32[16,128]{1,0:T(8,128)S(1)}, u32[]{:S(2)}, u32[]{:S(2)}) collective-permute-start(f32[16,128]{1,0:T(8,128)S(1)} %add.59), channel_id=1, source_target_pairs={{0,64},{4,20},{8,72},{12,28},{16,80},{20,4},{24,88},{28,12},{32,96... | collective-permute-start | bytes 24584 | tf_op jit(solution)/shard_map/ppermute | solution.py:32
  68.3 5.0 %collective-permute-start.18 = (f32[16,128]{1,0:T(8,128)S(1)}, f32[16,128]{1,0:T(8,128)S(1)}, u32[]{:S(2)}, u32[]{:S(2)}) collective-permute-start(f32[16,128]{1,0:T(8,128)S(1)} %add.59), channel_id=1, source_target_pairs={{0,32},{4,12},{8,40},{12,4},{16,48},{20,28},{24,56},{28,20},{32,0}... | collective-permute-start | bytes 24584 | tf_op jit(solution)/shard_map/ppermute | solution.py:32
  73.5 9.3 %collective-permute-start.23 = (bf16[1024,512]{1,0:T(8,128)(2,1)S(1)}, bf16[1024,512]{1,0:T(8,128)(2,1)S(1)}, u32[]{:S(2)}, u32[]{:S(2)}) collective-permute-start(bf16[1024,512]{1,0:T(8,128)(2,1)S(1)} %get-tuple-element.68.refs_3_), channel_id=1, source_target_pairs={{0,4},{4,0},{1,5},{5,1},{2,6},{6,2},{3,7},{7,3},{8,12},{12,8},{9,1... | collective-permute-start | bytes 3145736 | tf_op jit(solution)/shard_map/ppermute | solution.py:44
  78.1 5.8 %collective-permute-start.26 = (bf16[1024,512]{1,0:T(8,128)(2,1)S(1)}, bf16[1024,512]{1,0:T(8,128)(2,1)S(1)}, u32[]{:S(2)}, u32[]{:S(2)}) collective-permute-start(bf16[1024,512]{1,0:T(8,128)(2,1)S(1)} %collective-permute-done.21.ref.refs_4_), channel_id=1, source_target_pairs={{0,4},{4,0},{1,5},{5,1},{2,6},{6,2},{3,7},{7,3},{8,12},{12,8},{9,1... | collective-permute-start | bytes 3145736 | tf_op jit(solution)/shard_map/ppermute | solution.py:44
  78.2 5.7 %collective-permute-start.27 = (bf16[1024,512]{1,0:T(8,128)(2,1)S(1)}, bf16[1024,512]{1,0:T(8,128)(2,1)S(1)}, u32[]{:S(2)}, u32[]{:S(2)}) collective-permute-start(bf16[1024,512]{1,0:T(8,128)(2,1)S(1)} %collective-permute-done.22.ref.refs_5_), channel_id=1, source_target_pairs={{0,4},{4,0},{1,5},{5,1},{2,6},{6,2},{3,7},{7,3},{8,12},{12,8},{9,1... | collective-permute-start | bytes 3145736 | tf_op jit(solution)/shard_map/ppermute | solution.py:44
  78.7 9.6 %collective-permute-start.28 = (bf16[512,512]{1,0:T(8,128)(2,1)S(1)}, bf16[512,512]{1,0:T(8,128)(2,1)S(1)}, u32[]{:S(2)}, u32[]{:S(2)}) collective-permute-start(bf16[512,512]{1,0:T(8,128)(2,1)S(1)} %taken.3), channel_id=1, source_target_pairs={{0,32},{4,12},{8,40},{12,4},{16,48},{20,28},{24,56},{28,20},{32,0}... | collective-permute-start | bytes 1572872 | tf_op jit(solution)/shard_map/ppermute | solution.py:32
  79.5 10.1 %collective-permute-start.25 = (bf16[512,512]{1,0:T(8,128)(2,1)S(1)}, bf16[512,512]{1,0:T(8,128)(2,1)S(1)}, u32[]{:S(2)}, u32[]{:S(2)}) collective-permute-start(bf16[512,512]{1,0:T(8,128)(2,1)S(1)} %taken.2), channel_id=1, source_target_pairs={{0,96},{4,28},{8,104},{12,20},{16,112},{20,12},{24,120},{28,4},{32... | collective-permute-start | bytes 1572872 | tf_op jit(solution)/shard_map/ppermute | solution.py:32
  82.7 1.2 %collective-permute-start.24 = (f32[16,128]{1,0:T(8,128)S(1)}, f32[16,128]{1,0:T(8,128)S(1)}, u32[]{:S(2)}, u32[]{:S(2)}) collective-permute-start(f32[16,128]{1,0:T(8,128)S(1)} %add_add_fusion), channel_id=1, source_target_pairs={{0,4},{4,0},{1,5},{5,1},{2,6},{6,2},{3,7},{7,3},{8,12},{12,8},{9,1... | collective-permute-start | bytes 24584 | tf_op jit(solution)/shard_map/ppermute | solution.py:44
  89.5 1.9 %collective-permute-start.29 = (bf16[512,512]{1,0:T(8,128)(2,1)S(1)}, bf16[512,512]{1,0:T(8,128)(2,1)S(1)}, u32[]{:S(2)}, u32[]{:S(2)}) collective-permute-start(bf16[512,512]{1,0:T(8,128)(2,1)S(1)} %collective-permute-done.25.refs_3_), channel_id=1, source_target_pairs={{0,4},{4,0},{1,5},{5,1},{2,6},{6,2},{3,7},{7,3},{8,12},{12,8},{9,1... | collective-permute-start | bytes 1572872 | tf_op jit(solution)/shard_map/ppermute | solution.py:44
  89.9 2.3 %collective-permute-start.30 = (bf16[512,512]{1,0:T(8,128)(2,1)S(1)}, bf16[512,512]{1,0:T(8,128)(2,1)S(1)}, u32[]{:S(2)}, u32[]{:S(2)}) collective-permute-start(bf16[512,512]{1,0:T(8,128)(2,1)S(1)} %collective-permute-done.28.refs_4_), channel_id=1, source_target_pairs={{0,4},{4,0},{1,5},{5,1},{2,6},{6,2},{3,7},{7,3},{8,12},{12,8},{9,1... | collective-permute-start | bytes 1572872 | tf_op jit(solution)/shard_map/ppermute | solution.py:44
  (5 other events, 35.5 us)

commit v5 on v4

--- a/solution.py
+++ b/solution.py
@@ -439,14 +439,12 @@
         None,
     )
     far_low, far_high = after(far_low, new_weight), after(far_high, new_weight)
+    far_others = [sibling(far_low), sibling(far_high)]
     (new_weight,) = apply_update(
-        blocks,
-        own_unit(2) + other_unit(2),
-        sums,
-        weight,
-        [far_low, far_high, sibling(far_low), sibling(far_high)],
-        None,
-        new_weight,
+        blocks, own_unit(2), sums, weight, [far_low, far_high], None, new_weight
+    )
+    (new_weight,) = apply_update(
+        blocks, other_unit(2), sums, weight, far_others, None, new_weight
     )
     return (input_grad, new_weight, first_next, second_next, trust_step)
 

time: 94.5 us -> 94.2 us (level)
  waiting for transfers between devices: 27.2 us -> 25.5 us
  Pallas kernels: 28.9 us -> 30.2 us
    ppermute x10, waiting for transfers between devices: 3.36 us -> 1.65 us  [sibling(): return lax.ppermute(value, 'c', [(0, 1), (1, 0)])]
    pallas_call x2 -> x3, Pallas kernels: 6.4 us -> 7.71 us  [apply_update(): pl.pallas_call(body, out_shape=(jax.ShapeDtypeStruct(weight.shape, jnp.bf...]
  transfers between devices with their start and end apart: 31 -> 31, of which waited for: 16 -> 15; matrix products, arithmetic and copies ran while one was open for 0% -> 0% of each run, Pallas kernels for 22% -> 24%
where the time goes in v5:
time: 94.2 us; the launch traced here: 94 us
  starting transfers between devices  36.8 us (39%)
  Pallas kernels  30.2 us (32%)
  waiting for transfers between devices  25.5 us (27%)
  between operations  1.03 us (1%)
    ppermute x13, starting transfers between devices, along_first(): return lax.ppermute(value, DP, exchanges('first', k))  18.1 us
    ppermute x13, waiting for transfers between devices, along_first(): return lax.ppermute(value, DP, exchanges('first', k))  10.8 us
    ppermute x6, waiting for transfers between devices, along_second(): return lax.ppermute(value, DP, exchanges('second', k))  10.5 us
    pallas_call x7, Pallas kernels, terms(): pl.pallas_call(body, out_shape=tuple((jax.ShapeDtypeStruct((p * D, ROWS),...  8.98 us
    ppermute x10, starting transfers between devices, sibling(): return lax.ppermute(value, 'c', [(0, 1), (1, 0)])  8.05 us
    pallas_call x3, Pallas kernels, apply_update(): pl.pallas_call(body, out_shape=(jax.ShapeDtypeStruct(weight.shape, jnp.bf...  7.71 us
    pallas_call x2, Pallas kernels, back_columns(): pl.pallas_call(body, out_shape=jax.ShapeDtypeStruct(preactivation.shape,...  7.11 us
    ppermute x6, starting transfers between devices, along_second(): return lax.ppermute(value, DP, exchanges('second', k))  6.59 us
  transfers between devices with their start and end apart: 31, of which 15 were waited for; matrix products, arithmetic and copies ran while one was open for 0% of the time, Pallas kernels for 24%

profile of v5, /device:TPU:1, one launch (start us, length us, event | category | flops | bytes accessed | tf_op | source)
XLA Modules:
  0.0 94.0 jit_solution(2029434478111925611)
XLA Ops:
  0.7 4.1 %first_terms.1 = (bf16[2048,256]{1,0:T(8,128)(2,1)S(1)}, bf16[512,448]{1,0:T(8,128)(2,1)S(1)}) custom-call(s32[32]{0:T(128)S(1)} %fusion.3.refs_0_.block, bf16[448,512]{1,0:T(8,128)(2,1)} %refs_0_.1, bf16[448,8192]{1,0:T(8,128)(2,1)} %refs_1_.5), custom_call_target="tpu_custom_call" | custom-call | flops 17179869184 | bytes 67108864 | tf_op jit(solution)/shard_map/first_terms/pallas_call | solution.py:91
  4.8 1.5 %collective-permute-start = (bf16[2048,256]{1,0:T(8,128)(2,1)S(1)}, bf16[2048,256]{1,0:T(8,128)(2,1)S(1)}, u32[]{:S(2)}, u32[]{:S(2)}) collective-permute-start(bf16[2048,256]{1,0:T(8,128)(2,1)S(1)} %get-tuple-element.43), channel_id=1, source_target_pairs={{0,4},{4,0},{1,5},{5,1},{2,6},{6,2},{3,7},{7,3},{8,12},{12,8},{9,1... | collective-permute-start | bytes 3145736 | tf_op jit(solution)/shard_map/ppermute | solution.py:44
  6.3 1.3 %terms.7 = (bf16[1024,256]{1,0:T(8,128)(2,1)S(1)}, bf16[1024,256]{1,0:T(8,128)(2,1)S(1)}) custom-call(s32[32]{0:T(128)S(1)} %fusion.3.refs_0_.block, bf16[512,448]{1,0:T(8,128)(2,1)S(1)} %get-tuple-element.59.refs_1_, bf16[448,8192]{1,0:T(8,128)(2,1)S(1)} %copy-done), custom_call_target="tpu_custom_call" | custom-call | flops 17179869184 | bytes 67108864 | tf_op jit(solution)/shard_map/terms/pallas_call | solution.py:137
  7.5 1.3 %terms.8 = bf16[2048,256]{1,0:T(8,128)(2,1)S(1)} custom-call(s32[32]{0:T(128)S(1)} %fusion.3.refs_0_.block, bf16[512,448]{1,0:T(8,128)(2,1)S(1)} %get-tuple-element.59.refs_1_, bf16[448,8192]{1,0:T(8,128)(2,1)S(1)} %copy-done), custom_call_target="tpu_custom_call" | custom-call | flops 1048576 | bytes 65536 | tf_op jit(solution)/shard_map/terms/pallas_call | solution.py:137
  9.2 3.9 %collective-permute-start.3 = (bf16[1024,256]{1,0:T(8,128)(2,1)S(1)}, bf16[1024,256]{1,0:T(8,128)(2,1)S(1)}, u32[]{:S(2)}, u32[]{:S(2)}) collective-permute-start(bf16[1024,256]{1,0:T(8,128)(2,1)S(1)} %get-tuple-element.82), channel_id=1, source_target_pairs={{0,96},{4,28},{8,104},{12,20},{16,112},{20,12},{24,120},{28,4},{32... | collective-permute-start | bytes 1572872 | tf_op jit(solution)/shard_map/ppermute | solution.py:32
  14.4 1.3 %terms.10 = (bf16[1024,256]{1,0:T(8,128)(2,1)S(1)}, bf16[1024,256]{1,0:T(8,128)(2,1)S(1)}) custom-call(s32[32]{0:T(128)S(1)} %fusion.3.refs_0_.block, bf16[512,448]{1,0:T(8,128)(2,1)S(1)} %get-tuple-element.59.refs_1_, bf16[448,8192]{1,0:T(8,128)(2,1)S(1)} %copy-done, bf16[2048,256]{1,0:T(8,128)(2,1)S(1)} %collective-permute-done.1.refs_3_.refs_4_, ...), custom_call_target="tpu_custom_call" | custom-call | flops 1048576 | bytes 65536 | tf_op jit(solution)/shard_map/terms/pallas_call | solution.py:137
  15.7 1.5 %collective-permute-start.6 = (bf16[1024,256]{1,0:T(8,128)(2,1)S(1)}, bf16[1024,256]{1,0:T(8,128)(2,1)S(1)}, u32[]{:S(2)}, u32[]{:S(2)}) collective-permute-start(bf16[1024,256]{1,0:T(8,128)(2,1)S(1)} %get-tuple-element.52), channel_id=1, source_target_pairs={{0,32},{4,12},{8,40},{12,4},{16,48},{20,28},{24,56},{28,20},{32,0}... | collective-permute-start | bytes 1572872 | tf_op jit(solution)/shard_map/ppermute | solution.py:32
  20.1 1.3 %collective-permute-done.4.refs_6_ = bf16[1024,256]{1,0:T(8,128)(2,1)S(1)} collective-permute-done((bf16[1024,256]{1,0:T(8,128)(2,1)S(1)}, bf16[1024,256]{1,0:T(8,128)(2,1)S(1)}, u32[]{:S(2)}, u32[]{:S(2)}) %collective-permute-start.4) | collective-permute-done | bytes 524320 | tf_op jit(solution)/shard_map/ppermute | solution.py:32
  21.4 1.4 %terms.12 = (bf16[1024,256]{1,0:T(8,128)(2,1)S(1)}, bf16[1024,256]{1,0:T(8,128)(2,1)S(1)}) custom-call(s32[32]{0:T(128)S(1)} %fusion.3.refs_0_.block, bf16[512,448]{1,0:T(8,128)(2,1)S(1)} %get-tuple-element.59.refs_1_, bf16[448,8192]{1,0:T(8,128)(2,1)S(1)} %copy-done, bf16[2048,256]{1,0:T(8,128)(2,1)S(1)} %collective-permute-done.2.refs_3_.refs_5_, ...), custom_call_target="tpu_custom_call" | custom-call | flops 1048576 | bytes 65536 | tf_op jit(solution)/shard_map/terms/pallas_call | solution.py:137
  23.3 2.3 %collective-permute-start.7 = (bf16[1024,256]{1,0:T(8,128)(2,1)S(1)}, bf16[1024,256]{1,0:T(8,128)(2,1)S(1)}, u32[]{:S(2)}, u32[]{:S(2)}) collective-permute-start(bf16[1024,256]{1,0:T(8,128)(2,1)S(1)} %get-tuple-element.57), channel_id=1, source_target_pairs={{0,96},{4,28},{8,104},{12,20},{16,112},{20,12},{24,120},{28,4},{32... | collective-permute-start | bytes 1572872 | tf_op jit(solution)/shard_map/ppermute | solution.py:32
  25.6 3.6 %back_columns.2.refs_3_ = bf16[448,8192]{1,0:T(8,128)(2,1)} custom-call(bf16[448,512]{1,0:T(8,128)(2,1)S(1)} %copy-done.3, bf16[448,8192]{1,0:T(8,128)(2,1)S(1)} %copy-done, bf16[8192,512]{1,0:T(8,128)(2,1)S(1)} %bitcast.1), custom_call_target="tpu_custom_call" | custom-call | flops 17179869184 | bytes 67108864 | tf_op jit(solution)/shard_map/back_columns/pallas_call | solution.py:168
  29.2 1.3 %terms.13.g0 = bf16[2048,256]{1,0:T(8,128)(2,1)S(1)} custom-call(s32[32]{0:T(128)S(1)} %fusion.3.refs_0_.block, bf16[512,448]{1,0:T(8,128)(2,1)S(1)} %get-tuple-element.59.refs_1_, bf16[448,8192]{1,0:T(8,128)(2,1)S(1)} %copy-done, bf16[2048,256]{1,0:T(8,128)(2,1)S(1)} %collective-permute-done.5.refs_3_), custom_call_target="tpu_custom_call" | custom-call | flops 1048576 | bytes 65536 | tf_op jit(solution)/shard_map/terms/pallas_call | solution.py:137
  30.5 2.2 %collective-permute-done.8 = bf16[1024,256]{1,0:T(8,128)(2,1)S(1)} collective-permute-done((bf16[1024,256]{1,0:T(8,128)(2,1)S(1)}, bf16[1024,256]{1,0:T(8,128)(2,1)S(1)}, u32[]{:S(2)}, u32[]{:S(2)}) %collective-permute-start.8) | collective-permute-done | bytes 524320 | tf_op jit(solution)/shard_map/ppermute | solution.py:32
  33.2 2.3 %collective-permute-start.12 = (bf16[512,256]{1,0:T(8,128)(2,1)S(1)}, bf16[512,256]{1,0:T(8,128)(2,1)S(1)}, u32[]{:S(2)}, u32[]{:S(2)}) collective-permute-start(bf16[512,256]{1,0:T(8,128)(2,1)S(1)} %get-tuple-element.79), channel_id=1, source_target_pairs={{0,24},{4,100},{8,16},{12,108},{16,8},{20,116},{24,0},{28,124},{32... | collective-permute-start | bytes 786440 | tf_op jit(solution)/shard_map/ppermute | solution.py:36
  36.5 3.5 %back_columns.3 = bf16[448,8192]{1,0:T(8,128)(2,1)} custom-call(bf16[448,512]{1,0:T(8,128)(2,1)S(1)} %copy-done.3, bf16[448,8192]{1,0:T(8,128)(2,1)S(1)} %copy-done, bf16[8192,512]{1,0:T(8,128)(2,1)S(1)} %bitcast.1, bf16[448,8192]{1,0:T(8,128)(2,1)} %back_columns.2.refs_3_), custom_call_target="tpu_custom_call", output_to_operand_aliasing={{}: (3, {})} | custom-call | flops 17179869184 | bytes 67108864 | tf_op jit(solution)/shard_map/back_columns/pallas_call | solution.py:168
  40.0 2.4 %collective-permute-done.12.g5 = bf16[512,256]{1,0:T(8,128)(2,1)S(1)} collective-permute-done((bf16[512,256]{1,0:T(8,128)(2,1)S(1)}, bf16[512,256]{1,0:T(8,128)(2,1)S(1)}, u32[]{:S(2)}, u32[]{:S(2)}) %collective-permute-start.12) | collective-permute-done | bytes 262176 | tf_op jit(solution)/shard_map/ppermute | solution.py:36
  43.4 2.2 %update_rows.1 = (f32[256,512]{1,0:T(8,128)}, f32[256,512]{1,0:T(8,128)}, f32[256,512]{1,0:T(8,128)S(1)}, bf16[272,512]{1,0:T(8,128)(2,1)S(1)}) custom-call(s32[32]{0:T(128)S(1)} %fusion.3.refs_0_.block, bf16[2048,256]{1,0:T(8,128)(2,1)S(1)} %terms.13.g0, bf16[1024,256]{1,0:T(8,128)(2,1)S(1)} %collective-permute-done.6.g1, ...), custom_call_target="tpu_custom_call" | custom-call | flops 1048576 | bytes 65536 | tf_op jit(solution)/shard_map/update_rows/pallas_call | solution.py:226
  45.6 2.2 %collective-permute-start.15 = (bf16[272,512]{1,0:T(8,128)(2,1)S(1)}, bf16[272,512]{1,0:T(8,128)(2,1)S(1)}, u32[]{:S(2)}, u32[]{:S(2)}) collective-permute-start(bf16[272,512]{1,0:T(8,128)(2,1)S(1)} %get-tuple-element.62.refs_0_), channel_id=1, source_target_pairs={{0,24},{4,100},{8,16},{12,108},{16,8},{20,116},{24,0},{28,124},{32... | collective-permute-start | bytes 835592 | tf_op jit(solution)/shard_map/ppermute | solution.py:36
  48.8 6.6 %collective-permute-done.15.refs_3_ = bf16[272,512]{1,0:T(8,128)(2,1)S(1)} collective-permute-done((bf16[272,512]{1,0:T(8,128)(2,1)S(1)}, bf16[272,512]{1,0:T(8,128)(2,1)S(1)}, u32[]{:S(2)}, u32[]{:S(2)}) %collective-permute-start.15) | collective-permute-done | bytes 278560 | tf_op jit(solution)/shard_map/ppermute | solution.py:36
  56.0 2.5 %collective-permute-start.22 = (bf16[1024,512]{1,0:T(8,128)(2,1)S(1)}, bf16[1024,512]{1,0:T(8,128)(2,1)S(1)}, u32[]{:S(2)}, u32[]{:S(2)}) collective-permute-start(bf16[1024,512]{1,0:T(8,128)(2,1)S(1)} %get-tuple-element.68.refs_3_), channel_id=1, source_target_pairs={{0,96},{4,28},{8,104},{12,20},{16,112},{20,12},{24,120},{28,4},{32... | collective-permute-start | bytes 3145736 | tf_op jit(solution)/shard_map/ppermute | solution.py:32
  58.5 1.3 %collective-permute-start.16 = (f32[16,128]{1,0:T(8,128)S(1)}, f32[16,128]{1,0:T(8,128)S(1)}, u32[]{:S(2)}, u32[]{:S(2)}) collective-permute-start(f32[16,128]{1,0:T(8,128)S(1)} %get-tuple-element.63), channel_id=1, source_target_pairs={{0,1},{1,0},{2,3},{3,2},{4,5},{5,4},{6,7},{7,6},{8,9},{9,8},{10,11... | collective-permute-start | bytes 24584 | tf_op jit(solution)/shard_map/ppermute | solution.py:40
  61.0 2.7 %collective-permute-start.17 = (f32[16,128]{1,0:T(8,128)S(1)}, f32[16,128]{1,0:T(8,128)S(1)}, u32[]{:S(2)}, u32[]{:S(2)}) collective-permute-start(f32[16,128]{1,0:T(8,128)S(1)} %add.58), channel_id=1, source_target_pairs={{0,3},{1,2},{2,1},{3,0},{4,7},{5,6},{6,5},{7,4},{8,11},{9,10},{10,... | collective-permute-start | bytes 24584 | tf_op jit(solution)/shard_map/ppermute | solution.py:40
  63.7 1.3 %collective-permute-done.17 = f32[16,128]{1,0:T(8,128)S(1)} collective-permute-done((f32[16,128]{1,0:T(8,128)S(1)}, f32[16,128]{1,0:T(8,128)S(1)}, u32[]{:S(2)}, u32[]{:S(2)}) %collective-permute-start.17) | collective-permute-done | bytes 8224 | tf_op jit(solution)/shard_map/ppermute | solution.py:40
  65.3 3.0 %collective-permute-start.19 = (f32[16,128]{1,0:T(8,128)S(1)}, f32[16,128]{1,0:T(8,128)S(1)}, u32[]{:S(2)}, u32[]{:S(2)}) collective-permute-start(f32[16,128]{1,0:T(8,128)S(1)} %add.59), channel_id=1, source_target_pairs={{0,64},{4,20},{8,72},{12,28},{16,80},{20,4},{24,88},{28,12},{32,96... | collective-permute-start | bytes 24584 | tf_op jit(solution)/shard_map/ppermute | solution.py:32
  68.3 3.0 %collective-permute-done.20 = f32[16,128]{1,0:T(8,128)S(1)} collective-permute-done((f32[16,128]{1,0:T(8,128)S(1)}, f32[16,128]{1,0:T(8,128)S(1)}, u32[]{:S(2)}, u32[]{:S(2)}) %collective-permute-start.20) | collective-permute-done | bytes 8224 | tf_op jit(solution)/shard_map/ppermute | solution.py:32
  71.3 2.0 %collective-permute-done.19 = f32[16,128]{1,0:T(8,128)S(1)} collective-permute-done((f32[16,128]{1,0:T(8,128)S(1)}, f32[16,128]{1,0:T(8,128)S(1)}, u32[]{:S(2)}, u32[]{:S(2)}) %collective-permute-start.19) | collective-permute-done | bytes 8224 | tf_op jit(solution)/shard_map/ppermute | solution.py:32
  73.5 4.7 %collective-permute-start.23 = (bf16[1024,512]{1,0:T(8,128)(2,1)S(1)}, bf16[1024,512]{1,0:T(8,128)(2,1)S(1)}, u32[]{:S(2)}, u32[]{:S(2)}) collective-permute-start(bf16[1024,512]{1,0:T(8,128)(2,1)S(1)} %get-tuple-element.68.refs_3_), channel_id=1, source_target_pairs={{0,4},{4,0},{1,5},{5,1},{2,6},{6,2},{3,7},{7,3},{8,12},{12,8},{9,1... | collective-permute-start | bytes 3145736 | tf_op jit(solution)/shard_map/ppermute | solution.py:44
  79.4 3.3 %collective-permute-start.25 = (bf16[512,512]{1,0:T(8,128)(2,1)S(1)}, bf16[512,512]{1,0:T(8,128)(2,1)S(1)}, u32[]{:S(2)}, u32[]{:S(2)}) collective-permute-start(bf16[512,512]{1,0:T(8,128)(2,1)S(1)} %taken.2), channel_id=1, source_target_pairs={{0,96},{4,28},{8,104},{12,20},{16,112},{20,12},{24,120},{28,4},{32... | collective-permute-start | bytes 1572872 | tf_op jit(solution)/shard_map/ppermute | solution.py:32
  83.9 4.3 %apply_update.3 = (bf16[8192,512]{1,0:T(8,128)(2,1)}, f32[256,512]{1,0:T(8,128)}) custom-call(s32[32]{0:T(128)S(1)} %fusion.3.refs_0_.block, f32[16,128]{1,0:T(8,128)S(1)} %add.63.refs_1_, bf16[8192,512]{1,0:T(8,128)(2,1)S(1)} %bitcast.1, bf16[1024,512]{1,0:T(8,128)(2,1)S(1)} %get-tuple-element.68.refs_3_, ...), custom_call_target="tpu_custom_call" | custom-call | flops 1048576 | bytes 65536 | tf_op jit(solution)/shard_map/apply_update/pallas_call | solution.py:277
  88.2 1.3 %collective-permute-done.25.refs_3_ = bf16[512,512]{1,0:T(8,128)(2,1)S(1)} collective-permute-done((bf16[512,512]{1,0:T(8,128)(2,1)S(1)}, bf16[512,512]{1,0:T(8,128)(2,1)S(1)}, u32[]{:S(2)}, u32[]{:S(2)}) %collective-permute-start.25) | collective-permute-done | bytes 524320 | tf_op jit(solution)/shard_map/ppermute | solution.py:32
  90.0 1.7 %apply_update.4.refs_5_ = bf16[8192,512]{1,0:T(8,128)(2,1)} custom-call(s32[32]{0:T(128)S(1)} %fusion.3.refs_0_.block, f32[16,128]{1,0:T(8,128)S(1)} %add.63.refs_1_, bf16[8192,512]{1,0:T(8,128)(2,1)S(1)} %bitcast.1, bf16[512,512]{1,0:T(8,128)(2,1)S(1)} %collective-permute-done.25.refs_3_, ...), custom_call_target="tpu_custom_call", output_to_operand_aliasing={{}: (5, {})} | custom-call | flops 1048576 | bytes 65536 | tf_op jit(solution)/shard_map/apply_update/pallas_call | solution.py:277
  92.2 1.7 %apply_update.5 = bf16[8192,512]{1,0:T(8,128)(2,1)} custom-call(s32[32]{0:T(128)S(1)} %fusion.3.refs_0_.block, f32[16,128]{1,0:T(8,128)S(1)} %add.63.refs_1_, bf16[8192,512]{1,0:T(8,128)(2,1)S(1)} %bitcast.1, bf16[512,512]{1,0:T(8,128)(2,1)S(1)} %collective-permute-done.28.refs_3_, ...), custom_call_target="tpu_custom_call", output_to_operand_aliasing={{}: (5, {})} | custom-call | flops 1048576 | bytes 65536 | tf_op jit(solution)/shard_map/apply_update/pallas_call | solution.py:277
  (67 shorter events, 14.3 us)
Async XLA Ops:
  4.8 4.1 %collective-permute-start = (bf16[2048,256]{1,0:T(8,128)(2,1)S(1)}, bf16[2048,256]{1,0:T(8,128)(2,1)S(1)}, u32[]{:S(2)}, u32[]{:S(2)}) collective-permute-start(bf16[2048,256]{1,0:T(8,128)(2,1)S(1)} %get-tuple-element.43), channel_id=1, source_target_pairs={{0,4},{4,0},{1,5},{5,1},{2,6},{6,2},{3,7},{7,3},{8,12},{12,8},{9,1... | collective-permute-start | bytes 3145736 | tf_op jit(solution)/shard_map/ppermute | solution.py:44
  8.8 5.6 %collective-permute-start.1 = (bf16[2048,256]{1,0:T(8,128)(2,1)S(1)}, bf16[2048,256]{1,0:T(8,128)(2,1)S(1)}, u32[]{:S(2)}, u32[]{:S(2)}) collective-permute-start(bf16[2048,256]{1,0:T(8,128)(2,1)S(1)} %terms.8), channel_id=1, source_target_pairs={{0,4},{4,0},{1,5},{5,1},{2,6},{6,2},{3,7},{7,3},{8,12},{12,8},{9,1... | collective-permute-start | bytes 3145736 | tf_op jit(solution)/shard_map/ppermute | solution.py:44
  9.2 10.6 %collective-permute-start.3 = (bf16[1024,256]{1,0:T(8,128)(2,1)S(1)}, bf16[1024,256]{1,0:T(8,128)(2,1)S(1)}, u32[]{:S(2)}, u32[]{:S(2)}) collective-permute-start(bf16[1024,256]{1,0:T(8,128)(2,1)S(1)} %get-tuple-element.82), channel_id=1, source_target_pairs={{0,96},{4,28},{8,104},{12,20},{16,112},{20,12},{24,120},{28,4},{32... | collective-permute-start | bytes 1572872 | tf_op jit(solution)/shard_map/ppermute | solution.py:32
  13.1 8.3 %collective-permute-start.4 = (bf16[1024,256]{1,0:T(8,128)(2,1)S(1)}, bf16[1024,256]{1,0:T(8,128)(2,1)S(1)}, u32[]{:S(2)}, u32[]{:S(2)}) collective-permute-start(bf16[1024,256]{1,0:T(8,128)(2,1)S(1)} %get-tuple-element.83), channel_id=1, source_target_pairs={{0,32},{4,12},{8,40},{12,4},{16,48},{20,28},{24,56},{28,20},{32,0}... | collective-permute-start | bytes 1572872 | tf_op jit(solution)/shard_map/ppermute | solution.py:32
  15.7 14.8 %collective-permute-start.6 = (bf16[1024,256]{1,0:T(8,128)(2,1)S(1)}, bf16[1024,256]{1,0:T(8,128)(2,1)S(1)}, u32[]{:S(2)}, u32[]{:S(2)}) collective-permute-start(bf16[1024,256]{1,0:T(8,128)(2,1)S(1)} %get-tuple-element.52), channel_id=1, source_target_pairs={{0,32},{4,12},{8,40},{12,4},{16,48},{20,28},{24,56},{28,20},{32,0}... | collective-permute-start | bytes 1572872 | tf_op jit(solution)/shard_map/ppermute | solution.py:32
  17.2 8.4 %slice-start.1 = ((s8[8388608]{0:T(1024)(128)(4,1)}), s8[4194304]{0:T(1024)(128)(4,1)S(1)}, s32[]{:S(2)}) async-start(s8[8388608]{0:T(1024)(128)(4,1)} %bitcast), calls=%async_computation.1 | async-start | bytes 8388608
  17.2 13.2 %collective-permute-start.9 = (bf16[1024,256]{1,0:T(8,128)(2,1)S(1)}, bf16[1024,256]{1,0:T(8,128)(2,1)S(1)}, u32[]{:S(2)}, u32[]{:S(2)}) collective-permute-start(bf16[1024,256]{1,0:T(8,128)(2,1)S(1)} %get-tuple-element.53), channel_id=1, source_target_pairs={{0,96},{4,28},{8,104},{12,20},{16,112},{20,12},{24,120},{28,4},{32... | collective-permute-start | bytes 1572872 | tf_op jit(solution)/shard_map/ppermute | solution.py:32
  17.3 4.1 %collective-permute-start.2 = (bf16[2048,256]{1,0:T(8,128)(2,1)S(1)}, bf16[2048,256]{1,0:T(8,128)(2,1)S(1)}, u32[]{:S(2)}, u32[]{:S(2)}) collective-permute-start(bf16[2048,256]{1,0:T(8,128)(2,1)S(1)} %terms.9), channel_id=1, source_target_pairs={{0,4},{4,0},{1,5},{5,1},{2,6},{6,2},{3,7},{7,3},{8,12},{12,8},{9,1... | collective-permute-start | bytes 3145736 | tf_op jit(solution)/shard_map/ppermute | solution.py:44
  19.7 9.4 %collective-permute-start.5 = (bf16[2048,256]{1,0:T(8,128)(2,1)S(1)}, bf16[2048,256]{1,0:T(8,128)(2,1)S(1)}, u32[]{:S(2)}, u32[]{:S(2)}) collective-permute-start(bf16[2048,256]{1,0:T(8,128)(2,1)S(1)} %terms.11), channel_id=1, source_target_pairs={{0,4},{4,0},{1,5},{5,1},{2,6},{6,2},{3,7},{7,3},{8,12},{12,8},{9,1... | collective-permute-start | bytes 3145736 | tf_op jit(solution)/shard_map/ppermute | solution.py:44
  22.8 9.9 %collective-permute-start.8 = (bf16[1024,256]{1,0:T(8,128)(2,1)S(1)}, bf16[1024,256]{1,0:T(8,128)(2,1)S(1)}, u32[]{:S(2)}, u32[]{:S(2)}) collective-permute-start(bf16[1024,256]{1,0:T(8,128)(2,1)S(1)} %get-tuple-element.56), channel_id=1, source_target_pairs={{0,32},{4,12},{8,40},{12,4},{16,48},{20,28},{24,56},{28,20},{32,0}... | collective-permute-start | bytes 1572872 | tf_op jit(solution)/shard_map/ppermute | solution.py:32
  23.3 9.5 %collective-permute-start.7 = (bf16[1024,256]{1,0:T(8,128)(2,1)S(1)}, bf16[1024,256]{1,0:T(8,128)(2,1)S(1)}, u32[]{:S(2)}, u32[]{:S(2)}) collective-permute-start(bf16[1024,256]{1,0:T(8,128)(2,1)S(1)} %get-tuple-element.57), channel_id=1, source_target_pairs={{0,96},{4,28},{8,104},{12,20},{16,112},{20,12},{24,120},{28,4},{32... | collective-permute-start | bytes 1572872 | tf_op jit(solution)/shard_map/ppermute | solution.py:32
  33.2 9.3 %collective-permute-start.12 = (bf16[512,256]{1,0:T(8,128)(2,1)S(1)}, bf16[512,256]{1,0:T(8,128)(2,1)S(1)}, u32[]{:S(2)}, u32[]{:S(2)}) collective-permute-start(bf16[512,256]{1,0:T(8,128)(2,1)S(1)} %get-tuple-element.79), channel_id=1, source_target_pairs={{0,24},{4,100},{8,16},{12,108},{16,8},{20,116},{24,0},{28,124},{32... | collective-permute-start | bytes 786440 | tf_op jit(solution)/shard_map/ppermute | solution.py:36
  35.4 7.1 %collective-permute-start.11 = (bf16[512,256]{1,0:T(8,128)(2,1)S(1)}, bf16[512,256]{1,0:T(8,128)(2,1)S(1)}, u32[]{:S(2)}, u32[]{:S(2)}) collective-permute-start(bf16[512,256]{1,0:T(8,128)(2,1)S(1)} %get-tuple-element.80), channel_id=1, source_target_pairs={{0,16},{4,68},{8,24},{12,76},{16,0},{20,84},{24,8},{28,92},{32,48}... | collective-permute-start | bytes 786440 | tf_op jit(solution)/shard_map/ppermute | solution.py:36
  35.9 7.5 %collective-permute-start.10 = (bf16[512,256]{1,0:T(8,128)(2,1)S(1)}, bf16[512,256]{1,0:T(8,128)(2,1)S(1)}, u32[]{:S(2)}, u32[]{:S(2)}) collective-permute-start(bf16[512,256]{1,0:T(8,128)(2,1)S(1)} %get-tuple-element.81), channel_id=1, source_target_pairs={{0,8},{4,36},{8,0},{12,44},{16,24},{20,52},{24,16},{28,60},{32,40}... | collective-permute-start | bytes 786440 | tf_op jit(solution)/shard_map/ppermute | solution.py:36
  45.6 9.9 %collective-permute-start.15 = (bf16[272,512]{1,0:T(8,128)(2,1)S(1)}, bf16[272,512]{1,0:T(8,128)(2,1)S(1)}, u32[]{:S(2)}, u32[]{:S(2)}) collective-permute-start(bf16[272,512]{1,0:T(8,128)(2,1)S(1)} %get-tuple-element.62.refs_0_), channel_id=1, source_target_pairs={{0,24},{4,100},{8,16},{12,108},{16,8},{20,116},{24,0},{28,124},{32... | collective-permute-start | bytes 835592 | tf_op jit(solution)/shard_map/ppermute | solution.py:36
  47.8 7.7 %collective-permute-start.14 = (bf16[272,512]{1,0:T(8,128)(2,1)S(1)}, bf16[272,512]{1,0:T(8,128)(2,1)S(1)}, u32[]{:S(2)}, u32[]{:S(2)}) collective-permute-start(bf16[272,512]{1,0:T(8,128)(2,1)S(1)} %get-tuple-element.62.refs_0_), channel_id=1, source_target_pairs={{0,16},{4,68},{8,24},{12,76},{16,0},{20,84},{24,8},{28,92},{32,48}... | collective-permute-start | bytes 835592 | tf_op jit(solution)/shard_map/ppermute | solution.py:36
  48.3 7.7 %collective-permute-start.13 = (bf16[272,512]{1,0:T(8,128)(2,1)S(1)}, bf16[272,512]{1,0:T(8,128)(2,1)S(1)}, u32[]{:S(2)}, u32[]{:S(2)}) collective-permute-start(bf16[272,512]{1,0:T(8,128)(2,1)S(1)} %get-tuple-element.62.refs_0_), channel_id=1, source_target_pairs={{0,8},{4,36},{8,0},{12,44},{16,24},{20,52},{24,16},{28,60},{32,40}... | collective-permute-start | bytes 835592 | tf_op jit(solution)/shard_map/ppermute | solution.py:36
  56.0 17.3 %collective-permute-start.22 = (bf16[1024,512]{1,0:T(8,128)(2,1)S(1)}, bf16[1024,512]{1,0:T(8,128)(2,1)S(1)}, u32[]{:S(2)}, u32[]{:S(2)}) collective-permute-start(bf16[1024,512]{1,0:T(8,128)(2,1)S(1)} %get-tuple-element.68.refs_3_), channel_id=1, source_target_pairs={{0,96},{4,28},{8,104},{12,20},{16,112},{20,12},{24,120},{28,4},{32... | collective-permute-start | bytes 3145736 | tf_op jit(solution)/shard_map/ppermute | solution.py:32
  58.5 14.9 %collective-permute-start.21 = (bf16[1024,512]{1,0:T(8,128)(2,1)S(1)}, bf16[1024,512]{1,0:T(8,128)(2,1)S(1)}, u32[]{:S(2)}, u32[]{:S(2)}) collective-permute-start(bf16[1024,512]{1,0:T(8,128)(2,1)S(1)} %get-tuple-element.68.refs_3_), channel_id=1, source_target_pairs={{0,32},{4,12},{8,40},{12,4},{16,48},{20,28},{24,56},{28,20},{32,0}... | collective-permute-start | bytes 3145736 | tf_op jit(solution)/shard_map/ppermute | solution.py:32
  58.5 2.5 %collective-permute-start.16 = (f32[16,128]{1,0:T(8,128)S(1)}, f32[16,128]{1,0:T(8,128)S(1)}, u32[]{:S(2)}, u32[]{:S(2)}) collective-permute-start(f32[16,128]{1,0:T(8,128)S(1)} %get-tuple-element.63), channel_id=1, source_target_pairs={{0,1},{1,0},{2,3},{3,2},{4,5},{5,4},{6,7},{7,6},{8,9},{9,8},{10,11... | collective-permute-start | bytes 24584 | tf_op jit(solution)/shard_map/ppermute | solution.py:40
  61.0 4.1 %collective-permute-start.17 = (f32[16,128]{1,0:T(8,128)S(1)}, f32[16,128]{1,0:T(8,128)S(1)}, u32[]{:S(2)}, u32[]{:S(2)}) collective-permute-start(f32[16,128]{1,0:T(8,128)S(1)} %add.58), channel_id=1, source_target_pairs={{0,3},{1,2},{2,1},{3,0},{4,7},{5,6},{6,5},{7,4},{8,11},{9,10},{10,... | collective-permute-start | bytes 24584 | tf_op jit(solution)/shard_map/ppermute | solution.py:40
  65.1 6.3 %collective-permute-start.20 = (f32[16,128]{1,0:T(8,128)S(1)}, f32[16,128]{1,0:T(8,128)S(1)}, u32[]{:S(2)}, u32[]{:S(2)}) collective-permute-start(f32[16,128]{1,0:T(8,128)S(1)} %add.59), channel_id=1, source_target_pairs={{0,96},{4,28},{8,104},{12,20},{16,112},{20,12},{24,120},{28,4},{32... | collective-permute-start | bytes 24584 | tf_op jit(solution)/shard_map/ppermute | solution.py:32
  65.3 8.0 %collective-permute-start.19 = (f32[16,128]{1,0:T(8,128)S(1)}, f32[16,128]{1,0:T(8,128)S(1)}, u32[]{:S(2)}, u32[]{:S(2)}) collective-permute-start(f32[16,128]{1,0:T(8,128)S(1)} %add.59), channel_id=1, source_target_pairs={{0,64},{4,20},{8,72},{12,28},{16,80},{20,4},{24,88},{28,12},{32,96... | collective-permute-start | bytes 24584 | tf_op jit(solution)/shard_map/ppermute | solution.py:32
  68.3 5.0 %collective-permute-start.18 = (f32[16,128]{1,0:T(8,128)S(1)}, f32[16,128]{1,0:T(8,128)S(1)}, u32[]{:S(2)}, u32[]{:S(2)}) collective-permute-start(f32[16,128]{1,0:T(8,128)S(1)} %add.59), channel_id=1, source_target_pairs={{0,32},{4,12},{8,40},{12,4},{16,48},{20,28},{24,56},{28,20},{32,0}... | collective-permute-start | bytes 24584 | tf_op jit(solution)/shard_map/ppermute | solution.py:32
  73.5 9.2 %collective-permute-start.23 = (bf16[1024,512]{1,0:T(8,128)(2,1)S(1)}, bf16[1024,512]{1,0:T(8,128)(2,1)S(1)}, u32[]{:S(2)}, u32[]{:S(2)}) collective-permute-start(bf16[1024,512]{1,0:T(8,128)(2,1)S(1)} %get-tuple-element.68.refs_3_), channel_id=1, source_target_pairs={{0,4},{4,0},{1,5},{5,1},{2,6},{6,2},{3,7},{7,3},{8,12},{12,8},{9,1... | collective-permute-start | bytes 3145736 | tf_op jit(solution)/shard_map/ppermute | solution.py:44
  78.1 5.7 %collective-permute-start.26 = (bf16[1024,512]{1,0:T(8,128)(2,1)S(1)}, bf16[1024,512]{1,0:T(8,128)(2,1)S(1)}, u32[]{:S(2)}, u32[]{:S(2)}) collective-permute-start(bf16[1024,512]{1,0:T(8,128)(2,1)S(1)} %collective-permute-done.21.ref.refs_4_), channel_id=1, source_target_pairs={{0,4},{4,0},{1,5},{5,1},{2,6},{6,2},{3,7},{7,3},{8,12},{12,8},{9,1... | collective-permute-start | bytes 3145736 | tf_op jit(solution)/shard_map/ppermute | solution.py:44
  78.2 5.7 %collective-permute-start.27 = (bf16[1024,512]{1,0:T(8,128)(2,1)S(1)}, bf16[1024,512]{1,0:T(8,128)(2,1)S(1)}, u32[]{:S(2)}, u32[]{:S(2)}) collective-permute-start(bf16[1024,512]{1,0:T(8,128)(2,1)S(1)} %collective-permute-done.22.ref.refs_5_), channel_id=1, source_target_pairs={{0,4},{4,0},{1,5},{5,1},{2,6},{6,2},{3,7},{7,3},{8,12},{12,8},{9,1... | collective-permute-start | bytes 3145736 | tf_op jit(solution)/shard_map/ppermute | solution.py:44
  78.6 9.6 %collective-permute-start.29 = (bf16[512,512]{1,0:T(8,128)(2,1)S(1)}, bf16[512,512]{1,0:T(8,128)(2,1)S(1)}, u32[]{:S(2)}, u32[]{:S(2)}) collective-permute-start(bf16[512,512]{1,0:T(8,128)(2,1)S(1)} %taken.3), channel_id=1, source_target_pairs={{0,32},{4,12},{8,40},{12,4},{16,48},{20,28},{24,56},{28,20},{32,0}... | collective-permute-start | bytes 1572872 | tf_op jit(solution)/shard_map/ppermute | solution.py:32
  79.4 10.1 %collective-permute-start.25 = (bf16[512,512]{1,0:T(8,128)(2,1)S(1)}, bf16[512,512]{1,0:T(8,128)(2,1)S(1)}, u32[]{:S(2)}, u32[]{:S(2)}) collective-permute-start(bf16[512,512]{1,0:T(8,128)(2,1)S(1)} %taken.2), channel_id=1, source_target_pairs={{0,96},{4,28},{8,104},{12,20},{16,112},{20,12},{24,120},{28,4},{32... | collective-permute-start | bytes 1572872 | tf_op jit(solution)/shard_map/ppermute | solution.py:32
  82.7 1.2 %collective-permute-start.24 = (f32[16,128]{1,0:T(8,128)S(1)}, f32[16,128]{1,0:T(8,128)S(1)}, u32[]{:S(2)}, u32[]{:S(2)}) collective-permute-start(f32[16,128]{1,0:T(8,128)S(1)} %add_add_fusion), channel_id=1, source_target_pairs={{0,4},{4,0},{1,5},{5,1},{2,6},{6,2},{3,7},{7,3},{8,12},{12,8},{9,1... | collective-permute-start | bytes 24584 | tf_op jit(solution)/shard_map/ppermute | solution.py:44
  89.5 2.2 %collective-permute-start.28 = (bf16[512,512]{1,0:T(8,128)(2,1)S(1)}, bf16[512,512]{1,0:T(8,128)(2,1)S(1)}, u32[]{:S(2)}, u32[]{:S(2)}) collective-permute-start(bf16[512,512]{1,0:T(8,128)(2,1)S(1)} %collective-permute-done.25.refs_3_), channel_id=1, source_target_pairs={{0,4},{4,0},{1,5},{5,1},{2,6},{6,2},{3,7},{7,3},{8,12},{12,8},{9,1... | collective-permute-start | bytes 1572872 | tf_op jit(solution)/shard_map/ppermute | solution.py:44
  89.9 2.3 %collective-permute-start.30 = (bf16[512,512]{1,0:T(8,128)(2,1)S(1)}, bf16[512,512]{1,0:T(8,128)(2,1)S(1)}, u32[]{:S(2)}, u32[]{:S(2)}) collective-permute-start(bf16[512,512]{1,0:T(8,128)(2,1)S(1)} %collective-permute-done.29.refs_4_), channel_id=1, source_target_pairs={{0,4},{4,0},{1,5},{5,1},{2,6},{6,2},{3,7},{7,3},{8,12},{12,8},{9,1... | collective-permute-start | bytes 1572872 | tf_op jit(solution)/shard_map/ppermute | solution.py:44
  (5 other events, 35.5 us)

commit v6 on v4

--- a/solution.py
+++ b/solution.py
@@ -212,13 +212,12 @@
         weight_sq = weight_sq + jnp.sum(
             (own_weight * own_weight).reshape(ROWS // 8, 8, 128), axis=0
         )
-    for k, norm in enumerate((update_sq, weight_sq)):
-        lines = slice(ROWS + 8 * k, ROWS + 8 * k + 8)
-        for j in range(3):
-            piece = norm.astype(jnp.bfloat16)
-            short_out[lines, j * 128 : (j + 1) * 128] = piece
-            norm = norm - piece.astype(jnp.float32)
-        short_out[lines, 384:512] = jnp.zeros((8, 128), jnp.bfloat16)
+    norms = jnp.concatenate([update_sq, weight_sq])
+    for j in range(3):
+        piece = norms.astype(jnp.bfloat16)
+        short_out[ROWS : ROWS + 16, j * 128 : (j + 1) * 128] = piece
+        norms = norms - piece.astype(jnp.float32)
+    short_out[ROWS : ROWS + 16, 384:512] = jnp.zeros((16, 128), jnp.bfloat16)
 
 
 def update_rows(block, parts, first, second, weight):

time: 94.5 us -> 94.5 us (level)
  no operation moved by 1% of the time
where the time goes in v6:
time: 94.5 us; the launch traced here: 94.4 us
  starting transfers between devices  36.7 us (39%)
  Pallas kernels  28.9 us (31%)
  waiting for transfers between devices  27.2 us (29%)
  between operations  1.02 us (1%)
    ppermute x13, starting transfers between devices, along_first(): return lax.ppermute(value, DP, exchanges('first', k))  18.1 us
    ppermute x13, waiting for transfers between devices, along_first(): return lax.ppermute(value, DP, exchanges('first', k))  10.8 us
    ppermute x6, waiting for transfers between devices, along_second(): return lax.ppermute(value, DP, exchanges('second', k))  10.5 us
    pallas_call x7, Pallas kernels, terms(): pl.pallas_call(body, out_shape=tuple((jax.ShapeDtypeStruct((p * D, ROWS),...  8.95 us
    ppermute x10, starting transfers between devices, sibling(): return lax.ppermute(value, 'c', [(0, 1), (1, 0)])  8.04 us
    pallas_call x2, Pallas kernels, back_columns(): pl.pallas_call(body, out_shape=jax.ShapeDtypeStruct(preactivation.shape,...  7.12 us
    ppermute x6, starting transfers between devices, along_second(): return lax.ppermute(value, DP, exchanges('second', k))  6.59 us
    pallas_call x2, Pallas kernels, apply_update(): pl.pallas_call(body, out_shape=(jax.ShapeDtypeStruct(weight.shape, jnp.bf...  6.4 us
  transfers between devices with their start and end apart: 31, of which 16 were waited for; matrix products, arithmetic and copies ran while one was open for 0% of the time, Pallas kernels for 22%

profile of v6, /device:TPU:1, one launch (start us, length us, event | category | flops | bytes accessed | tf_op | source)
XLA Modules:
  0.0 94.4 jit_solution(14116072615298889139)
XLA Ops:
  0.7 4.1 %first_terms.1 = (bf16[2048,256]{1,0:T(8,128)(2,1)S(1)}, bf16[512,448]{1,0:T(8,128)(2,1)S(1)}) custom-call(s32[32]{0:T(128)S(1)} %fusion.3.refs_0_.block, bf16[448,512]{1,0:T(8,128)(2,1)} %refs_0_.1, bf16[448,8192]{1,0:T(8,128)(2,1)} %refs_1_.5), custom_call_target="tpu_custom_call" | custom-call | flops 17179869184 | bytes 67108864 | tf_op jit(solution)/shard_map/first_terms/pallas_call | solution.py:91
  4.8 1.5 %collective-permute-start = (bf16[2048,256]{1,0:T(8,128)(2,1)S(1)}, bf16[2048,256]{1,0:T(8,128)(2,1)S(1)}, u32[]{:S(2)}, u32[]{:S(2)}) collective-permute-start(bf16[2048,256]{1,0:T(8,128)(2,1)S(1)} %get-tuple-element.43), channel_id=1, source_target_pairs={{0,4},{4,0},{1,5},{5,1},{2,6},{6,2},{3,7},{7,3},{8,12},{12,8},{9,1... | collective-permute-start | bytes 3145736 | tf_op jit(solution)/shard_map/ppermute | solution.py:44
  6.3 1.3 %terms.7 = (bf16[1024,256]{1,0:T(8,128)(2,1)S(1)}, bf16[1024,256]{1,0:T(8,128)(2,1)S(1)}) custom-call(s32[32]{0:T(128)S(1)} %fusion.3.refs_0_.block, bf16[512,448]{1,0:T(8,128)(2,1)S(1)} %get-tuple-element.59.refs_1_, bf16[448,8192]{1,0:T(8,128)(2,1)S(1)} %copy-done), custom_call_target="tpu_custom_call" | custom-call | flops 17179869184 | bytes 67108864 | tf_op jit(solution)/shard_map/terms/pallas_call | solution.py:137
  7.6 1.3 %terms.8 = bf16[2048,256]{1,0:T(8,128)(2,1)S(1)} custom-call(s32[32]{0:T(128)S(1)} %fusion.3.refs_0_.block, bf16[512,448]{1,0:T(8,128)(2,1)S(1)} %get-tuple-element.59.refs_1_, bf16[448,8192]{1,0:T(8,128)(2,1)S(1)} %copy-done), custom_call_target="tpu_custom_call" | custom-call | flops 1048576 | bytes 65536 | tf_op jit(solution)/shard_map/terms/pallas_call | solution.py:137
  9.2 3.9 %collective-permute-start.3 = (bf16[1024,256]{1,0:T(8,128)(2,1)S(1)}, bf16[1024,256]{1,0:T(8,128)(2,1)S(1)}, u32[]{:S(2)}, u32[]{:S(2)}) collective-permute-start(bf16[1024,256]{1,0:T(8,128)(2,1)S(1)} %get-tuple-element.82), channel_id=1, source_target_pairs={{0,96},{4,28},{8,104},{12,20},{16,112},{20,12},{24,120},{28,4},{32... | collective-permute-start | bytes 1572872 | tf_op jit(solution)/shard_map/ppermute | solution.py:32
  13.1 1.3 %terms.9 = bf16[2048,256]{1,0:T(8,128)(2,1)S(1)} custom-call(s32[32]{0:T(128)S(1)} %fusion.3.refs_0_.block, bf16[512,448]{1,0:T(8,128)(2,1)S(1)} %get-tuple-element.59.refs_1_, bf16[448,8192]{1,0:T(8,128)(2,1)S(1)} %copy-done), custom_call_target="tpu_custom_call" | custom-call | flops 17179869184 | bytes 67108864 | tf_op jit(solution)/shard_map/terms/pallas_call | solution.py:137
  14.4 1.3 %terms.10 = (bf16[1024,256]{1,0:T(8,128)(2,1)S(1)}, bf16[1024,256]{1,0:T(8,128)(2,1)S(1)}) custom-call(s32[32]{0:T(128)S(1)} %fusion.3.refs_0_.block, bf16[512,448]{1,0:T(8,128)(2,1)S(1)} %get-tuple-element.59.refs_1_, bf16[448,8192]{1,0:T(8,128)(2,1)S(1)} %copy-done, bf16[2048,256]{1,0:T(8,128)(2,1)S(1)} %collective-permute-done.1.refs_3_.refs_4_, ...), custom_call_target="tpu_custom_call" | custom-call | flops 1048576 | bytes 65536 | tf_op jit(solution)/shard_map/terms/pallas_call | solution.py:137
  15.7 1.5 %collective-permute-start.6 = (bf16[1024,256]{1,0:T(8,128)(2,1)S(1)}, bf16[1024,256]{1,0:T(8,128)(2,1)S(1)}, u32[]{:S(2)}, u32[]{:S(2)}) collective-permute-start(bf16[1024,256]{1,0:T(8,128)(2,1)S(1)} %get-tuple-element.52), channel_id=1, source_target_pairs={{0,32},{4,12},{8,40},{12,4},{16,48},{20,28},{24,56},{28,20},{32,0}... | collective-permute-start | bytes 1572872 | tf_op jit(solution)/shard_map/ppermute | solution.py:32
  20.2 1.3 %collective-permute-done.4.refs_6_ = bf16[1024,256]{1,0:T(8,128)(2,1)S(1)} collective-permute-done((bf16[1024,256]{1,0:T(8,128)(2,1)S(1)}, bf16[1024,256]{1,0:T(8,128)(2,1)S(1)}, u32[]{:S(2)}, u32[]{:S(2)}) %collective-permute-start.4) | collective-permute-done | bytes 524320 | tf_op jit(solution)/shard_map/ppermute | solution.py:32
  21.5 1.4 %terms.12 = (bf16[1024,256]{1,0:T(8,128)(2,1)S(1)}, bf16[1024,256]{1,0:T(8,128)(2,1)S(1)}) custom-call(s32[32]{0:T(128)S(1)} %fusion.3.refs_0_.block, bf16[512,448]{1,0:T(8,128)(2,1)S(1)} %get-tuple-element.59.refs_1_, bf16[448,8192]{1,0:T(8,128)(2,1)S(1)} %copy-done, bf16[2048,256]{1,0:T(8,128)(2,1)S(1)} %collective-permute-done.2.refs_3_.refs_5_, ...), custom_call_target="tpu_custom_call" | custom-call | flops 1048576 | bytes 65536 | tf_op jit(solution)/shard_map/terms/pallas_call | solution.py:137
  23.3 2.2 %collective-permute-start.7 = (bf16[1024,256]{1,0:T(8,128)(2,1)S(1)}, bf16[1024,256]{1,0:T(8,128)(2,1)S(1)}, u32[]{:S(2)}, u32[]{:S(2)}) collective-permute-start(bf16[1024,256]{1,0:T(8,128)(2,1)S(1)} %get-tuple-element.57), channel_id=1, source_target_pairs={{0,96},{4,28},{8,104},{12,20},{16,112},{20,12},{24,120},{28,4},{32... | collective-permute-start | bytes 1572872 | tf_op jit(solution)/shard_map/ppermute | solution.py:32
  25.6 3.6 %back_columns.2.refs_3_ = bf16[448,8192]{1,0:T(8,128)(2,1)} custom-call(bf16[448,512]{1,0:T(8,128)(2,1)S(1)} %copy-done.3, bf16[448,8192]{1,0:T(8,128)(2,1)S(1)} %copy-done, bf16[8192,512]{1,0:T(8,128)(2,1)S(1)} %bitcast.1), custom_call_target="tpu_custom_call" | custom-call | flops 17179869184 | bytes 67108864 | tf_op jit(solution)/shard_map/back_columns/pallas_call | solution.py:168
  29.2 1.3 %terms.13.g0 = bf16[2048,256]{1,0:T(8,128)(2,1)S(1)} custom-call(s32[32]{0:T(128)S(1)} %fusion.3.refs_0_.block, bf16[512,448]{1,0:T(8,128)(2,1)S(1)} %get-tuple-element.59.refs_1_, bf16[448,8192]{1,0:T(8,128)(2,1)S(1)} %copy-done, bf16[2048,256]{1,0:T(8,128)(2,1)S(1)} %collective-permute-done.5.refs_3_), custom_call_target="tpu_custom_call" | custom-call | flops 1048576 | bytes 65536 | tf_op jit(solution)/shard_map/terms/pallas_call | solution.py:137
  30.5 2.2 %collective-permute-done.8 = bf16[1024,256]{1,0:T(8,128)(2,1)S(1)} collective-permute-done((bf16[1024,256]{1,0:T(8,128)(2,1)S(1)}, bf16[1024,256]{1,0:T(8,128)(2,1)S(1)}, u32[]{:S(2)}, u32[]{:S(2)}) %collective-permute-start.8) | collective-permute-done | bytes 524320 | tf_op jit(solution)/shard_map/ppermute | solution.py:32
  33.2 2.3 %collective-permute-start.12 = (bf16[512,256]{1,0:T(8,128)(2,1)S(1)}, bf16[512,256]{1,0:T(8,128)(2,1)S(1)}, u32[]{:S(2)}, u32[]{:S(2)}) collective-permute-start(bf16[512,256]{1,0:T(8,128)(2,1)S(1)} %get-tuple-element.79), channel_id=1, source_target_pairs={{0,24},{4,100},{8,16},{12,108},{16,8},{20,116},{24,0},{28,124},{32... | collective-permute-start | bytes 786440 | tf_op jit(solution)/shard_map/ppermute | solution.py:36
  36.5 3.5 %back_columns.3 = bf16[448,8192]{1,0:T(8,128)(2,1)} custom-call(bf16[448,512]{1,0:T(8,128)(2,1)S(1)} %copy-done.3, bf16[448,8192]{1,0:T(8,128)(2,1)S(1)} %copy-done, bf16[8192,512]{1,0:T(8,128)(2,1)S(1)} %bitcast.1, bf16[448,8192]{1,0:T(8,128)(2,1)} %back_columns.2.refs_3_), custom_call_target="tpu_custom_call", output_to_operand_aliasing={{}: (3, {})} | custom-call | flops 17179869184 | bytes 67108864 | tf_op jit(solution)/shard_map/back_columns/pallas_call | solution.py:168
  40.1 2.4 %collective-permute-done.12.g5 = bf16[512,256]{1,0:T(8,128)(2,1)S(1)} collective-permute-done((bf16[512,256]{1,0:T(8,128)(2,1)S(1)}, bf16[512,256]{1,0:T(8,128)(2,1)S(1)}, u32[]{:S(2)}, u32[]{:S(2)}) %collective-permute-start.12) | collective-permute-done | bytes 262176 | tf_op jit(solution)/shard_map/ppermute | solution.py:36
  43.4 2.1 %update_rows.1 = (f32[256,512]{1,0:T(8,128)}, f32[256,512]{1,0:T(8,128)}, f32[256,512]{1,0:T(8,128)S(1)}, bf16[272,512]{1,0:T(8,128)(2,1)S(1)}) custom-call(s32[32]{0:T(128)S(1)} %fusion.3.refs_0_.block, bf16[2048,256]{1,0:T(8,128)(2,1)S(1)} %terms.13.g0, bf16[1024,256]{1,0:T(8,128)(2,1)S(1)} %collective-permute-done.6.g1, ...), custom_call_target="tpu_custom_call" | custom-call | flops 1048576 | bytes 65536 | tf_op jit(solution)/shard_map/update_rows/pallas_call | solution.py:225
  45.6 2.2 %collective-permute-start.15 = (bf16[272,512]{1,0:T(8,128)(2,1)S(1)}, bf16[272,512]{1,0:T(8,128)(2,1)S(1)}, u32[]{:S(2)}, u32[]{:S(2)}) collective-permute-start(bf16[272,512]{1,0:T(8,128)(2,1)S(1)} %get-tuple-element.62.refs_0_), channel_id=1, source_target_pairs={{0,24},{4,100},{8,16},{12,108},{16,8},{20,116},{24,0},{28,124},{32... | collective-permute-start | bytes 835592 | tf_op jit(solution)/shard_map/ppermute | solution.py:36
  48.8 6.6 %collective-permute-done.15.refs_3_ = bf16[272,512]{1,0:T(8,128)(2,1)S(1)} collective-permute-done((bf16[272,512]{1,0:T(8,128)(2,1)S(1)}, bf16[272,512]{1,0:T(8,128)(2,1)S(1)}, u32[]{:S(2)}, u32[]{:S(2)}) %collective-permute-start.15) | collective-permute-done | bytes 278560 | tf_op jit(solution)/shard_map/ppermute | solution.py:36
  56.0 2.5 %collective-permute-start.22 = (bf16[1024,512]{1,0:T(8,128)(2,1)S(1)}, bf16[1024,512]{1,0:T(8,128)(2,1)S(1)}, u32[]{:S(2)}, u32[]{:S(2)}) collective-permute-start(bf16[1024,512]{1,0:T(8,128)(2,1)S(1)} %get-tuple-element.68.refs_3_), channel_id=1, source_target_pairs={{0,96},{4,28},{8,104},{12,20},{16,112},{20,12},{24,120},{28,4},{32... | collective-permute-start | bytes 3145736 | tf_op jit(solution)/shard_map/ppermute | solution.py:32
  58.5 1.3 %collective-permute-start.16 = (f32[16,128]{1,0:T(8,128)S(1)}, f32[16,128]{1,0:T(8,128)S(1)}, u32[]{:S(2)}, u32[]{:S(2)}) collective-permute-start(f32[16,128]{1,0:T(8,128)S(1)} %get-tuple-element.63), channel_id=1, source_target_pairs={{0,1},{1,0},{2,3},{3,2},{4,5},{5,4},{6,7},{7,6},{8,9},{9,8},{10,11... | collective-permute-start | bytes 24584 | tf_op jit(solution)/shard_map/ppermute | solution.py:40
  61.0 2.7 %collective-permute-start.17 = (f32[16,128]{1,0:T(8,128)S(1)}, f32[16,128]{1,0:T(8,128)S(1)}, u32[]{:S(2)}, u32[]{:S(2)}) collective-permute-start(f32[16,128]{1,0:T(8,128)S(1)} %add.58), channel_id=1, source_target_pairs={{0,3},{1,2},{2,1},{3,0},{4,7},{5,6},{6,5},{7,4},{8,11},{9,10},{10,... | collective-permute-start | bytes 24584 | tf_op jit(solution)/shard_map/ppermute | solution.py:40
  63.7 1.3 %collective-permute-done.17 = f32[16,128]{1,0:T(8,128)S(1)} collective-permute-done((f32[16,128]{1,0:T(8,128)S(1)}, f32[16,128]{1,0:T(8,128)S(1)}, u32[]{:S(2)}, u32[]{:S(2)}) %collective-permute-start.17) | collective-permute-done | bytes 8224 | tf_op jit(solution)/shard_map/ppermute | solution.py:40
  65.4 2.9 %collective-permute-start.19 = (f32[16,128]{1,0:T(8,128)S(1)}, f32[16,128]{1,0:T(8,128)S(1)}, u32[]{:S(2)}, u32[]{:S(2)}) collective-permute-start(f32[16,128]{1,0:T(8,128)S(1)} %add.59), channel_id=1, source_target_pairs={{0,64},{4,20},{8,72},{12,28},{16,80},{20,4},{24,88},{28,12},{32,96... | collective-permute-start | bytes 24584 | tf_op jit(solution)/shard_map/ppermute | solution.py:32
  68.3 3.0 %collective-permute-done.20 = f32[16,128]{1,0:T(8,128)S(1)} collective-permute-done((f32[16,128]{1,0:T(8,128)S(1)}, f32[16,128]{1,0:T(8,128)S(1)}, u32[]{:S(2)}, u32[]{:S(2)}) %collective-permute-start.20) | collective-permute-done | bytes 8224 | tf_op jit(solution)/shard_map/ppermute | solution.py:32
  71.3 2.0 %collective-permute-done.19 = f32[16,128]{1,0:T(8,128)S(1)} collective-permute-done((f32[16,128]{1,0:T(8,128)S(1)}, f32[16,128]{1,0:T(8,128)S(1)}, u32[]{:S(2)}, u32[]{:S(2)}) %collective-permute-start.19) | collective-permute-done | bytes 8224 | tf_op jit(solution)/shard_map/ppermute | solution.py:32
  73.5 4.7 %collective-permute-start.23 = (bf16[1024,512]{1,0:T(8,128)(2,1)S(1)}, bf16[1024,512]{1,0:T(8,128)(2,1)S(1)}, u32[]{:S(2)}, u32[]{:S(2)}) collective-permute-start(bf16[1024,512]{1,0:T(8,128)(2,1)S(1)} %get-tuple-element.68.refs_3_), channel_id=1, source_target_pairs={{0,4},{4,0},{1,5},{5,1},{2,6},{6,2},{3,7},{7,3},{8,12},{12,8},{9,1... | collective-permute-start | bytes 3145736 | tf_op jit(solution)/shard_map/ppermute | solution.py:44
  79.5 3.3 %collective-permute-start.25 = (bf16[512,512]{1,0:T(8,128)(2,1)S(1)}, bf16[512,512]{1,0:T(8,128)(2,1)S(1)}, u32[]{:S(2)}, u32[]{:S(2)}) collective-permute-start(bf16[512,512]{1,0:T(8,128)(2,1)S(1)} %taken.2), channel_id=1, source_target_pairs={{0,96},{4,28},{8,104},{12,20},{16,112},{20,12},{24,120},{28,4},{32... | collective-permute-start | bytes 1572872 | tf_op jit(solution)/shard_map/ppermute | solution.py:32
  83.9 4.3 %apply_update.2 = (bf16[8192,512]{1,0:T(8,128)(2,1)}, f32[256,512]{1,0:T(8,128)}) custom-call(s32[32]{0:T(128)S(1)} %fusion.3.refs_0_.block, f32[16,128]{1,0:T(8,128)S(1)} %add.63.refs_1_, bf16[8192,512]{1,0:T(8,128)(2,1)S(1)} %bitcast.1, bf16[1024,512]{1,0:T(8,128)(2,1)S(1)} %get-tuple-element.68.refs_3_, ...), custom_call_target="tpu_custom_call" | custom-call | flops 1048576 | bytes 65536 | tf_op jit(solution)/shard_map/apply_update/pallas_call | solution.py:276
  90.0 1.4 %collective-permute-done.29.refs_5_ = bf16[512,512]{1,0:T(8,128)(2,1)S(1)} collective-permute-done((bf16[512,512]{1,0:T(8,128)(2,1)S(1)}, bf16[512,512]{1,0:T(8,128)(2,1)S(1)}, u32[]{:S(2)}, u32[]{:S(2)}) %collective-permute-start.29) | collective-permute-done | bytes 524320 | tf_op jit(solution)/shard_map/ppermute | solution.py:44
  92.2 2.1 %apply_update.3 = bf16[8192,512]{1,0:T(8,128)(2,1)} custom-call(s32[32]{0:T(128)S(1)} %fusion.3.refs_0_.block, f32[16,128]{1,0:T(8,128)S(1)} %add.63.refs_1_, bf16[8192,512]{1,0:T(8,128)(2,1)S(1)} %bitcast.1, bf16[512,512]{1,0:T(8,128)(2,1)S(1)} %collective-permute-done.25.refs_3_, ...), custom_call_target="tpu_custom_call", output_to_operand_aliasing={{}: (7, {})} | custom-call | flops 1048576 | bytes 65536 | tf_op jit(solution)/shard_map/apply_update/pallas_call | solution.py:276
  (66 shorter events, 14.6 us)
Async XLA Ops:
  4.8 4.2 %collective-permute-start = (bf16[2048,256]{1,0:T(8,128)(2,1)S(1)}, bf16[2048,256]{1,0:T(8,128)(2,1)S(1)}, u32[]{:S(2)}, u32[]{:S(2)}) collective-permute-start(bf16[2048,256]{1,0:T(8,128)(2,1)S(1)} %get-tuple-element.43), channel_id=1, source_target_pairs={{0,4},{4,0},{1,5},{5,1},{2,6},{6,2},{3,7},{7,3},{8,12},{12,8},{9,1... | collective-permute-start | bytes 3145736 | tf_op jit(solution)/shard_map/ppermute | solution.py:44
  8.8 5.6 %collective-permute-start.1 = (bf16[2048,256]{1,0:T(8,128)(2,1)S(1)}, bf16[2048,256]{1,0:T(8,128)(2,1)S(1)}, u32[]{:S(2)}, u32[]{:S(2)}) collective-permute-start(bf16[2048,256]{1,0:T(8,128)(2,1)S(1)} %terms.8), channel_id=1, source_target_pairs={{0,4},{4,0},{1,5},{5,1},{2,6},{6,2},{3,7},{7,3},{8,12},{12,8},{9,1... | collective-permute-start | bytes 3145736 | tf_op jit(solution)/shard_map/ppermute | solution.py:44
  9.2 10.6 %collective-permute-start.3 = (bf16[1024,256]{1,0:T(8,128)(2,1)S(1)}, bf16[1024,256]{1,0:T(8,128)(2,1)S(1)}, u32[]{:S(2)}, u32[]{:S(2)}) collective-permute-start(bf16[1024,256]{1,0:T(8,128)(2,1)S(1)} %get-tuple-element.82), channel_id=1, source_target_pairs={{0,96},{4,28},{8,104},{12,20},{16,112},{20,12},{24,120},{28,4},{32... | collective-permute-start | bytes 1572872 | tf_op jit(solution)/shard_map/ppermute | solution.py:32
  13.1 8.3 %collective-permute-start.4 = (bf16[1024,256]{1,0:T(8,128)(2,1)S(1)}, bf16[1024,256]{1,0:T(8,128)(2,1)S(1)}, u32[]{:S(2)}, u32[]{:S(2)}) collective-permute-start(bf16[1024,256]{1,0:T(8,128)(2,1)S(1)} %get-tuple-element.83), channel_id=1, source_target_pairs={{0,32},{4,12},{8,40},{12,4},{16,48},{20,28},{24,56},{28,20},{32,0}... | collective-permute-start | bytes 1572872 | tf_op jit(solution)/shard_map/ppermute | solution.py:32
  15.7 14.8 %collective-permute-start.6 = (bf16[1024,256]{1,0:T(8,128)(2,1)S(1)}, bf16[1024,256]{1,0:T(8,128)(2,1)S(1)}, u32[]{:S(2)}, u32[]{:S(2)}) collective-permute-start(bf16[1024,256]{1,0:T(8,128)(2,1)S(1)} %get-tuple-element.52), channel_id=1, source_target_pairs={{0,32},{4,12},{8,40},{12,4},{16,48},{20,28},{24,56},{28,20},{32,0}... | collective-permute-start | bytes 1572872 | tf_op jit(solution)/shard_map/ppermute | solution.py:32
  17.2 8.4 %slice-start.1 = ((s8[8388608]{0:T(1024)(128)(4,1)}), s8[4194304]{0:T(1024)(128)(4,1)S(1)}, s32[]{:S(2)}) async-start(s8[8388608]{0:T(1024)(128)(4,1)} %bitcast), calls=%async_computation.1 | async-start | bytes 8388608
  17.2 13.2 %collective-permute-start.9 = (bf16[1024,256]{1,0:T(8,128)(2,1)S(1)}, bf16[1024,256]{1,0:T(8,128)(2,1)S(1)}, u32[]{:S(2)}, u32[]{:S(2)}) collective-permute-start(bf16[1024,256]{1,0:T(8,128)(2,1)S(1)} %get-tuple-element.53), channel_id=1, source_target_pairs={{0,96},{4,28},{8,104},{12,20},{16,112},{20,12},{24,120},{28,4},{32... | collective-permute-start | bytes 1572872 | tf_op jit(solution)/shard_map/ppermute | solution.py:32
  17.3 4.1 %collective-permute-start.2 = (bf16[2048,256]{1,0:T(8,128)(2,1)S(1)}, bf16[2048,256]{1,0:T(8,128)(2,1)S(1)}, u32[]{:S(2)}, u32[]{:S(2)}) collective-permute-start(bf16[2048,256]{1,0:T(8,128)(2,1)S(1)} %terms.9), channel_id=1, source_target_pairs={{0,4},{4,0},{1,5},{5,1},{2,6},{6,2},{3,7},{7,3},{8,12},{12,8},{9,1... | collective-permute-start | bytes 3145736 | tf_op jit(solution)/shard_map/ppermute | solution.py:44
  19.8 9.4 %collective-permute-start.5 = (bf16[2048,256]{1,0:T(8,128)(2,1)S(1)}, bf16[2048,256]{1,0:T(8,128)(2,1)S(1)}, u32[]{:S(2)}, u32[]{:S(2)}) collective-permute-start(bf16[2048,256]{1,0:T(8,128)(2,1)S(1)} %terms.11), channel_id=1, source_target_pairs={{0,4},{4,0},{1,5},{5,1},{2,6},{6,2},{3,7},{7,3},{8,12},{12,8},{9,1... | collective-permute-start | bytes 3145736 | tf_op jit(solution)/shard_map/ppermute | solution.py:44
  22.8 9.9 %collective-permute-start.8 = (bf16[1024,256]{1,0:T(8,128)(2,1)S(1)}, bf16[1024,256]{1,0:T(8,128)(2,1)S(1)}, u32[]{:S(2)}, u32[]{:S(2)}) collective-permute-start(bf16[1024,256]{1,0:T(8,128)(2,1)S(1)} %get-tuple-element.56), channel_id=1, source_target_pairs={{0,32},{4,12},{8,40},{12,4},{16,48},{20,28},{24,56},{28,20},{32,0}... | collective-permute-start | bytes 1572872 | tf_op jit(solution)/shard_map/ppermute | solution.py:32
  23.3 9.5 %collective-permute-start.7 = (bf16[1024,256]{1,0:T(8,128)(2,1)S(1)}, bf16[1024,256]{1,0:T(8,128)(2,1)S(1)}, u32[]{:S(2)}, u32[]{:S(2)}) collective-permute-start(bf16[1024,256]{1,0:T(8,128)(2,1)S(1)} %get-tuple-element.57), channel_id=1, source_target_pairs={{0,96},{4,28},{8,104},{12,20},{16,112},{20,12},{24,120},{28,4},{32... | collective-permute-start | bytes 1572872 | tf_op jit(solution)/shard_map/ppermute | solution.py:32
  33.2 9.3 %collective-permute-start.12 = (bf16[512,256]{1,0:T(8,128)(2,1)S(1)}, bf16[512,256]{1,0:T(8,128)(2,1)S(1)}, u32[]{:S(2)}, u32[]{:S(2)}) collective-permute-start(bf16[512,256]{1,0:T(8,128)(2,1)S(1)} %get-tuple-element.79), channel_id=1, source_target_pairs={{0,24},{4,100},{8,16},{12,108},{16,8},{20,116},{24,0},{28,124},{32... | collective-permute-start | bytes 786440 | tf_op jit(solution)/shard_map/ppermute | solution.py:36
  35.4 7.1 %collective-permute-start.11 = (bf16[512,256]{1,0:T(8,128)(2,1)S(1)}, bf16[512,256]{1,0:T(8,128)(2,1)S(1)}, u32[]{:S(2)}, u32[]{:S(2)}) collective-permute-start(bf16[512,256]{1,0:T(8,128)(2,1)S(1)} %get-tuple-element.80), channel_id=1, source_target_pairs={{0,16},{4,68},{8,24},{12,76},{16,0},{20,84},{24,8},{28,92},{32,48}... | collective-permute-start | bytes 786440 | tf_op jit(solution)/shard_map/ppermute | solution.py:36
  36.0 7.5 %collective-permute-start.10 = (bf16[512,256]{1,0:T(8,128)(2,1)S(1)}, bf16[512,256]{1,0:T(8,128)(2,1)S(1)}, u32[]{:S(2)}, u32[]{:S(2)}) collective-permute-start(bf16[512,256]{1,0:T(8,128)(2,1)S(1)} %get-tuple-element.81), channel_id=1, source_target_pairs={{0,8},{4,36},{8,0},{12,44},{16,24},{20,52},{24,16},{28,60},{32,40}... | collective-permute-start | bytes 786440 | tf_op jit(solution)/shard_map/ppermute | solution.py:36
  45.6 9.9 %collective-permute-start.15 = (bf16[272,512]{1,0:T(8,128)(2,1)S(1)}, bf16[272,512]{1,0:T(8,128)(2,1)S(1)}, u32[]{:S(2)}, u32[]{:S(2)}) collective-permute-start(bf16[272,512]{1,0:T(8,128)(2,1)S(1)} %get-tuple-element.62.refs_0_), channel_id=1, source_target_pairs={{0,24},{4,100},{8,16},{12,108},{16,8},{20,116},{24,0},{28,124},{32... | collective-permute-start | bytes 835592 | tf_op jit(solution)/shard_map/ppermute | solution.py:36
  47.7 7.7 %collective-permute-start.14 = (bf16[272,512]{1,0:T(8,128)(2,1)S(1)}, bf16[272,512]{1,0:T(8,128)(2,1)S(1)}, u32[]{:S(2)}, u32[]{:S(2)}) collective-permute-start(bf16[272,512]{1,0:T(8,128)(2,1)S(1)} %get-tuple-element.62.refs_0_), channel_id=1, source_target_pairs={{0,16},{4,68},{8,24},{12,76},{16,0},{20,84},{24,8},{28,92},{32,48}... | collective-permute-start | bytes 835592 | tf_op jit(solution)/shard_map/ppermute | solution.py:36
  48.3 7.7 %collective-permute-start.13 = (bf16[272,512]{1,0:T(8,128)(2,1)S(1)}, bf16[272,512]{1,0:T(8,128)(2,1)S(1)}, u32[]{:S(2)}, u32[]{:S(2)}) collective-permute-start(bf16[272,512]{1,0:T(8,128)(2,1)S(1)} %get-tuple-element.62.refs_0_), channel_id=1, source_target_pairs={{0,8},{4,36},{8,0},{12,44},{16,24},{20,52},{24,16},{28,60},{32,40}... | collective-permute-start | bytes 835592 | tf_op jit(solution)/shard_map/ppermute | solution.py:36
  56.0 17.3 %collective-permute-start.22 = (bf16[1024,512]{1,0:T(8,128)(2,1)S(1)}, bf16[1024,512]{1,0:T(8,128)(2,1)S(1)}, u32[]{:S(2)}, u32[]{:S(2)}) collective-permute-start(bf16[1024,512]{1,0:T(8,128)(2,1)S(1)} %get-tuple-element.68.refs_3_), channel_id=1, source_target_pairs={{0,96},{4,28},{8,104},{12,20},{16,112},{20,12},{24,120},{28,4},{32... | collective-permute-start | bytes 3145736 | tf_op jit(solution)/shard_map/ppermute | solution.py:32
  58.5 14.9 %collective-permute-start.21 = (bf16[1024,512]{1,0:T(8,128)(2,1)S(1)}, bf16[1024,512]{1,0:T(8,128)(2,1)S(1)}, u32[]{:S(2)}, u32[]{:S(2)}) collective-permute-start(bf16[1024,512]{1,0:T(8,128)(2,1)S(1)} %get-tuple-element.68.refs_3_), channel_id=1, source_target_pairs={{0,32},{4,12},{8,40},{12,4},{16,48},{20,28},{24,56},{28,20},{32,0}... | collective-permute-start | bytes 3145736 | tf_op jit(solution)/shard_map/ppermute | solution.py:32
  58.5 2.5 %collective-permute-start.16 = (f32[16,128]{1,0:T(8,128)S(1)}, f32[16,128]{1,0:T(8,128)S(1)}, u32[]{:S(2)}, u32[]{:S(2)}) collective-permute-start(f32[16,128]{1,0:T(8,128)S(1)} %get-tuple-element.63), channel_id=1, source_target_pairs={{0,1},{1,0},{2,3},{3,2},{4,5},{5,4},{6,7},{7,6},{8,9},{9,8},{10,11... | collective-permute-start | bytes 24584 | tf_op jit(solution)/shard_map/ppermute | solution.py:40
  61.0 4.1 %collective-permute-start.17 = (f32[16,128]{1,0:T(8,128)S(1)}, f32[16,128]{1,0:T(8,128)S(1)}, u32[]{:S(2)}, u32[]{:S(2)}) collective-permute-start(f32[16,128]{1,0:T(8,128)S(1)} %add.58), channel_id=1, source_target_pairs={{0,3},{1,2},{2,1},{3,0},{4,7},{5,6},{6,5},{7,4},{8,11},{9,10},{10,... | collective-permute-start | bytes 24584 | tf_op jit(solution)/shard_map/ppermute | solution.py:40
  65.0 6.3 %collective-permute-start.20 = (f32[16,128]{1,0:T(8,128)S(1)}, f32[16,128]{1,0:T(8,128)S(1)}, u32[]{:S(2)}, u32[]{:S(2)}) collective-permute-start(f32[16,128]{1,0:T(8,128)S(1)} %add.59), channel_id=1, source_target_pairs={{0,96},{4,28},{8,104},{12,20},{16,112},{20,12},{24,120},{28,4},{32... | collective-permute-start | bytes 24584 | tf_op jit(solution)/shard_map/ppermute | solution.py:32
  65.4 8.0 %collective-permute-start.19 = (f32[16,128]{1,0:T(8,128)S(1)}, f32[16,128]{1,0:T(8,128)S(1)}, u32[]{:S(2)}, u32[]{:S(2)}) collective-permute-start(f32[16,128]{1,0:T(8,128)S(1)} %add.59), channel_id=1, source_target_pairs={{0,64},{4,20},{8,72},{12,28},{16,80},{20,4},{24,88},{28,12},{32,96... | collective-permute-start | bytes 24584 | tf_op jit(solution)/shard_map/ppermute | solution.py:32
  68.3 5.0 %collective-permute-start.18 = (f32[16,128]{1,0:T(8,128)S(1)}, f32[16,128]{1,0:T(8,128)S(1)}, u32[]{:S(2)}, u32[]{:S(2)}) collective-permute-start(f32[16,128]{1,0:T(8,128)S(1)} %add.59), channel_id=1, source_target_pairs={{0,32},{4,12},{8,40},{12,4},{16,48},{20,28},{24,56},{28,20},{32,0}... | collective-permute-start | bytes 24584 | tf_op jit(solution)/shard_map/ppermute | solution.py:32
  73.5 9.3 %collective-permute-start.23 = (bf16[1024,512]{1,0:T(8,128)(2,1)S(1)}, bf16[1024,512]{1,0:T(8,128)(2,1)S(1)}, u32[]{:S(2)}, u32[]{:S(2)}) collective-permute-start(bf16[1024,512]{1,0:T(8,128)(2,1)S(1)} %get-tuple-element.68.refs_3_), channel_id=1, source_target_pairs={{0,4},{4,0},{1,5},{5,1},{2,6},{6,2},{3,7},{7,3},{8,12},{12,8},{9,1... | collective-permute-start | bytes 3145736 | tf_op jit(solution)/shard_map/ppermute | solution.py:44
  78.1 5.8 %collective-permute-start.26 = (bf16[1024,512]{1,0:T(8,128)(2,1)S(1)}, bf16[1024,512]{1,0:T(8,128)(2,1)S(1)}, u32[]{:S(2)}, u32[]{:S(2)}) collective-permute-start(bf16[1024,512]{1,0:T(8,128)(2,1)S(1)} %collective-permute-done.21.ref.refs_4_), channel_id=1, source_target_pairs={{0,4},{4,0},{1,5},{5,1},{2,6},{6,2},{3,7},{7,3},{8,12},{12,8},{9,1... | collective-permute-start | bytes 3145736 | tf_op jit(solution)/shard_map/ppermute | solution.py:44
  78.2 5.7 %collective-permute-start.27 = (bf16[1024,512]{1,0:T(8,128)(2,1)S(1)}, bf16[1024,512]{1,0:T(8,128)(2,1)S(1)}, u32[]{:S(2)}, u32[]{:S(2)}) collective-permute-start(bf16[1024,512]{1,0:T(8,128)(2,1)S(1)} %collective-permute-done.22.ref.refs_5_), channel_id=1, source_target_pairs={{0,4},{4,0},{1,5},{5,1},{2,6},{6,2},{3,7},{7,3},{8,12},{12,8},{9,1... | collective-permute-start | bytes 3145736 | tf_op jit(solution)/shard_map/ppermute | solution.py:44
  78.7 9.6 %collective-permute-start.28 = (bf16[512,512]{1,0:T(8,128)(2,1)S(1)}, bf16[512,512]{1,0:T(8,128)(2,1)S(1)}, u32[]{:S(2)}, u32[]{:S(2)}) collective-permute-start(bf16[512,512]{1,0:T(8,128)(2,1)S(1)} %taken.3), channel_id=1, source_target_pairs={{0,32},{4,12},{8,40},{12,4},{16,48},{20,28},{24,56},{28,20},{32,0}... | collective-permute-start | bytes 1572872 | tf_op jit(solution)/shard_map/ppermute | solution.py:32
  79.5 10.1 %collective-permute-start.25 = (bf16[512,512]{1,0:T(8,128)(2,1)S(1)}, bf16[512,512]{1,0:T(8,128)(2,1)S(1)}, u32[]{:S(2)}, u32[]{:S(2)}) collective-permute-start(bf16[512,512]{1,0:T(8,128)(2,1)S(1)} %taken.2), channel_id=1, source_target_pairs={{0,96},{4,28},{8,104},{12,20},{16,112},{20,12},{24,120},{28,4},{32... | collective-permute-start | bytes 1572872 | tf_op jit(solution)/shard_map/ppermute | solution.py:32
  82.7 1.2 %collective-permute-start.24 = (f32[16,128]{1,0:T(8,128)S(1)}, f32[16,128]{1,0:T(8,128)S(1)}, u32[]{:S(2)}, u32[]{:S(2)}) collective-permute-start(f32[16,128]{1,0:T(8,128)S(1)} %add_add_fusion), channel_id=1, source_target_pairs={{0,4},{4,0},{1,5},{5,1},{2,6},{6,2},{3,7},{7,3},{8,12},{12,8},{9,1... | collective-permute-start | bytes 24584 | tf_op jit(solution)/shard_map/ppermute | solution.py:44
  89.5 1.9 %collective-permute-start.29 = (bf16[512,512]{1,0:T(8,128)(2,1)S(1)}, bf16[512,512]{1,0:T(8,128)(2,1)S(1)}, u32[]{:S(2)}, u32[]{:S(2)}) collective-permute-start(bf16[512,512]{1,0:T(8,128)(2,1)S(1)} %collective-permute-done.25.refs_3_), channel_id=1, source_target_pairs={{0,4},{4,0},{1,5},{5,1},{2,6},{6,2},{3,7},{7,3},{8,12},{12,8},{9,1... | collective-permute-start | bytes 1572872 | tf_op jit(solution)/shard_map/ppermute | solution.py:44
  89.9 2.3 %collective-permute-start.30 = (bf16[512,512]{1,0:T(8,128)(2,1)S(1)}, bf16[512,512]{1,0:T(8,128)(2,1)S(1)}, u32[]{:S(2)}, u32[]{:S(2)}) collective-permute-start(bf16[512,512]{1,0:T(8,128)(2,1)S(1)} %collective-permute-done.28.refs_4_), channel_id=1, source_target_pairs={{0,4},{4,0},{1,5},{5,1},{2,6},{6,2},{3,7},{7,3},{8,12},{12,8},{9,1... | collective-permute-start | bytes 1572872 | tf_op jit(solution)/shard_map/ppermute | solution.py:44
  (5 other events, 35.5 us)

commit v7 on v6

--- a/solution.py
+++ b/solution.py
@@ -418,7 +418,7 @@
     near_one = along_first(mine, 1)
     near_three = along_first(mine, 3)
     sums = sums + along_y(sums, 1)
-    sums = sums + along_y(sums, 3)
+    sums = sums + along_y(sums, 2)
     sums = sums + along_first(sums, 1) + along_first(sums, 2) + along_first(sums, 3)
     low = taken(after(near_one, sums), 0)
     high = taken(after(near_three, sums), 2 * ROWS)

time: 94.5 us -> 94.8 us (level)
  no operation moved by 1% of the time
where the time goes in v7:
time: 94.8 us; the launch traced here: 94.7 us
  starting transfers between devices  37 us (39%)
  Pallas kernels  28.9 us (30%)
  waiting for transfers between devices  27.2 us (29%)
  between operations  1.02 us (1%)
    ppermute x13, starting transfers between devices, along_first(): return lax.ppermute(value, DP, exchanges('first', k))  17.9 us
    ppermute x13, waiting for transfers between devices, along_first(): return lax.ppermute(value, DP, exchanges('first', k))  10.9 us
    ppermute x6, waiting for transfers between devices, along_second(): return lax.ppermute(value, DP, exchanges('second', k))  10.5 us
    pallas_call x7, Pallas kernels, terms(): pl.pallas_call(body, out_shape=tuple((jax.ShapeDtypeStruct((p * D, ROWS),...  8.95 us
    ppermute x10, starting transfers between devices, sibling(): return lax.ppermute(value, 'c', [(0, 1), (1, 0)])  8.4 us
    pallas_call x2, Pallas kernels, back_columns(): pl.pallas_call(body, out_shape=jax.ShapeDtypeStruct(preactivation.shape,...  7.12 us
    ppermute x6, starting transfers between devices, along_second(): return lax.ppermute(value, DP, exchanges('second', k))  6.59 us
    pallas_call x2, Pallas kernels, apply_update(): pl.pallas_call(body, out_shape=(jax.ShapeDtypeStruct(weight.shape, jnp.bf...  6.4 us
  transfers between devices with their start and end apart: 31, of which 16 were waited for; matrix products, arithmetic and copies ran while one was open for 0% of the time, Pallas kernels for 22%

profile of v7, /device:TPU:1, one launch (start us, length us, event | category | flops | bytes accessed | tf_op | source)
XLA Modules:
  0.0 94.7 jit_solution(16773889670811930534)
XLA Ops:
  0.7 4.1 %first_terms.1 = (bf16[2048,256]{1,0:T(8,128)(2,1)S(1)}, bf16[512,448]{1,0:T(8,128)(2,1)S(1)}) custom-call(s32[32]{0:T(128)S(1)} %fusion.3.refs_0_.block, bf16[448,512]{1,0:T(8,128)(2,1)} %refs_0_.1, bf16[448,8192]{1,0:T(8,128)(2,1)} %refs_1_.5), custom_call_target="tpu_custom_call" | custom-call | flops 17179869184 | bytes 67108864 | tf_op jit(solution)/shard_map/first_terms/pallas_call | solution.py:91
  4.8 1.5 %collective-permute-start = (bf16[2048,256]{1,0:T(8,128)(2,1)S(1)}, bf16[2048,256]{1,0:T(8,128)(2,1)S(1)}, u32[]{:S(2)}, u32[]{:S(2)}) collective-permute-start(bf16[2048,256]{1,0:T(8,128)(2,1)S(1)} %get-tuple-element.43), channel_id=1, source_target_pairs={{0,4},{4,0},{1,5},{5,1},{2,6},{6,2},{3,7},{7,3},{8,12},{12,8},{9,1... | collective-permute-start | bytes 3145736 | tf_op jit(solution)/shard_map/ppermute | solution.py:44
  6.3 1.3 %terms.7 = (bf16[1024,256]{1,0:T(8,128)(2,1)S(1)}, bf16[1024,256]{1,0:T(8,128)(2,1)S(1)}) custom-call(s32[32]{0:T(128)S(1)} %fusion.3.refs_0_.block, bf16[512,448]{1,0:T(8,128)(2,1)S(1)} %get-tuple-element.59.refs_1_, bf16[448,8192]{1,0:T(8,128)(2,1)S(1)} %copy-done), custom_call_target="tpu_custom_call" | custom-call | flops 17179869184 | bytes 67108864 | tf_op jit(solution)/shard_map/terms/pallas_call | solution.py:137
  7.6 1.3 %terms.8 = bf16[2048,256]{1,0:T(8,128)(2,1)S(1)} custom-call(s32[32]{0:T(128)S(1)} %fusion.3.refs_0_.block, bf16[512,448]{1,0:T(8,128)(2,1)S(1)} %get-tuple-element.59.refs_1_, bf16[448,8192]{1,0:T(8,128)(2,1)S(1)} %copy-done), custom_call_target="tpu_custom_call" | custom-call | flops 1048576 | bytes 65536 | tf_op jit(solution)/shard_map/terms/pallas_call | solution.py:137
  9.2 3.9 %collective-permute-start.3 = (bf16[1024,256]{1,0:T(8,128)(2,1)S(1)}, bf16[1024,256]{1,0:T(8,128)(2,1)S(1)}, u32[]{:S(2)}, u32[]{:S(2)}) collective-permute-start(bf16[1024,256]{1,0:T(8,128)(2,1)S(1)} %get-tuple-element.82), channel_id=1, source_target_pairs={{0,96},{4,28},{8,104},{12,20},{16,112},{20,12},{24,120},{28,4},{32... | collective-permute-start | bytes 1572872 | tf_op jit(solution)/shard_map/ppermute | solution.py:32
  13.1 1.3 %terms.9 = bf16[2048,256]{1,0:T(8,128)(2,1)S(1)} custom-call(s32[32]{0:T(128)S(1)} %fusion.3.refs_0_.block, bf16[512,448]{1,0:T(8,128)(2,1)S(1)} %get-tuple-element.59.refs_1_, bf16[448,8192]{1,0:T(8,128)(2,1)S(1)} %copy-done), custom_call_target="tpu_custom_call" | custom-call | flops 17179869184 | bytes 67108864 | tf_op jit(solution)/shard_map/terms/pallas_call | solution.py:137
  14.4 1.3 %terms.10 = (bf16[1024,256]{1,0:T(8,128)(2,1)S(1)}, bf16[1024,256]{1,0:T(8,128)(2,1)S(1)}) custom-call(s32[32]{0:T(128)S(1)} %fusion.3.refs_0_.block, bf16[512,448]{1,0:T(8,128)(2,1)S(1)} %get-tuple-element.59.refs_1_, bf16[448,8192]{1,0:T(8,128)(2,1)S(1)} %copy-done, bf16[2048,256]{1,0:T(8,128)(2,1)S(1)} %collective-permute-done.1.refs_3_.refs_4_, ...), custom_call_target="tpu_custom_call" | custom-call | flops 1048576 | bytes 65536 | tf_op jit(solution)/shard_map/terms/pallas_call | solution.py:137
  15.7 1.5 %collective-permute-start.6 = (bf16[1024,256]{1,0:T(8,128)(2,1)S(1)}, bf16[1024,256]{1,0:T(8,128)(2,1)S(1)}, u32[]{:S(2)}, u32[]{:S(2)}) collective-permute-start(bf16[1024,256]{1,0:T(8,128)(2,1)S(1)} %get-tuple-element.52), channel_id=1, source_target_pairs={{0,32},{4,12},{8,40},{12,4},{16,48},{20,28},{24,56},{28,20},{32,0}... | collective-permute-start | bytes 1572872 | tf_op jit(solution)/shard_map/ppermute | solution.py:32
  20.2 1.3 %collective-permute-done.4.refs_6_ = bf16[1024,256]{1,0:T(8,128)(2,1)S(1)} collective-permute-done((bf16[1024,256]{1,0:T(8,128)(2,1)S(1)}, bf16[1024,256]{1,0:T(8,128)(2,1)S(1)}, u32[]{:S(2)}, u32[]{:S(2)}) %collective-permute-start.4) | collective-permute-done | bytes 524320 | tf_op jit(solution)/shard_map/ppermute | solution.py:32
  21.5 1.4 %terms.12 = (bf16[1024,256]{1,0:T(8,128)(2,1)S(1)}, bf16[1024,256]{1,0:T(8,128)(2,1)S(1)}) custom-call(s32[32]{0:T(128)S(1)} %fusion.3.refs_0_.block, bf16[512,448]{1,0:T(8,128)(2,1)S(1)} %get-tuple-element.59.refs_1_, bf16[448,8192]{1,0:T(8,128)(2,1)S(1)} %copy-done, bf16[2048,256]{1,0:T(8,128)(2,1)S(1)} %collective-permute-done.2.refs_3_.refs_5_, ...), custom_call_target="tpu_custom_call" | custom-call | flops 1048576 | bytes 65536 | tf_op jit(solution)/shard_map/terms/pallas_call | solution.py:137
  23.3 2.2 %collective-permute-start.7 = (bf16[1024,256]{1,0:T(8,128)(2,1)S(1)}, bf16[1024,256]{1,0:T(8,128)(2,1)S(1)}, u32[]{:S(2)}, u32[]{:S(2)}) collective-permute-start(bf16[1024,256]{1,0:T(8,128)(2,1)S(1)} %get-tuple-element.57), channel_id=1, source_target_pairs={{0,96},{4,28},{8,104},{12,20},{16,112},{20,12},{24,120},{28,4},{32... | collective-permute-start | bytes 1572872 | tf_op jit(solution)/shard_map/ppermute | solution.py:32
  25.6 3.6 %back_columns.2.refs_3_ = bf16[448,8192]{1,0:T(8,128)(2,1)} custom-call(bf16[448,512]{1,0:T(8,128)(2,1)S(1)} %copy-done.3, bf16[448,8192]{1,0:T(8,128)(2,1)S(1)} %copy-done, bf16[8192,512]{1,0:T(8,128)(2,1)S(1)} %bitcast.1), custom_call_target="tpu_custom_call" | custom-call | flops 17179869184 | bytes 67108864 | tf_op jit(solution)/shard_map/back_columns/pallas_call | solution.py:168
  29.2 1.3 %terms.13.g0 = bf16[2048,256]{1,0:T(8,128)(2,1)S(1)} custom-call(s32[32]{0:T(128)S(1)} %fusion.3.refs_0_.block, bf16[512,448]{1,0:T(8,128)(2,1)S(1)} %get-tuple-element.59.refs_1_, bf16[448,8192]{1,0:T(8,128)(2,1)S(1)} %copy-done, bf16[2048,256]{1,0:T(8,128)(2,1)S(1)} %collective-permute-done.5.refs_3_), custom_call_target="tpu_custom_call" | custom-call | flops 1048576 | bytes 65536 | tf_op jit(solution)/shard_map/terms/pallas_call | solution.py:137
  30.5 2.2 %collective-permute-done.8 = bf16[1024,256]{1,0:T(8,128)(2,1)S(1)} collective-permute-done((bf16[1024,256]{1,0:T(8,128)(2,1)S(1)}, bf16[1024,256]{1,0:T(8,128)(2,1)S(1)}, u32[]{:S(2)}, u32[]{:S(2)}) %collective-permute-start.8) | collective-permute-done | bytes 524320 | tf_op jit(solution)/shard_map/ppermute | solution.py:32
  33.2 2.3 %collective-permute-start.12 = (bf16[512,256]{1,0:T(8,128)(2,1)S(1)}, bf16[512,256]{1,0:T(8,128)(2,1)S(1)}, u32[]{:S(2)}, u32[]{:S(2)}) collective-permute-start(bf16[512,256]{1,0:T(8,128)(2,1)S(1)} %get-tuple-element.79), channel_id=1, source_target_pairs={{0,24},{4,100},{8,16},{12,108},{16,8},{20,116},{24,0},{28,124},{32... | collective-permute-start | bytes 786440 | tf_op jit(solution)/shard_map/ppermute | solution.py:36
  36.5 3.5 %back_columns.3 = bf16[448,8192]{1,0:T(8,128)(2,1)} custom-call(bf16[448,512]{1,0:T(8,128)(2,1)S(1)} %copy-done.3, bf16[448,8192]{1,0:T(8,128)(2,1)S(1)} %copy-done, bf16[8192,512]{1,0:T(8,128)(2,1)S(1)} %bitcast.1, bf16[448,8192]{1,0:T(8,128)(2,1)} %back_columns.2.refs_3_), custom_call_target="tpu_custom_call", output_to_operand_aliasing={{}: (3, {})} | custom-call | flops 17179869184 | bytes 67108864 | tf_op jit(solution)/shard_map/back_columns/pallas_call | solution.py:168
  40.1 2.4 %collective-permute-done.12.g5 = bf16[512,256]{1,0:T(8,128)(2,1)S(1)} collective-permute-done((bf16[512,256]{1,0:T(8,128)(2,1)S(1)}, bf16[512,256]{1,0:T(8,128)(2,1)S(1)}, u32[]{:S(2)}, u32[]{:S(2)}) %collective-permute-start.12) | collective-permute-done | bytes 262176 | tf_op jit(solution)/shard_map/ppermute | solution.py:36
  43.4 2.1 %update_rows.1 = (f32[256,512]{1,0:T(8,128)}, f32[256,512]{1,0:T(8,128)}, f32[256,512]{1,0:T(8,128)S(1)}, bf16[272,512]{1,0:T(8,128)(2,1)S(1)}) custom-call(s32[32]{0:T(128)S(1)} %fusion.3.refs_0_.block, bf16[2048,256]{1,0:T(8,128)(2,1)S(1)} %terms.13.g0, bf16[1024,256]{1,0:T(8,128)(2,1)S(1)} %collective-permute-done.6.g1, ...), custom_call_target="tpu_custom_call" | custom-call | flops 1048576 | bytes 65536 | tf_op jit(solution)/shard_map/update_rows/pallas_call | solution.py:225
  45.6 2.2 %collective-permute-start.15 = (bf16[272,512]{1,0:T(8,128)(2,1)S(1)}, bf16[272,512]{1,0:T(8,128)(2,1)S(1)}, u32[]{:S(2)}, u32[]{:S(2)}) collective-permute-start(bf16[272,512]{1,0:T(8,128)(2,1)S(1)} %get-tuple-element.62.refs_0_), channel_id=1, source_target_pairs={{0,24},{4,100},{8,16},{12,108},{16,8},{20,116},{24,0},{28,124},{32... | collective-permute-start | bytes 835592 | tf_op jit(solution)/shard_map/ppermute | solution.py:36
  48.8 6.6 %collective-permute-done.15.refs_3_ = bf16[272,512]{1,0:T(8,128)(2,1)S(1)} collective-permute-done((bf16[272,512]{1,0:T(8,128)(2,1)S(1)}, bf16[272,512]{1,0:T(8,128)(2,1)S(1)}, u32[]{:S(2)}, u32[]{:S(2)}) %collective-permute-start.15) | collective-permute-done | bytes 278560 | tf_op jit(solution)/shard_map/ppermute | solution.py:36
  56.0 2.5 %collective-permute-start.22 = (bf16[1024,512]{1,0:T(8,128)(2,1)S(1)}, bf16[1024,512]{1,0:T(8,128)(2,1)S(1)}, u32[]{:S(2)}, u32[]{:S(2)}) collective-permute-start(bf16[1024,512]{1,0:T(8,128)(2,1)S(1)} %get-tuple-element.68.refs_3_), channel_id=1, source_target_pairs={{0,96},{4,28},{8,104},{12,20},{16,112},{20,12},{24,120},{28,4},{32... | collective-permute-start | bytes 3145736 | tf_op jit(solution)/shard_map/ppermute | solution.py:32
  58.5 1.3 %collective-permute-start.16 = (f32[16,128]{1,0:T(8,128)S(1)}, f32[16,128]{1,0:T(8,128)S(1)}, u32[]{:S(2)}, u32[]{:S(2)}) collective-permute-start(f32[16,128]{1,0:T(8,128)S(1)} %get-tuple-element.63), channel_id=1, source_target_pairs={{0,1},{1,0},{2,3},{3,2},{4,5},{5,4},{6,7},{7,6},{8,9},{9,8},{10,11... | collective-permute-start | bytes 24584 | tf_op jit(solution)/shard_map/ppermute | solution.py:40
  61.0 2.9 %collective-permute-start.17 = (f32[16,128]{1,0:T(8,128)S(1)}, f32[16,128]{1,0:T(8,128)S(1)}, u32[]{:S(2)}, u32[]{:S(2)}) collective-permute-start(f32[16,128]{1,0:T(8,128)S(1)} %add.58), channel_id=1, source_target_pairs={{0,2},{1,3},{2,0},{3,1},{4,6},{5,7},{6,4},{7,5},{8,10},{9,11},{10,... | collective-permute-start | bytes 24584 | tf_op jit(solution)/shard_map/ppermute | solution.py:40
  65.6 2.7 %collective-permute-start.19 = (f32[16,128]{1,0:T(8,128)S(1)}, f32[16,128]{1,0:T(8,128)S(1)}, u32[]{:S(2)}, u32[]{:S(2)}) collective-permute-start(f32[16,128]{1,0:T(8,128)S(1)} %add.59), channel_id=1, source_target_pairs={{0,64},{4,20},{8,72},{12,28},{16,80},{20,4},{24,88},{28,12},{32,96... | collective-permute-start | bytes 24584 | tf_op jit(solution)/shard_map/ppermute | solution.py:32
  68.3 3.1 %collective-permute-done.20 = f32[16,128]{1,0:T(8,128)S(1)} collective-permute-done((f32[16,128]{1,0:T(8,128)S(1)}, f32[16,128]{1,0:T(8,128)S(1)}, u32[]{:S(2)}, u32[]{:S(2)}) %collective-permute-start.20) | collective-permute-done | bytes 8224 | tf_op jit(solution)/shard_map/ppermute | solution.py:32
  71.3 2.0 %collective-permute-done.19 = f32[16,128]{1,0:T(8,128)S(1)} collective-permute-done((f32[16,128]{1,0:T(8,128)S(1)}, f32[16,128]{1,0:T(8,128)S(1)}, u32[]{:S(2)}, u32[]{:S(2)}) %collective-permute-start.19) | collective-permute-done | bytes 8224 | tf_op jit(solution)/shard_map/ppermute | solution.py:32
  73.5 4.9 %collective-permute-start.23 = (bf16[1024,512]{1,0:T(8,128)(2,1)S(1)}, bf16[1024,512]{1,0:T(8,128)(2,1)S(1)}, u32[]{:S(2)}, u32[]{:S(2)}) collective-permute-start(bf16[1024,512]{1,0:T(8,128)(2,1)S(1)} %get-tuple-element.68.refs_3_), channel_id=1, source_target_pairs={{0,4},{4,0},{1,5},{5,1},{2,6},{6,2},{3,7},{7,3},{8,12},{12,8},{9,1... | collective-permute-start | bytes 3145736 | tf_op jit(solution)/shard_map/ppermute | solution.py:44
  79.7 3.0 %collective-permute-start.25 = (bf16[512,512]{1,0:T(8,128)(2,1)S(1)}, bf16[512,512]{1,0:T(8,128)(2,1)S(1)}, u32[]{:S(2)}, u32[]{:S(2)}) collective-permute-start(bf16[512,512]{1,0:T(8,128)(2,1)S(1)} %taken.2), channel_id=1, source_target_pairs={{0,96},{4,28},{8,104},{12,20},{16,112},{20,12},{24,120},{28,4},{32... | collective-permute-start | bytes 1572872 | tf_op jit(solution)/shard_map/ppermute | solution.py:32
  83.9 4.3 %apply_update.2 = (bf16[8192,512]{1,0:T(8,128)(2,1)}, f32[256,512]{1,0:T(8,128)}) custom-call(s32[32]{0:T(128)S(1)} %fusion.3.refs_0_.block, f32[16,128]{1,0:T(8,128)S(1)} %add.63.refs_1_, bf16[8192,512]{1,0:T(8,128)(2,1)S(1)} %bitcast.1, bf16[1024,512]{1,0:T(8,128)(2,1)S(1)} %get-tuple-element.68.refs_3_, ...), custom_call_target="tpu_custom_call" | custom-call | flops 1048576 | bytes 65536 | tf_op jit(solution)/shard_map/apply_update/pallas_call | solution.py:276
  88.3 1.3 %collective-permute-done.25.refs_3_ = bf16[512,512]{1,0:T(8,128)(2,1)S(1)} collective-permute-done((bf16[512,512]{1,0:T(8,128)(2,1)S(1)}, bf16[512,512]{1,0:T(8,128)(2,1)S(1)}, u32[]{:S(2)}, u32[]{:S(2)}) %collective-permute-start.25) | collective-permute-done | bytes 524320 | tf_op jit(solution)/shard_map/ppermute | solution.py:32
  90.2 1.5 %collective-permute-done.29.refs_5_ = bf16[512,512]{1,0:T(8,128)(2,1)S(1)} collective-permute-done((bf16[512,512]{1,0:T(8,128)(2,1)S(1)}, bf16[512,512]{1,0:T(8,128)(2,1)S(1)}, u32[]{:S(2)}, u32[]{:S(2)}) %collective-permute-start.29) | collective-permute-done | bytes 524320 | tf_op jit(solution)/shard_map/ppermute | solution.py:44
  92.5 2.1 %apply_update.3 = bf16[8192,512]{1,0:T(8,128)(2,1)} custom-call(s32[32]{0:T(128)S(1)} %fusion.3.refs_0_.block, f32[16,128]{1,0:T(8,128)S(1)} %add.63.refs_1_, bf16[8192,512]{1,0:T(8,128)(2,1)S(1)} %bitcast.1, bf16[512,512]{1,0:T(8,128)(2,1)S(1)} %collective-permute-done.25.refs_3_, ...), custom_call_target="tpu_custom_call", output_to_operand_aliasing={{}: (7, {})} | custom-call | flops 1048576 | bytes 65536 | tf_op jit(solution)/shard_map/apply_update/pallas_call | solution.py:276
  (66 shorter events, 14.8 us)
Async XLA Ops:
  4.8 4.2 %collective-permute-start = (bf16[2048,256]{1,0:T(8,128)(2,1)S(1)}, bf16[2048,256]{1,0:T(8,128)(2,1)S(1)}, u32[]{:S(2)}, u32[]{:S(2)}) collective-permute-start(bf16[2048,256]{1,0:T(8,128)(2,1)S(1)} %get-tuple-element.43), channel_id=1, source_target_pairs={{0,4},{4,0},{1,5},{5,1},{2,6},{6,2},{3,7},{7,3},{8,12},{12,8},{9,1... | collective-permute-start | bytes 3145736 | tf_op jit(solution)/shard_map/ppermute | solution.py:44
  8.8 5.6 %collective-permute-start.1 = (bf16[2048,256]{1,0:T(8,128)(2,1)S(1)}, bf16[2048,256]{1,0:T(8,128)(2,1)S(1)}, u32[]{:S(2)}, u32[]{:S(2)}) collective-permute-start(bf16[2048,256]{1,0:T(8,128)(2,1)S(1)} %terms.8), channel_id=1, source_target_pairs={{0,4},{4,0},{1,5},{5,1},{2,6},{6,2},{3,7},{7,3},{8,12},{12,8},{9,1... | collective-permute-start | bytes 3145736 | tf_op jit(solution)/shard_map/ppermute | solution.py:44
  9.2 10.6 %collective-permute-start.3 = (bf16[1024,256]{1,0:T(8,128)(2,1)S(1)}, bf16[1024,256]{1,0:T(8,128)(2,1)S(1)}, u32[]{:S(2)}, u32[]{:S(2)}) collective-permute-start(bf16[1024,256]{1,0:T(8,128)(2,1)S(1)} %get-tuple-element.82), channel_id=1, source_target_pairs={{0,96},{4,28},{8,104},{12,20},{16,112},{20,12},{24,120},{28,4},{32... | collective-permute-start | bytes 1572872 | tf_op jit(solution)/shard_map/ppermute | solution.py:32
  13.1 8.3 %collective-permute-start.4 = (bf16[1024,256]{1,0:T(8,128)(2,1)S(1)}, bf16[1024,256]{1,0:T(8,128)(2,1)S(1)}, u32[]{:S(2)}, u32[]{:S(2)}) collective-permute-start(bf16[1024,256]{1,0:T(8,128)(2,1)S(1)} %get-tuple-element.83), channel_id=1, source_target_pairs={{0,32},{4,12},{8,40},{12,4},{16,48},{20,28},{24,56},{28,20},{32,0}... | collective-permute-start | bytes 1572872 | tf_op jit(solution)/shard_map/ppermute | solution.py:32
  15.7 14.8 %collective-permute-start.6 = (bf16[1024,256]{1,0:T(8,128)(2,1)S(1)}, bf16[1024,256]{1,0:T(8,128)(2,1)S(1)}, u32[]{:S(2)}, u32[]{:S(2)}) collective-permute-start(bf16[1024,256]{1,0:T(8,128)(2,1)S(1)} %get-tuple-element.52), channel_id=1, source_target_pairs={{0,32},{4,12},{8,40},{12,4},{16,48},{20,28},{24,56},{28,20},{32,0}... | collective-permute-start | bytes 1572872 | tf_op jit(solution)/shard_map/ppermute | solution.py:32
  17.2 8.4 %slice-start.1 = ((s8[8388608]{0:T(1024)(128)(4,1)}), s8[4194304]{0:T(1024)(128)(4,1)S(1)}, s32[]{:S(2)}) async-start(s8[8388608]{0:T(1024)(128)(4,1)} %bitcast), calls=%async_computation.1 | async-start | bytes 8388608
  17.2 13.2 %collective-permute-start.9 = (bf16[1024,256]{1,0:T(8,128)(2,1)S(1)}, bf16[1024,256]{1,0:T(8,128)(2,1)S(1)}, u32[]{:S(2)}, u32[]{:S(2)}) collective-permute-start(bf16[1024,256]{1,0:T(8,128)(2,1)S(1)} %get-tuple-element.53), channel_id=1, source_target_pairs={{0,96},{4,28},{8,104},{12,20},{16,112},{20,12},{24,120},{28,4},{32... | collective-permute-start | bytes 1572872 | tf_op jit(solution)/shard_map/ppermute | solution.py:32
  17.3 4.1 %collective-permute-start.2 = (bf16[2048,256]{1,0:T(8,128)(2,1)S(1)}, bf16[2048,256]{1,0:T(8,128)(2,1)S(1)}, u32[]{:S(2)}, u32[]{:S(2)}) collective-permute-start(bf16[2048,256]{1,0:T(8,128)(2,1)S(1)} %terms.9), channel_id=1, source_target_pairs={{0,4},{4,0},{1,5},{5,1},{2,6},{6,2},{3,7},{7,3},{8,12},{12,8},{9,1... | collective-permute-start | bytes 3145736 | tf_op jit(solution)/shard_map/ppermute | solution.py:44
  19.8 9.4 %collective-permute-start.5 = (bf16[2048,256]{1,0:T(8,128)(2,1)S(1)}, bf16[2048,256]{1,0:T(8,128)(2,1)S(1)}, u32[]{:S(2)}, u32[]{:S(2)}) collective-permute-start(bf16[2048,256]{1,0:T(8,128)(2,1)S(1)} %terms.11), channel_id=1, source_target_pairs={{0,4},{4,0},{1,5},{5,1},{2,6},{6,2},{3,7},{7,3},{8,12},{12,8},{9,1... | collective-permute-start | bytes 3145736 | tf_op jit(solution)/shard_map/ppermute | solution.py:44
  22.8 9.9 %collective-permute-start.8 = (bf16[1024,256]{1,0:T(8,128)(2,1)S(1)}, bf16[1024,256]{1,0:T(8,128)(2,1)S(1)}, u32[]{:S(2)}, u32[]{:S(2)}) collective-permute-start(bf16[1024,256]{1,0:T(8,128)(2,1)S(1)} %get-tuple-element.56), channel_id=1, source_target_pairs={{0,32},{4,12},{8,40},{12,4},{16,48},{20,28},{24,56},{28,20},{32,0}... | collective-permute-start | bytes 1572872 | tf_op jit(solution)/shard_map/ppermute | solution.py:32
  23.3 9.5 %collective-permute-start.7 = (bf16[1024,256]{1,0:T(8,128)(2,1)S(1)}, bf16[1024,256]{1,0:T(8,128)(2,1)S(1)}, u32[]{:S(2)}, u32[]{:S(2)}) collective-permute-start(bf16[1024,256]{1,0:T(8,128)(2,1)S(1)} %get-tuple-element.57), channel_id=1, source_target_pairs={{0,96},{4,28},{8,104},{12,20},{16,112},{20,12},{24,120},{28,4},{32... | collective-permute-start | bytes 1572872 | tf_op jit(solution)/shard_map/ppermute | solution.py:32
  33.2 9.3 %collective-permute-start.12 = (bf16[512,256]{1,0:T(8,128)(2,1)S(1)}, bf16[512,256]{1,0:T(8,128)(2,1)S(1)}, u32[]{:S(2)}, u32[]{:S(2)}) collective-permute-start(bf16[512,256]{1,0:T(8,128)(2,1)S(1)} %get-tuple-element.79), channel_id=1, source_target_pairs={{0,24},{4,100},{8,16},{12,108},{16,8},{20,116},{24,0},{28,124},{32... | collective-permute-start | bytes 786440 | tf_op jit(solution)/shard_map/ppermute | solution.py:36
  35.4 7.1 %collective-permute-start.11 = (bf16[512,256]{1,0:T(8,128)(2,1)S(1)}, bf16[512,256]{1,0:T(8,128)(2,1)S(1)}, u32[]{:S(2)}, u32[]{:S(2)}) collective-permute-start(bf16[512,256]{1,0:T(8,128)(2,1)S(1)} %get-tuple-element.80), channel_id=1, source_target_pairs={{0,16},{4,68},{8,24},{12,76},{16,0},{20,84},{24,8},{28,92},{32,48}... | collective-permute-start | bytes 786440 | tf_op jit(solution)/shard_map/ppermute | solution.py:36
  36.0 7.5 %collective-permute-start.10 = (bf16[512,256]{1,0:T(8,128)(2,1)S(1)}, bf16[512,256]{1,0:T(8,128)(2,1)S(1)}, u32[]{:S(2)}, u32[]{:S(2)}) collective-permute-start(bf16[512,256]{1,0:T(8,128)(2,1)S(1)} %get-tuple-element.81), channel_id=1, source_target_pairs={{0,8},{4,36},{8,0},{12,44},{16,24},{20,52},{24,16},{28,60},{32,40}... | collective-permute-start | bytes 786440 | tf_op jit(solution)/shard_map/ppermute | solution.py:36
  45.6 9.9 %collective-permute-start.15 = (bf16[272,512]{1,0:T(8,128)(2,1)S(1)}, bf16[272,512]{1,0:T(8,128)(2,1)S(1)}, u32[]{:S(2)}, u32[]{:S(2)}) collective-permute-start(bf16[272,512]{1,0:T(8,128)(2,1)S(1)} %get-tuple-element.62.refs_0_), channel_id=1, source_target_pairs={{0,24},{4,100},{8,16},{12,108},{16,8},{20,116},{24,0},{28,124},{32... | collective-permute-start | bytes 835592 | tf_op jit(solution)/shard_map/ppermute | solution.py:36
  47.7 7.7 %collective-permute-start.14 = (bf16[272,512]{1,0:T(8,128)(2,1)S(1)}, bf16[272,512]{1,0:T(8,128)(2,1)S(1)}, u32[]{:S(2)}, u32[]{:S(2)}) collective-permute-start(bf16[272,512]{1,0:T(8,128)(2,1)S(1)} %get-tuple-element.62.refs_0_), channel_id=1, source_target_pairs={{0,16},{4,68},{8,24},{12,76},{16,0},{20,84},{24,8},{28,92},{32,48}... | collective-permute-start | bytes 835592 | tf_op jit(solution)/shard_map/ppermute | solution.py:36
  48.3 7.7 %collective-permute-start.13 = (bf16[272,512]{1,0:T(8,128)(2,1)S(1)}, bf16[272,512]{1,0:T(8,128)(2,1)S(1)}, u32[]{:S(2)}, u32[]{:S(2)}) collective-permute-start(bf16[272,512]{1,0:T(8,128)(2,1)S(1)} %get-tuple-element.62.refs_0_), channel_id=1, source_target_pairs={{0,8},{4,36},{8,0},{12,44},{16,24},{20,52},{24,16},{28,60},{32,40}... | collective-permute-start | bytes 835592 | tf_op jit(solution)/shard_map/ppermute | solution.py:36
  56.0 17.3 %collective-permute-start.22 = (bf16[1024,512]{1,0:T(8,128)(2,1)S(1)}, bf16[1024,512]{1,0:T(8,128)(2,1)S(1)}, u32[]{:S(2)}, u32[]{:S(2)}) collective-permute-start(bf16[1024,512]{1,0:T(8,128)(2,1)S(1)} %get-tuple-element.68.refs_3_), channel_id=1, source_target_pairs={{0,96},{4,28},{8,104},{12,20},{16,112},{20,12},{24,120},{28,4},{32... | collective-permute-start | bytes 3145736 | tf_op jit(solution)/shard_map/ppermute | solution.py:32
  58.5 14.9 %collective-permute-start.21 = (bf16[1024,512]{1,0:T(8,128)(2,1)S(1)}, bf16[1024,512]{1,0:T(8,128)(2,1)S(1)}, u32[]{:S(2)}, u32[]{:S(2)}) collective-permute-start(bf16[1024,512]{1,0:T(8,128)(2,1)S(1)} %get-tuple-element.68.refs_3_), channel_id=1, source_target_pairs={{0,32},{4,12},{8,40},{12,4},{16,48},{20,28},{24,56},{28,20},{32,0}... | collective-permute-start | bytes 3145736 | tf_op jit(solution)/shard_map/ppermute | solution.py:32
  58.5 2.5 %collective-permute-start.16 = (f32[16,128]{1,0:T(8,128)S(1)}, f32[16,128]{1,0:T(8,128)S(1)}, u32[]{:S(2)}, u32[]{:S(2)}) collective-permute-start(f32[16,128]{1,0:T(8,128)S(1)} %get-tuple-element.63), channel_id=1, source_target_pairs={{0,1},{1,0},{2,3},{3,2},{4,5},{5,4},{6,7},{7,6},{8,9},{9,8},{10,11... | collective-permute-start | bytes 24584 | tf_op jit(solution)/shard_map/ppermute | solution.py:40
  61.0 4.0 %collective-permute-start.17 = (f32[16,128]{1,0:T(8,128)S(1)}, f32[16,128]{1,0:T(8,128)S(1)}, u32[]{:S(2)}, u32[]{:S(2)}) collective-permute-start(f32[16,128]{1,0:T(8,128)S(1)} %add.58), channel_id=1, source_target_pairs={{0,2},{1,3},{2,0},{3,1},{4,6},{5,7},{6,4},{7,5},{8,10},{9,11},{10,... | collective-permute-start | bytes 24584 | tf_op jit(solution)/shard_map/ppermute | solution.py:40
  65.0 6.3 %collective-permute-start.20 = (f32[16,128]{1,0:T(8,128)S(1)}, f32[16,128]{1,0:T(8,128)S(1)}, u32[]{:S(2)}, u32[]{:S(2)}) collective-permute-start(f32[16,128]{1,0:T(8,128)S(1)} %add.59), channel_id=1, source_target_pairs={{0,96},{4,28},{8,104},{12,20},{16,112},{20,12},{24,120},{28,4},{32... | collective-permute-start | bytes 24584 | tf_op jit(solution)/shard_map/ppermute | solution.py:32
  65.6 7.8 %collective-permute-start.19 = (f32[16,128]{1,0:T(8,128)S(1)}, f32[16,128]{1,0:T(8,128)S(1)}, u32[]{:S(2)}, u32[]{:S(2)}) collective-permute-start(f32[16,128]{1,0:T(8,128)S(1)} %add.59), channel_id=1, source_target_pairs={{0,64},{4,20},{8,72},{12,28},{16,80},{20,4},{24,88},{28,12},{32,96... | collective-permute-start | bytes 24584 | tf_op jit(solution)/shard_map/ppermute | solution.py:32
  68.2 5.1 %collective-permute-start.18 = (f32[16,128]{1,0:T(8,128)S(1)}, f32[16,128]{1,0:T(8,128)S(1)}, u32[]{:S(2)}, u32[]{:S(2)}) collective-permute-start(f32[16,128]{1,0:T(8,128)S(1)} %add.59), channel_id=1, source_target_pairs={{0,32},{4,12},{8,40},{12,4},{16,48},{20,28},{24,56},{28,20},{32,0}... | collective-permute-start | bytes 24584 | tf_op jit(solution)/shard_map/ppermute | solution.py:32
  73.5 9.3 %collective-permute-start.23 = (bf16[1024,512]{1,0:T(8,128)(2,1)S(1)}, bf16[1024,512]{1,0:T(8,128)(2,1)S(1)}, u32[]{:S(2)}, u32[]{:S(2)}) collective-permute-start(bf16[1024,512]{1,0:T(8,128)(2,1)S(1)} %get-tuple-element.68.refs_3_), channel_id=1, source_target_pairs={{0,4},{4,0},{1,5},{5,1},{2,6},{6,2},{3,7},{7,3},{8,12},{12,8},{9,1... | collective-permute-start | bytes 3145736 | tf_op jit(solution)/shard_map/ppermute | solution.py:44
  78.4 5.5 %collective-permute-start.26 = (bf16[1024,512]{1,0:T(8,128)(2,1)S(1)}, bf16[1024,512]{1,0:T(8,128)(2,1)S(1)}, u32[]{:S(2)}, u32[]{:S(2)}) collective-permute-start(bf16[1024,512]{1,0:T(8,128)(2,1)S(1)} %collective-permute-done.21.ref.refs_4_), channel_id=1, source_target_pairs={{0,4},{4,0},{1,5},{5,1},{2,6},{6,2},{3,7},{7,3},{8,12},{12,8},{9,1... | collective-permute-start | bytes 3145736 | tf_op jit(solution)/shard_map/ppermute | solution.py:44
  78.5 5.4 %collective-permute-start.27 = (bf16[1024,512]{1,0:T(8,128)(2,1)S(1)}, bf16[1024,512]{1,0:T(8,128)(2,1)S(1)}, u32[]{:S(2)}, u32[]{:S(2)}) collective-permute-start(bf16[1024,512]{1,0:T(8,128)(2,1)S(1)} %collective-permute-done.22.ref.refs_5_), channel_id=1, source_target_pairs={{0,4},{4,0},{1,5},{5,1},{2,6},{6,2},{3,7},{7,3},{8,12},{12,8},{9,1... | collective-permute-start | bytes 3145736 | tf_op jit(solution)/shard_map/ppermute | solution.py:44
  78.9 9.4 %collective-permute-start.28 = (bf16[512,512]{1,0:T(8,128)(2,1)S(1)}, bf16[512,512]{1,0:T(8,128)(2,1)S(1)}, u32[]{:S(2)}, u32[]{:S(2)}) collective-permute-start(bf16[512,512]{1,0:T(8,128)(2,1)S(1)} %taken.3), channel_id=1, source_target_pairs={{0,32},{4,12},{8,40},{12,4},{16,48},{20,28},{24,56},{28,20},{32,0}... | collective-permute-start | bytes 1572872 | tf_op jit(solution)/shard_map/ppermute | solution.py:32
  79.7 9.9 %collective-permute-start.25 = (bf16[512,512]{1,0:T(8,128)(2,1)S(1)}, bf16[512,512]{1,0:T(8,128)(2,1)S(1)}, u32[]{:S(2)}, u32[]{:S(2)}) collective-permute-start(bf16[512,512]{1,0:T(8,128)(2,1)S(1)} %taken.2), channel_id=1, source_target_pairs={{0,96},{4,28},{8,104},{12,20},{16,112},{20,12},{24,120},{28,4},{32... | collective-permute-start | bytes 1572872 | tf_op jit(solution)/shard_map/ppermute | solution.py:32
  82.7 1.2 %collective-permute-start.24 = (f32[16,128]{1,0:T(8,128)S(1)}, f32[16,128]{1,0:T(8,128)S(1)}, u32[]{:S(2)}, u32[]{:S(2)}) collective-permute-start(f32[16,128]{1,0:T(8,128)S(1)} %add_add_fusion), channel_id=1, source_target_pairs={{0,4},{4,0},{1,5},{5,1},{2,6},{6,2},{3,7},{7,3},{8,12},{12,8},{9,1... | collective-permute-start | bytes 24584 | tf_op jit(solution)/shard_map/ppermute | solution.py:44
  89.6 2.1 %collective-permute-start.29 = (bf16[512,512]{1,0:T(8,128)(2,1)S(1)}, bf16[512,512]{1,0:T(8,128)(2,1)S(1)}, u32[]{:S(2)}, u32[]{:S(2)}) collective-permute-start(bf16[512,512]{1,0:T(8,128)(2,1)S(1)} %collective-permute-done.25.refs_3_), channel_id=1, source_target_pairs={{0,4},{4,0},{1,5},{5,1},{2,6},{6,2},{3,7},{7,3},{8,12},{12,8},{9,1... | collective-permute-start | bytes 1572872 | tf_op jit(solution)/shard_map/ppermute | solution.py:44
  90.2 2.3 %collective-permute-start.30 = (bf16[512,512]{1,0:T(8,128)(2,1)S(1)}, bf16[512,512]{1,0:T(8,128)(2,1)S(1)}, u32[]{:S(2)}, u32[]{:S(2)}) collective-permute-start(bf16[512,512]{1,0:T(8,128)(2,1)S(1)} %collective-permute-done.28.refs_4_), channel_id=1, source_target_pairs={{0,4},{4,0},{1,5},{5,1},{2,6},{6,2},{3,7},{7,3},{8,12},{12,8},{9,1... | collective-permute-start | bytes 1572872 | tf_op jit(solution)/shard_map/ppermute | solution.py:44
  (5 other events, 35.5 us)
